TPU v7x, 32 devices: a whole 2x2x4 slice. The times are simulated.
32 devices in a mesh: grp: 2 (over x), attn: 1, exp: 16 (over z, y, core).
Axes of the slice: x: 2, y: 2, z: 4, core: 2. Of those that a mesh axis runs over, the one named last changes fastest.
Arguments:
- hidden_rows: bfloat16 [16, 64, 5120], P('exp', 'grp', 'attn'), may hold values from -6 to 6
- routes: int32 [16, 64, 6], P('exp'), may hold values from 0 to 15, all different within a row; in each aligned block of 64 rows (0 to 63, 64 to 127, ..., all dimensions but the last counted through in order) at most 32 rows name the same one
- route_gain: float32 [16, 64, 6], P('exp'), may hold values from 0.1 to 1
- gate_weight: bfloat16 [16, 1536, 5120], P('exp', 'grp', 'attn'), may hold values from -0.078125 to 0.078125
- up_weight: bfloat16 [16, 1536, 5120], P('exp', 'grp', 'attn'), may hold values from -0.078125 to 0.078125
- down_weight: bfloat16 [16, 1536, 5120], P('exp', 'grp', 'attn'), may hold values from -0.21875 to 0.21875
Outputs:
- layer_out: bfloat16 [16, 64, 5120], P('exp', 'grp', 'attn')
Inputs may be any that keep to these rules, and one draw needn't show every extreme that they name: `routes`: each row names 6 different experts. Among the 64 rows of one line no expert is named more than 32 times, and in every draw some expert is named exactly 32 times by the rows of one line; every expert is named somewhere.
All inputs are finite; a program needn't handle non-finite values.
Results may differ from a plain program's by a relative error of at most 0.022.
Values may be sent and summed in bfloat16 or wider, within the bound.
No kernel may reach another device: no remote copies, remote signals or barrier semaphores. Data moves between devices by JAX's collectives and lax.ppermute only.
A program may use at most 128 MiB of HBM per device.

v0:
```python
import jax
import jax.numpy as jnp
from jax import lax
from jax.sharding import PartitionSpec as P


def slot_tables(routes_line, experts, caps):
    slab = routes_line.shape[0]
    picks = (routes_line[:, :, None] == jnp.arange(experts, dtype=jnp.int32)[None, None, :]).astype(
        jnp.float32
    )
    counts = jnp.sum(picks, axis=1)
    lower = (jnp.arange(slab)[:, None] > jnp.arange(slab)[None, :]).astype(jnp.float32)
    before = jnp.dot(lower, counts, precision=lax.Precision.HIGHEST)
    grid = jnp.arange(caps).astype(jnp.float32)
    send = counts[:, :, None] * (before[:, :, None] == grid).astype(jnp.float32)
    send = jnp.transpose(send, (1, 2, 0)).reshape(experts * caps, slab)
    gather_tab = picks[:, :, :, None] * (before[:, None, :, None] == grid).astype(jnp.float32)
    gather_tab = gather_tab.reshape(slab, picks.shape[1], experts * caps)
    return (send.astype(jnp.bfloat16), gather_tab)


def body(hidden_rows, routes, route_gain, gate_weight, up_weight, down_weight):
    n_lines = lax.axis_size("exp")
    local_experts = gate_weight.shape[0]
    experts = n_lines * local_experts
    slab = routes.shape[1]
    topk = routes.shape[2]
    caps = min(slab, slab * topk * 4 // (3 * experts))
    send_tab, gather_tab = slot_tables(routes[0], experts, caps)
    block = hidden_rows[0]
    half_rows = block.shape[0]
    width = block.shape[1]
    whole = lax.all_gather(block, "grp", axis=0, tiled=True)
    outgoing = jnp.dot(send_tab, whole, preferred_element_type=jnp.float32).astype(jnp.bfloat16)
    outgoing = outgoing.reshape(n_lines, local_experts, caps, width)
    arrived = lax.all_to_all(outgoing, "exp", split_axis=0, concat_axis=0, tiled=True)
    gate = jnp.einsum("sjcd,jfd->sjcf", arrived, gate_weight, preferred_element_type=jnp.float32)
    upper = jnp.einsum("sjcd,jfd->sjcf", arrived, up_weight, preferred_element_type=jnp.float32)
    gate, upper = (
        lax.psum(gate.astype(jnp.bfloat16), "attn").astype(jnp.float32),
        lax.psum(upper.astype(jnp.bfloat16), "attn").astype(jnp.float32),
    )
    act = (jax.nn.silu(gate) * upper).astype(jnp.bfloat16)
    part = jnp.einsum(
        "sjcf,jfd->sjcd", act, down_weight, preferred_element_type=jnp.float32
    ).astype(jnp.bfloat16)
    summed = lax.psum(part, "grp").astype(jnp.float32)
    returned = lax.all_to_all(
        summed.astype(jnp.bfloat16), "exp", split_axis=0, concat_axis=0, tiled=True
    ).astype(summed.dtype)
    returned = returned.reshape(experts * caps, width)
    start = lax.axis_index("grp") * half_rows
    table = lax.dynamic_slice_in_dim(gather_tab, start, half_rows, 0)
    gains = lax.dynamic_slice_in_dim(route_gain[0], start, half_rows, 0)
    picked = jnp.einsum("skm,md->skd", table, returned, precision=lax.Precision.HIGHEST)
    moe = jnp.sum(gains[:, :, None] * picked, axis=1)
    return (block.astype(jnp.float32) + moe).astype(jnp.bfloat16)[None]


def solution(mesh):
    placed = (
        P("exp", "grp", "attn"),
        P("exp", None, None),
        P("exp", None, None),
        P("exp", "grp", "attn"),
        P("exp", "grp", "attn"),
        P("exp", "grp", "attn"),
    )
    return jax.shard_map(
        body, mesh=mesh, in_specs=placed, out_specs=P("exp", "grp", "attn"), check_vma=False
    )
```

profile of v0, /device:TPU:13, one launch (start us, length us, event | category | flops | bytes accessed | tf_op | source)
XLA Modules:
  0.0 424.6 jit_solution(4344887049220619597)
XLA Ops:
  6.5 0.0 copy-start
  6.5 0.0 all-reduce.2.cloned.1.call-start
  6.5 0.7 copy.21
  7.3 0.1 fusion.56
  7.4 0.1 eq.73
  7.5 9.5 %all-gather = bf16[1,64,5120]{2,1,0:T(8,128)(2,1)S(1)} all-gather(bf16[1,32,5120]{2,1,0:T(8,128)(2,1)} %param.6), channel_id=2, replica_groups=mesh['grp'=2,'attn'=1,'exp'=16] {'grp'}, dimensions={1}, use_global_device_ids=true | all-gather | bytes 983040 | tf_op jit(solution)/shard_map/all_gather | solution.py:34
  17.0 0.1 fusion.52
  17.1 0.0 slice-start
  17.1 1.5 convolution_convert_fusion
  18.6 0.0 slice-start.1
  18.6 122.2 %all_to_all.10 = bf16[16,1,32,5120]{3,2,1,0:T(8,128)(2,1)S(1)} all-to-all(bf16[16,1,32,5120]{3,2,1,0:T(8,128)(2,1)S(1)} %bitcast.110), channel_id=1, replica_groups=mesh['grp'=2,'attn'=1,'exp'=16] {'exp'}, dimensions={0} | all-to-all | bytes 10485760 | tf_op jit(solution)/shard_map/all_to_all | solution.py:37
  140.8 0.0 slice-done
  140.8 0.0 slice-done.1
  140.8 0.0 slice-start.2
  140.8 4.3 %fusion.39 = bf16[16,1,32,768]{3,2,0,1:T(8,128)(2,1)S(1)} fusion(bf16[1,768,5120]{2,1,0:T(8,128)(2,1)S(1)} %bitcast.119, bf16[16,1,32,5120]{3,2,1,0:T(8,128)(2,1)S(1)} %all_to_all.10), kind=kOutput, calls=%fused_computation.23 | convolution fusion | flops 4026925056 | bytes 13893632 | tf_op jit(solution)/shard_map/sjcd,jfd->sjcf/dot_general | solution.py:38
  145.2 0.0 slice-start.3
  145.2 7.9 %fusion.44 = bf16[16,32,768]{2,1,0:T(8,128)(2,1)S(1)} fusion(bf16[1,768,5120]{2,1,0:T(8,128)(2,1)} %param.10, bf16[16,1,32,5120]{3,2,1,0:T(8,128)(2,1)S(1)} %all_to_all.10, bf16[16,1,32,768]{3,2,0,1:T(8,128)(2,1)S(1)} %fusion.39), kind=kOutput, calls=%fused_computation.24 | convolution fusion | flops 4030070784 | bytes 14680064 | tf_op jit(solution)/shard_map/sjcd,jfd->sjcf/dot_general | solution.py:39
  153.0 0.0 slice-done.2
  153.0 0.0 slice-done.3
  153.1 6.1 %fusion.9 = bf16[16,1,32,5120]{3,2,0,1:T(8,128)(2,1)} fusion(bf16[16,32,768]{2,1,0:T(8,128)(2,1)S(1)} %fusion.44, bf16[1,768,5120]{2,1,0:T(8,128)(2,1)S(1)} %bitcast.121), kind=kOutput, calls=%fused_computation.8 | convolution fusion | flops 4029153280 | bytes 13893632 | tf_op jit(solution)/shard_map/sjcf,jfd->sjcd/dot_general | solution.py:45
  159.2 0.0 all-reduce.2.cloned.1.call-update
  159.2 130.6 %all-reduce.2.cloned.1.call-done = bf16[16,1,32,5120]{3,2,0,1:T(8,128)(2,1)} async-done(((bf16[16,1,32,5120]{3,2,0,1:T(8,128)(2,1)}), bf16[16,1,32,5120]{3,2,0,1:T(8,128)(2,1)}) %all-reduce.2.cloned.1.call-update) | async-done | bytes 5242896 | tf_op jit(solution)/shard_map/psum | solution.py:48
  289.8 6.4 %all-to-all-start.1 = ((bf16[16,1,32,5120]{3,2,1,0:T(8,128)(2,1)}), bf16[16,1,32,5120]{3,2,1,0:T(8,128)(2,1)}, u32[]{:S(2)}, u32[]{:S(2)}) async-start(bf16[16,1,32,5120]{3,2,1,0:T(8,128)(2,1)} %bitcast.112), calls=%async_computation.1 | async-start | bytes 10485760 | tf_op jit(solution)/shard_map/all_to_all | solution.py:49
  296.2 0.1 fusion.53
  296.3 0.1 copy.12
  296.5 0.1 mul.51
  296.6 0.5 constant_dynamic-slice_fusion
  297.0 0.0 copy-start.1
  297.1 0.4 copy.18
  297.5 0.0 copy-done
  297.5 0.1 constant_dynamic-slice_fusion.2
  297.6 113.5 %all-to-all-done.1 = bf16[16,1,32,5120]{3,2,1,0:T(8,128)(2,1)} async-done(((bf16[16,1,32,5120]{3,2,1,0:T(8,128)(2,1)}), bf16[16,1,32,5120]{3,2,1,0:T(8,128)(2,1)}, u32[]{:S(2)}, u32[]{:S(2)}) %all-to-all-start.1) | async-done | bytes 5242912 | tf_op jit(solution)/shard_map/all_to_all | solution.py:49
  411.1 5.8 %fusion.14 = f32[32,5120]{1,0:T(8,128)S(1)} fusion(bf16[512,5120,1]{1,0,2:T(8,128)(2,1)} %bitcast.30, f32[32,6]{0,1:T(8,128)S(1)} %bitcast.117, f32[32,6,512]{2,0,1:T(8,128)S(1)} %copy.18, f32[32,512]{1,0:T(8,128)S(1)} %constant_dynamic-slice_fusion.1), kind=kOutput, calls=%fused_computation.14 | convolution fusion | flops 6041698304 | bytes 6357760 | tf_op jit(solution)/shard_map/skm,md->skd/dot_general | solution.py:56
  417.0 0.0 copy-done.1
  417.0 0.8 fusion.49
  (8 shorter events, 0.0 us)
Async XLA Ops:
  6.5 291.0 %copy-start = (f32[1,64,6]{1,0,2:T(1,128)S(1)}, f32[1,64,6]{1,0,2:T(1,128)}, u32[]{:S(2)}) copy-start(f32[1,64,6]{1,0,2:T(1,128)} %param.8) | copy-start | bytes 4612
  6.5 283.3 %all-reduce.2.cloned.1.call-start = ((), (), s32[]{:S(2)}) async-start(), calls=%async_computation.2 | async-start | bytes 10485760 | tf_op jit(solution)/shard_map/psum | solution.py:48
  17.1 123.7 %slice-start = ((s8[7864320]{0:T(1024)(128)(4,1)}), s8[4194304]{0:T(1024)(128)(4,1)S(1)}, s32[]{:S(2)}) async-start(s8[7864320]{0:T(1024)(128)(4,1)} %bitcast.118), calls=%async_computation.3 | async-start | bytes 8388608
  18.6 122.2 %slice-start.1 = ((s8[7864320]{0:T(1024)(128)(4,1)}), s8[3670016]{0:T(1024)(128)(4,1)S(1)}, s32[]{:S(2)}) async-start(s8[7864320]{0:T(1024)(128)(4,1)} %bitcast.118), calls=%async_computation.4 | async-start | bytes 7340032
  140.8 12.2 %slice-start.2 = ((s8[7864320]{0:T(1024)(128)(4,1)}), s8[3670016]{0:T(1024)(128)(4,1)S(1)}, s32[]{:S(2)}) async-start(s8[7864320]{0:T(1024)(128)(4,1)} %bitcast.120), calls=%async_computation.5 | async-start | bytes 7340032
  145.2 7.9 %slice-start.3 = ((s8[7864320]{0:T(1024)(128)(4,1)}), s8[4194304]{0:T(1024)(128)(4,1)S(1)}, s32[]{:S(2)}) async-start(s8[7864320]{0:T(1024)(128)(4,1)} %bitcast.120), calls=%async_computation.6 | async-start | bytes 8388608
  289.8 121.3 %all-to-all-start.1 = ((bf16[16,1,32,5120]{3,2,1,0:T(8,128)(2,1)}), bf16[16,1,32,5120]{3,2,1,0:T(8,128)(2,1)}, u32[]{:S(2)}, u32[]{:S(2)}) async-start(bf16[16,1,32,5120]{3,2,1,0:T(8,128)(2,1)} %bitcast.112), calls=%async_computation.1 | async-start | bytes 10485760 | tf_op jit(solution)/shard_map/all_to_all | solution.py:49
  297.0 119.9 %copy-start.1 = (bf16[1,32,5120]{2,1,0:T(8,128)(2,1)S(1)}, bf16[1,32,5120]{2,1,0:T(8,128)(2,1)}, u32[]{:S(2)}) copy-start(bf16[1,32,5120]{2,1,0:T(8,128)(2,1)} %param.6) | copy-start | bytes 983044
Sparse Core Ops, SparseCore 0:
  159.3 130.4 all-reduce.1
where the time goes:
time: 425 us
  waiting for transfers between devices  244 us (57%)
  blocking collectives  132 us (31%)
  matrix products  25.7 us (6%)
  between operations  13.5 us (3%)
  starting transfers between devices  6.38 us (2%)
    psum x1, waiting for transfers between devices, body(): summed = lax.psum(part, 'grp').astype(jnp.float32)  131 us
    all_to_all x1, blocking collectives, body(): lax.all_to_all(outgoing, 'exp', split_axis=0, concat_axis=0, tiled=True)  122 us
    all_to_all x1, waiting for transfers between devices, body(): lax.all_to_all(summed.astype(jnp.bfloat16), 'exp', split_axis=0, concat_a...  114 us
    all_gather x1, blocking collectives, body(): whole = lax.all_gather(block, 'grp', axis=0, tiled=True)  9.46 us
  transfers between devices with their start and end apart: 2, of which 2 were waited for; matrix products, arithmetic and copies ran while one was open for 0% of the time, Pallas kernels for 0%

commit v1 on v0

v1 whole, which is shorter than its diff:
```python
import jax
import jax.numpy as jnp
from jax import lax
from jax.sharding import Mesh, PartitionSpec as P

CHUNK_EDGES = (0, 11, 22, 31, 40)
SCATTER_ORDER = (2, 3, 0, 1)
GAIN_CHUNK = 2
LANES = 128


def expert_tables(info, topk, expert, caps):
    routes, gains = info[:, :topk], info[:, topk:]
    named = (routes == expert.astype(jnp.float32)).astype(jnp.float32)
    count = jnp.sum(named, axis=1)
    gain = jnp.sum(named * gains, axis=1)
    slab = count.shape[1]
    earlier = (jnp.arange(slab)[:, None] < jnp.arange(slab)[None, :]).astype(jnp.float32)
    before = jnp.dot(count, earlier, precision=lax.Precision.HIGHEST)
    grid = jnp.arange(caps).astype(jnp.float32)
    sel = count[:, None, :] * (before[:, None, :] == grid[None, :, None]).astype(jnp.float32)
    return sel, gain


def body(hidden_rows, routes, route_gain, gate_weight, up_weight, down_weight):
    n_lines = lax.axis_size("exp")
    n_grp = lax.axis_size("grp")
    slab, topk = routes.shape[1:]
    caps = min(slab, slab * topk * 4 // (3 * n_lines))
    block = hidden_rows[0]
    half_rows, width = block.shape
    expert = lax.axis_index("exp")

    info = jnp.concatenate([routes[0].astype(jnp.float32), route_gain[0]], axis=1).T
    info = lax.all_gather(info, "exp", axis=0)
    rows = lax.all_gather(block, ("exp", "grp"), axis=0).reshape(n_lines, slab, width)
    sel, gain = expert_tables(info, topk, expert, caps)
    sel = sel.astype(jnp.bfloat16)

    taken = jnp.einsum("lcr,lrd->lcd", sel, rows, preferred_element_type=jnp.float32)
    taken = taken.astype(jnp.bfloat16).reshape(n_lines * caps, width)
    dims = (((1,), (1,)), ((), ()))
    gate = lax.dot_general(taken, gate_weight[0], dims, preferred_element_type=jnp.float32)
    upper = lax.dot_general(taken, up_weight[0], dims, preferred_element_type=jnp.float32)
    gate = lax.psum(gate, "attn")
    upper = lax.psum(upper, "attn")
    act = (jax.nn.silu(gate) * upper).astype(jnp.bfloat16).reshape(n_lines, caps, -1)
    spread = jnp.einsum("lcr,lcf->lrf", sel, act, preferred_element_type=jnp.float32)
    spread = (spread * gain[:, :, None]).astype(jnp.bfloat16).reshape(n_lines * slab, -1)
    part = jnp.dot(spread, down_weight[0], preferred_element_type=jnp.float32).astype(jnp.bfloat16)
    part = part.reshape(n_lines * n_grp, half_rows, width)
    moe = lax.psum_scatter(part, ("exp", "grp"), scatter_dimension=0, tiled=True)[0]
    return (block.astype(jnp.float32) + moe.astype(jnp.float32)).astype(jnp.bfloat16)[None]


NX, NZ, NY, NCORE = 2, 4, 2, 2
AXES = ("x", "z", "y", "core")


def swap(value, axis, flip=1):
    size = {"x": NX, "z": NZ, "y": NY, "core": NCORE}[axis]
    return lax.ppermute(value, axis, [(i, i ^ flip) for i in range(size)])


def after(value, *others):
    return lax.optimization_barrier((value,) + others)[0] if others else value


def gain_columns(routes, route_gain, experts):
    named = routes[:, :, None] == jnp.arange(experts, dtype=jnp.int32)
    rest = jnp.sum(jnp.where(named, route_gain[:, :, None], 0.0), axis=1)
    columns = []
    for _ in range(3):
        piece = lax.reduce_precision(rest, 8, 7)
        columns.append(piece.astype(jnp.bfloat16))
        rest = rest - piece
    columns = jnp.concatenate(columns, axis=1)
    return jnp.pad(columns, ((0, 0), (0, LANES - columns.shape[1])))


def ordered(blocks, y_first):
    return [blocks[0], blocks[2], blocks[1], blocks[3]] if y_first else blocks


def grown(value, *flip):
    return jnp.concatenate([value, swap(value, *flip)], axis=0)


def added(a, b):
    return (a.astype(jnp.float32) + b.astype(jnp.float32)).astype(jnp.bfloat16)


def halved(value, *flip):
    cut = value.shape[0] // 2
    return added(value[:cut], swap(value[cut:], *flip))


def ring_body(hidden_rows, routes, route_gain, gate_weight, up_weight, down_weight):
    n_lines = NZ * NY * NCORE
    block = hidden_rows[0]
    half, width = block.shape
    x, z, y, core = [lax.axis_index(name) for name in AXES]
    expert = (z * NY + y) * NCORE + core
    columns = gain_columns(
        lax.dynamic_slice_in_dim(routes[0], x * half, half, 0),
        lax.dynamic_slice_in_dim(route_gain[0], x * half, half, 0),
        n_lines,
    )
    edges = [width * part // CHUNK_EDGES[-1] for part in CHUNK_EDGES]
    spans = [slice(start, stop) for start, stop in zip(edges, edges[1:])]
    n_chunks = len(spans)
    planes = [("x", "y") if c % 2 == 0 else ("y", "x") for c in range(n_chunks)]
    dims = (((1,), (1,)), ((), ()))

    far, in_z, in_first, received = {}, [], [], []
    for c in range(n_chunks):
        value = block[:, spans[c]]
        if c == GAIN_CHUNK:
            value = jnp.concatenate([value, columns], axis=1)
        if c >= 2:
            value = after(value, *in_z[:2])
        far[c] = grown(value, "z", 2)
        in_z.append(grown(after(far[c], *in_first[:2]) if c >= 2 else far[c], "z", 1))
        value = grown(in_z[c], planes[c][0])
        in_first.append(value)
        if c < 2:
            received.append(swap(value, planes[c][1]))
    joined = lax.optimization_barrier(received + in_first[2:])
    in_first[2:] = joined[2:]
    received = joined[:2] + [swap(in_first[c], planes[c][1]) for c in (2, 3)]

    halves = [{"gate": 0.0, "up": 0.0}, {"gate": 0.0, "up": 0.0}]
    for c in range(n_chunks):
        if c == 2:
            ties = [sums[name] for sums in halves for name in ("gate", "up")]
            received[2:] = lax.optimization_barrier(received[2:] + ties)[:2]
        pieces = jnp.split(in_first[c], 2, axis=0) + jnp.split(received[c], 2, axis=0)
        own = jnp.concatenate(ordered(pieces, c % 2 == 1), axis=0)
        for rows, sums in zip((own, swap(own, "core")), halves):
            if c == GAIN_CHUNK:
                lane = lax.broadcasted_iota(jnp.int32, (rows.shape[0], LANES), 1)
                gains = jnp.where(lax.rem(lane, n_lines) == expert, rows[:, -LANES:].astype(jnp.float32), 0.0)
                sums["gain"] = jnp.sum(gains, axis=1, keepdims=True)
                rows = rows[:, :-LANES]
            for name, weight in (("gate", gate_weight), ("up", up_weight)):
                sums[name] += lax.dot_general(rows, weight[0, :, spans[c]], dims, preferred_element_type=jnp.float32)

    def act(side, *before):
        gate, upper = after(halves[side]["gate"], *before), halves[side]["up"]
        value = (jax.nn.silu(gate) * upper * halves[side]["gain"]).astype(jnp.bfloat16)
        return lax.optimization_barrier(value)

    def down(value, c):
        return jnp.dot(value, down_weight[0, :, spans[c]], preferred_element_type=jnp.float32)

    away = act(1)
    to_core = {c: down(away, c).astype(jnp.bfloat16) for c in SCATTER_ORDER[:2]}
    here = act(0, *to_core.values())
    away = after(away, *to_core.values())
    to_core.update({c: down(away, c).astype(jnp.bfloat16) for c in SCATTER_ORDER[2:]})
    parts, sent, kept = {}, {}, {}
    for c in SCATTER_ORDER:
        part = (down(here, c) + swap(to_core[c], "core").astype(jnp.float32)).astype(jnp.bfloat16)
        parts[c] = jnp.concatenate(ordered(jnp.split(part, 4, axis=0), c % 2 == 1), axis=0)
        kept[c], goes = jnp.split(parts[c], 2, axis=0)
        sent[c] = swap(goes, planes[c][1])
    following = {c: SCATTER_ORDER[i + 2 - i % 2:i + 4 - i % 2] for i, c in enumerate(SCATTER_ORDER)}
    outs, first = {}, {}
    for c in SCATTER_ORDER:
        first[c] = added(kept[c], after(sent[c], *[parts[d] for d in following[c]]))
    for c in SCATTER_ORDER:
        stays, goes = jnp.split(first[c], 2, axis=0)
        part = added(stays, after(swap(goes, planes[c][0]), *[first[d] for d in following[c]]))
        part = halved(part, "z", 1)
        total = block[:, spans[c]].astype(jnp.float32) + part[:half].astype(jnp.float32)
        total += swap(part[half:], "z", 2).astype(jnp.float32)
        outs[c] = total.astype(jnp.bfloat16)
    return jnp.concatenate([outs[c] for c in range(n_chunks)], axis=1)[None]


def solution(mesh):
    small = dict(mesh.shape) == {"grp": NX, "attn": 1, "exp": NZ * NY * NCORE}
    if small:
        mesh = Mesh(mesh.devices.reshape(NX, NZ, NY, NCORE), AXES)
        exp, grp, attn, run = ("z", "y", "core"), "x", None, ring_body
    else:
        exp, grp, attn, run = "exp", "grp", "attn", body
    placed = (
        P(exp, grp, attn),
        P(exp, None, None),
        P(exp, None, None),
        P(exp, grp, attn),
        P(exp, grp, attn),
        P(exp, grp, attn),
    )
    return jax.shard_map(run, mesh=mesh, in_specs=placed, out_specs=P(exp, grp, attn), check_vma=False)
```

time: 425 us -> 163 us (0.38)
  the two profiles are of different devices: /device:TPU:13 before, /device:TPU:0 now
where the time goes in v1:
time: 163 us; the launch traced here: 162 us
  waiting for transfers between devices  74.7 us (46%)
  starting transfers between devices  45.9 us (28%)
  matrix products  33.9 us (21%)
  local copies, waits for them, and re-layouts  4.6 us (3%)
  other arithmetic  2.77 us (2%)
    ppermute x40, waiting for transfers between devices, swap(): return lax.ppermute(value, axis, [(i, i ^ flip) for i in range(size)])  74.7 us
    ppermute x40, starting transfers between devices, swap(): return lax.ppermute(value, axis, [(i, i ^ flip) for i in range(size)])  45.9 us
    dot_general x16, matrix products, ring_body(): lax.dot_general(rows, weight[0, :, spans[c]], dims, preferred_element_typ...  23.1 us
    dot_general x8, matrix products, down(): jnp.dot(value, down_weight[0, :, spans[c]], preferred_element_type=jnp.fl...  10.7 us
  transfers between devices with their start and end apart: 40, of which 21 were waited for; matrix products, arithmetic and copies ran while one was open for 20% of the time, Pallas kernels for 0%

profile of v1, /device:TPU:0, one launch (start us, length us, event | category | flops | bytes accessed | tf_op | source)
XLA Modules:
  0.0 162.5 jit_solution(13852123881323248093)
XLA Ops:
  1.0 4.1 %collective-permute-start.4 = (bf16[32,1408]{1,0:T(8,128)(2,1)S(1)}, bf16[32,1408]{1,0:T(8,128)(2,1)S(1)}, u32[]{:S(2)}, u32[]{:S(2)}) collective-permute-start(bf16[32,1408]{1,0:T(8,128)(2,1)S(1)} %get-tuple-element.57), channel_id=1, source_target_pairs={{0,8},{4,12},{8,0},{12,4},{1,9},{5,13},{9,1},{13,5},{2,10},{6,14},... | collective-permute-start | bytes 270344 | tf_op jit(solution)/shard_map/ppermute | solution.py:62
  7.1 5.1 %collective-permute-done.4 = bf16[32,1408]{1,0:T(8,128)(2,1)S(1)} collective-permute-done((bf16[32,1408]{1,0:T(8,128)(2,1)S(1)}, bf16[32,1408]{1,0:T(8,128)(2,1)S(1)}, u32[]{:S(2)}, u32[]{:S(2)}) %collective-permute-start.4) | collective-permute-done | bytes 90144 | tf_op jit(solution)/shard_map/ppermute | solution.py:62
  14.5 5.0 %collective-permute-done.5 = bf16[64,1408]{1,0:T(8,128)(2,1)S(1)} collective-permute-done((bf16[64,1408]{1,0:T(8,128)(2,1)S(1)}, bf16[64,1408]{1,0:T(8,128)(2,1)S(1)}, u32[]{:S(2)}, u32[]{:S(2)}) %collective-permute-start.5) | collective-permute-done | bytes 180256 | tf_op jit(solution)/shard_map/ppermute | solution.py:62
  19.5 1.6 collective-permute-start.6
  21.4 1.6 collective-permute-start.2
  23.0 3.0 %collective-permute-start.11 = (bf16[32,1152]{1,0:T(8,128)(2,1)S(1)}, bf16[32,1152]{1,0:T(8,128)(2,1)S(1)}, u32[]{:S(2)}, u32[]{:S(2)}) collective-permute-start(bf16[32,1152]{1,0:T(8,128)(2,1)S(1)} %get-tuple-element.23), channel_id=1, source_target_pairs={{0,8},{4,12},{8,0},{12,4},{1,9},{5,13},{9,1},{13,5},{2,10},{6,14},... | collective-permute-start | bytes 221192 | tf_op jit(solution)/shard_map/ppermute | solution.py:62
  26.0 2.4 %collective-permute-done.11 = bf16[32,1152]{1,0:T(8,128)(2,1)S(1)} collective-permute-done((bf16[32,1152]{1,0:T(8,128)(2,1)S(1)}, bf16[32,1152]{1,0:T(8,128)(2,1)S(1)}, u32[]{:S(2)}, u32[]{:S(2)}) %collective-permute-start.11) | collective-permute-done | bytes 73760 | tf_op jit(solution)/shard_map/ppermute | solution.py:62
  29.8 2.5 %collective-permute-start.12 = (bf16[64,1152]{1,0:T(8,128)(2,1)S(1)}, bf16[64,1152]{1,0:T(8,128)(2,1)S(1)}, u32[]{:S(2)}, u32[]{:S(2)}) collective-permute-start(bf16[64,1152]{1,0:T(8,128)(2,1)S(1)} %pad_maximum_fusion.15), channel_id=1, source_target_pairs={{0,4},{4,0},{8,12},{12,8},{1,5},{5,1},{9,13},{13,9},{2,6},{6,2},{1... | collective-permute-start | bytes 442376 | tf_op jit(solution)/shard_map/ppermute | solution.py:62
  32.7 1.6 collective-permute-start.3
  35.8 2.7 %collective-permute-start.13 = (bf16[128,1152]{1,0:T(8,128)(2,1)S(1)}, bf16[128,1152]{1,0:T(8,128)(2,1)S(1)}, u32[]{:S(2)}, u32[]{:S(2)}) collective-permute-start(bf16[128,1152]{1,0:T(8,128)(2,1)S(1)} %pad_maximum_fusion.11), channel_id=1, source_target_pairs={{0,2},{2,0},{1,3},{3,1},{4,6},{6,4},{5,7},{7,5},{8,10},{10,8},{9,1... | collective-permute-start | bytes 884744 | tf_op jit(solution)/shard_map/ppermute | solution.py:62
  38.5 2.2 %collective-permute-done.9 = bf16[64,1280]{1,0:T(8,128)(2,1)S(1)} collective-permute-done((bf16[64,1280]{1,0:T(8,128)(2,1)S(1)}, bf16[64,1280]{1,0:T(8,128)(2,1)S(1)}, u32[]{:S(2)}, u32[]{:S(2)}) %collective-permute-start.9) | collective-permute-done | bytes 163872 | tf_op jit(solution)/shard_map/ppermute | solution.py:62
  41.8 14.0 %collective-permute-done.13 = bf16[128,1152]{1,0:T(8,128)(2,1)S(1)} collective-permute-done((bf16[128,1152]{1,0:T(8,128)(2,1)S(1)}, bf16[128,1152]{1,0:T(8,128)(2,1)S(1)}, u32[]{:S(2)}, u32[]{:S(2)}) %collective-permute-start.13) | collective-permute-done | bytes 294944 | tf_op jit(solution)/shard_map/ppermute | solution.py:62
  55.9 1.9 %collective-permute-done.10 = bf16[128,1280]{1,0:T(8,128)(2,1)S(1)} collective-permute-done((bf16[128,1280]{1,0:T(8,128)(2,1)S(1)}, bf16[128,1280]{1,0:T(8,128)(2,1)S(1)}, u32[]{:S(2)}, u32[]{:S(2)}) %collective-permute-start.10) | collective-permute-done | bytes 327712 | tf_op jit(solution)/shard_map/ppermute | solution.py:62
  59.8 1.4 fusion.12
  61.3 2.6 %fusion.82 = f32[512,768]{1,0:T(8,128)} fusion(f32[512,768]{1,0:T(8,128)S(1)} %fusion.12, bf16[512,1408]{1,0:T(8,128)(2,1)S(1)} %constant_dynamic-update-slice_fusion, bf16[1,768,5120]{2,1,0:T(8,128)(2,1)S(1)} %bitcast.118), kind=kOutput, calls=%fused_computation.84 | convolution fusion | flops 1107689472 | bytes 6750208 | tf_op jit(solution)/shard_map/dot_general | solution.py:146
  63.9 1.4 fusion.20
  65.4 1.4 fusion.76
  66.9 1.4 fusion.10
  68.3 1.4 fusion.85
  69.7 1.4 fusion.18
  71.2 1.4 fusion.79
  74.7 1.4 fusion.48
  76.1 1.2 add_add_fusion
  81.2 1.5 multiply_convert_fusion.1
  86.5 1.4 convolution_convert_fusion.3
  88.0 1.4 convolution_convert_fusion.2
  89.9 1.5 multiply_convert_fusion
  92.8 1.5 add_convert_fusion.3
  94.3 1.6 collective-permute-start.31
  95.9 1.6 collective-permute-start.36
  97.5 1.4 add_convert_fusion
  99.0 1.4 add_convert_fusion.1
  101.8 8.8 %collective-permute-done.31 = bf16[256,1152]{1,0:T(8,128)(2,1)S(1)} collective-permute-done((bf16[256,1152]{1,0:T(8,128)(2,1)S(1)}, bf16[256,1152]{1,0:T(8,128)(2,1)S(1)}, u32[]{:S(2)}, u32[]{:S(2)}) %collective-permute-start.31) | collective-permute-done | bytes 589856 | tf_op jit(solution)/shard_map/ppermute | solution.py:62
  110.7 1.5 collective-permute-done.36
  113.0 1.5 collective-permute-start.32
  114.5 11.5 %collective-permute-done.21 = bf16[256,1408]{1,0:T(8,128)(2,1)S(1)} collective-permute-done((bf16[256,1408]{1,0:T(8,128)(2,1)S(1)}, bf16[256,1408]{1,0:T(8,128)(2,1)S(1)}, u32[]{:S(2)}, u32[]{:S(2)}) %collective-permute-start.21) | collective-permute-done | bytes 720928 | tf_op jit(solution)/shard_map/ppermute | solution.py:62
  126.2 1.6 collective-permute-start.22
  128.0 3.4 %collective-permute-done.37 = bf16[128,1152]{1,0:T(8,128)(2,1)S(1)} collective-permute-done((bf16[128,1152]{1,0:T(8,128)(2,1)S(1)}, bf16[128,1152]{1,0:T(8,128)(2,1)S(1)}, u32[]{:S(2)}, u32[]{:S(2)}) %collective-permute-start.37) | collective-permute-done | bytes 294944 | tf_op jit(solution)/shard_map/ppermute | solution.py:62
  131.5 2.5 %collective-permute-done.32 = bf16[128,1152]{1,0:T(8,128)(2,1)S(1)} collective-permute-done((bf16[128,1152]{1,0:T(8,128)(2,1)S(1)}, bf16[128,1152]{1,0:T(8,128)(2,1)S(1)}, u32[]{:S(2)}, u32[]{:S(2)}) %collective-permute-start.32) | collective-permute-done | bytes 294944 | tf_op jit(solution)/shard_map/ppermute | solution.py:62
  134.0 1.8 %collective-permute-start.38 = (bf16[64,1152]{1,0:T(8,128)(2,1)S(1)}, bf16[64,1152]{1,0:T(8,128)(2,1)S(1)}, u32[]{:S(2)}, u32[]{:S(2)}) collective-permute-start(bf16[64,1152]{1,0:T(8,128)(2,1)S(1)} %slice.190), channel_id=1, source_target_pairs={{0,4},{4,0},{8,12},{12,8},{1,5},{5,1},{9,13},{13,9},{2,6},{6,2},{1... | collective-permute-start | bytes 442376 | tf_op jit(solution)/shard_map/ppermute | solution.py:62
  137.1 2.1 %collective-permute-done.38 = bf16[64,1152]{1,0:T(8,128)(2,1)S(1)} collective-permute-done((bf16[64,1152]{1,0:T(8,128)(2,1)S(1)}, bf16[64,1152]{1,0:T(8,128)(2,1)S(1)}, u32[]{:S(2)}, u32[]{:S(2)}) %collective-permute-start.38) | collective-permute-done | bytes 147488 | tf_op jit(solution)/shard_map/ppermute | solution.py:62
  139.3 3.8 %collective-permute-start.39 = (bf16[32,1152]{1,0:T(8,128)(2,1)S(1)}, bf16[32,1152]{1,0:T(8,128)(2,1)S(1)}, u32[]{:S(2)}, u32[]{:S(2)}) collective-permute-start(bf16[32,1152]{1,0:T(8,128)(2,1)S(1)} %slice.192), channel_id=1, source_target_pairs={{0,8},{4,12},{8,0},{12,4},{1,9},{5,13},{9,1},{13,5},{2,10},{6,14},... | collective-permute-start | bytes 221192 | tf_op jit(solution)/shard_map/ppermute | solution.py:62
  143.1 2.2 %collective-permute-start.34 = (bf16[32,1152]{1,0:T(8,128)(2,1)S(1)}, bf16[32,1152]{1,0:T(8,128)(2,1)S(1)}, u32[]{:S(2)}, u32[]{:S(2)}) collective-permute-start(bf16[32,1152]{1,0:T(8,128)(2,1)S(1)} %slice.188), channel_id=1, source_target_pairs={{0,8},{4,12},{8,0},{12,4},{1,9},{5,13},{9,1},{13,5},{2,10},{6,14},... | collective-permute-start | bytes 221192 | tf_op jit(solution)/shard_map/ppermute | solution.py:62
  145.4 1.5 collective-permute-start.23
  147.6 4.6 %collective-permute-done.23 = bf16[64,1408]{1,0:T(8,128)(2,1)S(1)} collective-permute-done((bf16[64,1408]{1,0:T(8,128)(2,1)S(1)}, bf16[64,1408]{1,0:T(8,128)(2,1)S(1)}, u32[]{:S(2)}, u32[]{:S(2)}) %collective-permute-start.23) | collective-permute-done | bytes 180256 | tf_op jit(solution)/shard_map/ppermute | solution.py:62
  152.3 1.9 %collective-permute-start.24 = (bf16[32,1408]{1,0:T(8,128)(2,1)S(1)}, bf16[32,1408]{1,0:T(8,128)(2,1)S(1)}, u32[]{:S(2)}, u32[]{:S(2)}) collective-permute-start(bf16[32,1408]{1,0:T(8,128)(2,1)S(1)} %slice.180), channel_id=1, source_target_pairs={{0,8},{4,12},{8,0},{12,4},{1,9},{5,13},{9,1},{13,5},{2,10},{6,14},... | collective-permute-start | bytes 270344 | tf_op jit(solution)/shard_map/ppermute | solution.py:62
  156.2 1.6 collective-permute-done.24
  157.8 3.9 %collective-permute-done.29 = bf16[32,1408]{1,0:T(8,128)(2,1)S(1)} collective-permute-done((bf16[32,1408]{1,0:T(8,128)(2,1)S(1)}, bf16[32,1408]{1,0:T(8,128)(2,1)S(1)}, u32[]{:S(2)}, u32[]{:S(2)}) %collective-permute-start.29) | collective-permute-done | bytes 90144 | tf_op jit(solution)/shard_map/ppermute | solution.py:62
  (151 shorter events, 31.7 us)
Async XLA Ops:
  0.0 6.1 %copy-start = (s32[1,64,6]{1,0,2:T(1,128)S(1)}, s32[1,64,6]{1,0,2:T(1,128)}, u32[]{:S(2)}) copy-start(s32[1,64,6]{1,0,2:T(1,128)} %param.7) | copy-start | bytes 4612
  1.0 11.3 %collective-permute-start.4 = (bf16[32,1408]{1,0:T(8,128)(2,1)S(1)}, bf16[32,1408]{1,0:T(8,128)(2,1)S(1)}, u32[]{:S(2)}, u32[]{:S(2)}) collective-permute-start(bf16[32,1408]{1,0:T(8,128)(2,1)S(1)} %get-tuple-element.57), channel_id=1, source_target_pairs={{0,8},{4,12},{8,0},{12,4},{1,9},{5,13},{9,1},{13,5},{2,10},{6,14},... | collective-permute-start | bytes 270344 | tf_op jit(solution)/shard_map/ppermute | solution.py:62
  5.1 8.4 %collective-permute-start = (bf16[32,1408]{1,0:T(8,128)(2,1)S(1)}, bf16[32,1408]{1,0:T(8,128)(2,1)S(1)}, u32[]{:S(2)}, u32[]{:S(2)}) collective-permute-start(bf16[32,1408]{1,0:T(8,128)(2,1)S(1)} %get-tuple-element.58), channel_id=1, source_target_pairs={{0,8},{4,12},{8,0},{12,4},{1,9},{5,13},{9,1},{13,5},{2,10},{6,14},... | collective-permute-start | bytes 270344 | tf_op jit(solution)/shard_map/ppermute | solution.py:62
  12.3 7.2 %collective-permute-start.5 = (bf16[64,1408]{1,0:T(8,128)(2,1)S(1)}, bf16[64,1408]{1,0:T(8,128)(2,1)S(1)}, u32[]{:S(2)}, u32[]{:S(2)}) collective-permute-start(bf16[64,1408]{1,0:T(8,128)(2,1)S(1)} %pad_maximum_fusion.13), channel_id=1, source_target_pairs={{0,4},{4,0},{8,12},{12,8},{1,5},{5,1},{9,13},{13,9},{2,6},{6,2},{1... | collective-permute-start | bytes 540680 | tf_op jit(solution)/shard_map/ppermute | solution.py:62
  13.5 7.8 %collective-permute-start.1 = (bf16[64,1408]{1,0:T(8,128)(2,1)S(1)}, bf16[64,1408]{1,0:T(8,128)(2,1)S(1)}, u32[]{:S(2)}, u32[]{:S(2)}) collective-permute-start(bf16[64,1408]{1,0:T(8,128)(2,1)S(1)} %pad_maximum_fusion.12), channel_id=1, source_target_pairs={{0,4},{4,0},{8,12},{12,8},{1,5},{5,1},{9,13},{13,9},{2,6},{6,2},{1... | collective-permute-start | bytes 540680 | tf_op jit(solution)/shard_map/ppermute | solution.py:62
  19.4 40.4 %slice-start.2 = ((s8[7864320]{0:T(1024)(128)(4,1)}), s8[4194304]{0:T(1024)(128)(4,1)S(1)}, s32[]{:S(2)}) async-start(s8[7864320]{0:T(1024)(128)(4,1)} %bitcast.117), calls=%async_computation.2 | async-start | bytes 8388608
  19.5 9.0 %collective-permute-start.6 = (bf16[128,1408]{1,0:T(8,128)(2,1)S(1)}, bf16[128,1408]{1,0:T(8,128)(2,1)S(1)}, u32[]{:S(2)}, u32[]{:S(2)}) collective-permute-start(bf16[128,1408]{1,0:T(8,128)(2,1)S(1)} %pad_maximum_fusion.9), channel_id=1, source_target_pairs={{0,2},{2,0},{1,3},{3,1},{4,6},{6,4},{5,7},{7,5},{8,10},{10,8},{9,1... | collective-permute-start | bytes 1081352 | tf_op jit(solution)/shard_map/ppermute | solution.py:62
  21.4 8.3 %collective-permute-start.2 = (bf16[128,1408]{1,0:T(8,128)(2,1)S(1)}, bf16[128,1408]{1,0:T(8,128)(2,1)S(1)}, u32[]{:S(2)}, u32[]{:S(2)}) collective-permute-start(bf16[128,1408]{1,0:T(8,128)(2,1)S(1)} %pad_maximum_fusion.8), channel_id=1, source_target_pairs={{0,16},{16,0},{1,17},{17,1},{2,18},{18,2},{3,19},{19,3},{4,20},{20... | collective-permute-start | bytes 1081352 | tf_op jit(solution)/shard_map/ppermute | solution.py:62
  23.0 5.5 %collective-permute-start.11 = (bf16[32,1152]{1,0:T(8,128)(2,1)S(1)}, bf16[32,1152]{1,0:T(8,128)(2,1)S(1)}, u32[]{:S(2)}, u32[]{:S(2)}) collective-permute-start(bf16[32,1152]{1,0:T(8,128)(2,1)S(1)} %get-tuple-element.23), channel_id=1, source_target_pairs={{0,8},{4,12},{8,0},{12,4},{1,9},{5,13},{9,1},{13,5},{2,10},{6,14},... | collective-permute-start | bytes 221192 | tf_op jit(solution)/shard_map/ppermute | solution.py:62
  25.9 6.8 %collective-permute-start.8 = (bf16[32,1280]{1,0:T(8,128)(2,1)S(1)}, bf16[32,1280]{1,0:T(8,128)(2,1)S(1)}, u32[]{:S(2)}, u32[]{:S(2)}) collective-permute-start(bf16[32,1280]{1,0:T(8,128)(2,1)S(1)} %fusion.99), channel_id=1, source_target_pairs={{0,8},{4,12},{8,0},{12,4},{1,9},{5,13},{9,1},{13,5},{2,10},{6,14},... | collective-permute-start | bytes 245768 | tf_op jit(solution)/shard_map/ppermute | solution.py:62
  29.8 6.0 %collective-permute-start.12 = (bf16[64,1152]{1,0:T(8,128)(2,1)S(1)}, bf16[64,1152]{1,0:T(8,128)(2,1)S(1)}, u32[]{:S(2)}, u32[]{:S(2)}) collective-permute-start(bf16[64,1152]{1,0:T(8,128)(2,1)S(1)} %pad_maximum_fusion.15), channel_id=1, source_target_pairs={{0,4},{4,0},{8,12},{12,8},{1,5},{5,1},{9,13},{13,9},{2,6},{6,2},{1... | collective-permute-start | bytes 442376 | tf_op jit(solution)/shard_map/ppermute | solution.py:62
  32.7 25.1 %collective-permute-start.3 = (bf16[256,1408]{1,0:T(8,128)(2,1)S(1)}, bf16[256,1408]{1,0:T(8,128)(2,1)S(1)}, u32[]{:S(2)}, u32[]{:S(2)}) collective-permute-start(bf16[256,1408]{1,0:T(8,128)(2,1)S(1)} %pad_maximum_fusion.2), channel_id=1, source_target_pairs={{0,2},{2,0},{1,3},{3,1},{4,6},{6,4},{5,7},{7,5},{8,10},{10,8},{9,1... | collective-permute-start | bytes 2162696 | tf_op jit(solution)/shard_map/ppermute | solution.py:62
  34.3 23.5 %collective-permute-start.7 = (bf16[256,1408]{1,0:T(8,128)(2,1)S(1)}, bf16[256,1408]{1,0:T(8,128)(2,1)S(1)}, u32[]{:S(2)}, u32[]{:S(2)}) collective-permute-start(bf16[256,1408]{1,0:T(8,128)(2,1)S(1)} %pad_maximum_fusion.3), channel_id=1, source_target_pairs={{0,16},{16,0},{1,17},{17,1},{2,18},{18,2},{3,19},{19,3},{4,20},{20... | collective-permute-start | bytes 2162696 | tf_op jit(solution)/shard_map/ppermute | solution.py:62
  35.3 5.3 %collective-permute-start.9 = (bf16[64,1280]{1,0:T(8,128)(2,1)S(1)}, bf16[64,1280]{1,0:T(8,128)(2,1)S(1)}, u32[]{:S(2)}, u32[]{:S(2)}) collective-permute-start(bf16[64,1280]{1,0:T(8,128)(2,1)S(1)} %pad_maximum_fusion.14), channel_id=1, source_target_pairs={{0,4},{4,0},{8,12},{12,8},{1,5},{5,1},{9,13},{13,9},{2,6},{6,2},{1... | collective-permute-start | bytes 491528 | tf_op jit(solution)/shard_map/ppermute | solution.py:62
  35.8 20.0 %collective-permute-start.13 = (bf16[128,1152]{1,0:T(8,128)(2,1)S(1)}, bf16[128,1152]{1,0:T(8,128)(2,1)S(1)}, u32[]{:S(2)}, u32[]{:S(2)}) collective-permute-start(bf16[128,1152]{1,0:T(8,128)(2,1)S(1)} %pad_maximum_fusion.11), channel_id=1, source_target_pairs={{0,2},{2,0},{1,3},{3,1},{4,6},{6,4},{5,7},{7,5},{8,10},{10,8},{9,1... | collective-permute-start | bytes 884744 | tf_op jit(solution)/shard_map/ppermute | solution.py:62
  40.7 19.2 %slice-start.3 = ((s8[7864320]{0:T(1024)(128)(4,1)}), s8[3670016]{0:T(1024)(128)(4,1)S(1)}, s32[]{:S(2)}) async-start(s8[7864320]{0:T(1024)(128)(4,1)} %bitcast.117), calls=%async_computation.3 | async-start | bytes 7340032
  40.7 17.1 %collective-permute-start.10 = (bf16[128,1280]{1,0:T(8,128)(2,1)S(1)}, bf16[128,1280]{1,0:T(8,128)(2,1)S(1)}, u32[]{:S(2)}, u32[]{:S(2)}) collective-permute-start(bf16[128,1280]{1,0:T(8,128)(2,1)S(1)} %pad_maximum_fusion.10), channel_id=1, source_target_pairs={{0,16},{16,0},{1,17},{17,1},{2,18},{18,2},{3,19},{19,3},{4,20},{20... | collective-permute-start | bytes 983048 | tf_op jit(solution)/shard_map/ppermute | solution.py:62
  57.8 14.8 %collective-permute-start.14 = (bf16[256,1280]{1,0:T(8,128)(2,1)S(1)}, bf16[256,1280]{1,0:T(8,128)(2,1)S(1)}, u32[]{:S(2)}, u32[]{:S(2)}) collective-permute-start(bf16[256,1280]{1,0:T(8,128)(2,1)S(1)} %pad_maximum_fusion.5), channel_id=1, source_target_pairs={{0,2},{2,0},{1,3},{3,1},{4,6},{6,4},{5,7},{7,5},{8,10},{10,8},{9,1... | collective-permute-start | bytes 1966088 | tf_op jit(solution)/shard_map/ppermute | solution.py:62
  58.6 14.0 %collective-permute-start.15 = (bf16[256,1152]{1,0:T(8,128)(2,1)S(1)}, bf16[256,1152]{1,0:T(8,128)(2,1)S(1)}, u32[]{:S(2)}, u32[]{:S(2)}) collective-permute-start(bf16[256,1152]{1,0:T(8,128)(2,1)S(1)} %pad_maximum_fusion.6), channel_id=1, source_target_pairs={{0,16},{16,0},{1,17},{17,1},{2,18},{18,2},{3,19},{19,3},{4,20},{20... | collective-permute-start | bytes 1769480 | tf_op jit(solution)/shard_map/ppermute | solution.py:62
  59.2 7.7 %collective-permute-start.17 = (bf16[512,1408]{1,0:T(8,128)(2,1)S(1)}, bf16[512,1408]{1,0:T(8,128)(2,1)S(1)}, u32[]{:S(2)}, u32[]{:S(2)}) collective-permute-start(bf16[512,1408]{1,0:T(8,128)(2,1)S(1)} %slice_dynamic-update-slice_fusion), channel_id=1, source_target_pairs={{0,1},{1,0},{2,3},{3,2},{4,5},{5,4},{6,7},{7,6},{8,9},{9,8},{10,11... | collective-permute-start | bytes 4325384 | tf_op jit(solution)/shard_map/ppermute | solution.py:62
  59.3 9.1 %collective-permute-start.16 = (bf16[512,1408]{1,0:T(8,128)(2,1)S(1)}, bf16[512,1408]{1,0:T(8,128)(2,1)S(1)}, u32[]{:S(2)}, u32[]{:S(2)}) collective-permute-start(bf16[512,1408]{1,0:T(8,128)(2,1)S(1)} %constant_dynamic-update-slice_fusion), channel_id=1, source_target_pairs={{0,1},{1,0},{2,3},{3,2},{4,5},{5,4},{6,7},{7,6},{8,9},{9,8},{10,11... | collective-permute-start | bytes 4325384 | tf_op jit(solution)/shard_map/ppermute | solution.py:62
  59.8 4.1 %slice-start = ((s8[7864320]{0:T(1024)(128)(4,1)}), s8[4194304]{0:T(1024)(128)(4,1)S(1)}, s32[]{:S(2)}) async-start(s8[7864320]{0:T(1024)(128)(4,1)} %bitcast.113), calls=%async_computation | async-start | bytes 8388608
  61.3 2.7 %slice-start.1 = ((s8[7864320]{0:T(1024)(128)(4,1)}), s8[3670016]{0:T(1024)(128)(4,1)S(1)}, s32[]{:S(2)}) async-start(s8[7864320]{0:T(1024)(128)(4,1)} %bitcast.113), calls=%async_computation.1 | async-start | bytes 7340032
  72.8 4.6 %collective-permute-start.19 = (bf16[512,1152]{1,0:T(8,128)(2,1)S(1)}, bf16[512,1152]{1,0:T(8,128)(2,1)S(1)}, u32[]{:S(2)}, u32[]{:S(2)}) collective-permute-start(bf16[512,1152]{1,0:T(8,128)(2,1)S(1)} %pad_maximum_fusion.1), channel_id=1, source_target_pairs={{0,1},{1,0},{2,3},{3,2},{4,5},{5,4},{6,7},{7,6},{8,9},{9,8},{10,11... | collective-permute-start | bytes 3538952 | tf_op jit(solution)/shard_map/ppermute | solution.py:62
  72.9 5.7 %collective-permute-start.18 = (bf16[512,1280]{1,0:T(8,128)(2,1)S(1)}, bf16[512,1280]{1,0:T(8,128)(2,1)S(1)}, u32[]{:S(2)}, u32[]{:S(2)}) collective-permute-start(bf16[512,1280]{1,0:T(8,128)(2,1)S(1)} %constant_dynamic-update-slice_fusion.9), channel_id=1, source_target_pairs={{0,1},{1,0},{2,3},{3,2},{4,5},{5,4},{6,7},{7,6},{8,9},{9,8},{10,11... | collective-permute-start | bytes 3932168 | tf_op jit(solution)/shard_map/ppermute | solution.py:62
  79.8 2.9 %slice-start.4 = ((s8[7864320]{0:T(1024)(128)(4,1)}), s8[4194304]{0:T(1024)(128)(4,1)S(1)}, s32[]{:S(2)}) async-start(s8[7864320]{0:T(1024)(128)(4,1)} %bitcast.119), calls=%async_computation.4 | async-start | bytes 8388608
  85.9 6.9 %collective-permute-start.30 = (bf16[512,1152]{1,0:T(8,128)(2,1)S(1)}, bf16[512,1152]{1,0:T(8,128)(2,1)S(1)}, u32[]{:S(2)}, u32[]{:S(2)}) collective-permute-start(bf16[512,1152]{1,0:T(8,128)(2,1)S(1)} %convolution_convert_fusion.1), channel_id=1, source_target_pairs={{0,1},{1,0},{2,3},{3,2},{4,5},{5,4},{6,7},{7,6},{8,9},{9,8},{10,11... | collective-permute-start | bytes 3538952 | tf_op jit(solution)/shard_map/ppermute | solution.py:62
  86.0 5.4 %collective-permute-start.35 = (bf16[512,1152]{1,0:T(8,128)(2,1)S(1)}, bf16[512,1152]{1,0:T(8,128)(2,1)S(1)}, u32[]{:S(2)}, u32[]{:S(2)}) collective-permute-start(bf16[512,1152]{1,0:T(8,128)(2,1)S(1)} %convolution_convert_fusion), channel_id=1, source_target_pairs={{0,1},{1,0},{2,3},{3,2},{4,5},{5,4},{6,7},{7,6},{8,9},{9,8},{10,11... | collective-permute-start | bytes 3538952 | tf_op jit(solution)/shard_map/ppermute | solution.py:62
  87.9 11.1 %collective-permute-start.20 = (bf16[512,1408]{1,0:T(8,128)(2,1)S(1)}, bf16[512,1408]{1,0:T(8,128)(2,1)S(1)}, u32[]{:S(2)}, u32[]{:S(2)}) collective-permute-start(bf16[512,1408]{1,0:T(8,128)(2,1)S(1)} %convolution_convert_fusion.3), channel_id=1, source_target_pairs={{0,1},{1,0},{2,3},{3,2},{4,5},{5,4},{6,7},{7,6},{8,9},{9,8},{10,11... | collective-permute-start | bytes 4325384 | tf_op jit(solution)/shard_map/ppermute | solution.py:62
  89.4 8.0 %collective-permute-start.25 = (bf16[512,1408]{1,0:T(8,128)(2,1)S(1)}, bf16[512,1408]{1,0:T(8,128)(2,1)S(1)}, u32[]{:S(2)}, u32[]{:S(2)}) collective-permute-start(bf16[512,1408]{1,0:T(8,128)(2,1)S(1)} %convolution_convert_fusion.2), channel_id=1, source_target_pairs={{0,1},{1,0},{2,3},{3,2},{4,5},{5,4},{6,7},{7,6},{8,9},{9,8},{10,11... | collective-permute-start | bytes 4325384 | tf_op jit(solution)/shard_map/ppermute | solution.py:62
  94.3 16.3 %collective-permute-start.31 = (bf16[256,1152]{1,0:T(8,128)(2,1)S(1)}, bf16[256,1152]{1,0:T(8,128)(2,1)S(1)}, u32[]{:S(2)}, u32[]{:S(2)}) collective-permute-start(bf16[256,1152]{1,0:T(8,128)(2,1)S(1)} %split.133), channel_id=1, source_target_pairs={{0,2},{2,0},{1,3},{3,1},{4,6},{6,4},{5,7},{7,5},{8,10},{10,8},{9,1... | collective-permute-start | bytes 1769480 | tf_op jit(solution)/shard_map/ppermute | solution.py:62
  95.9 16.3 %collective-permute-start.36 = (bf16[256,1152]{1,0:T(8,128)(2,1)S(1)}, bf16[256,1152]{1,0:T(8,128)(2,1)S(1)}, u32[]{:S(2)}, u32[]{:S(2)}) collective-permute-start(bf16[256,1152]{1,0:T(8,128)(2,1)S(1)} %pad_maximum_fusion.7), channel_id=1, source_target_pairs={{0,16},{16,0},{1,17},{17,1},{2,18},{18,2},{3,19},{19,3},{4,20},{20... | collective-permute-start | bytes 1769480 | tf_op jit(solution)/shard_map/ppermute | solution.py:62
  100.5 25.5 %collective-permute-start.21 = (bf16[256,1408]{1,0:T(8,128)(2,1)S(1)}, bf16[256,1408]{1,0:T(8,128)(2,1)S(1)}, u32[]{:S(2)}, u32[]{:S(2)}) collective-permute-start(bf16[256,1408]{1,0:T(8,128)(2,1)S(1)} %split.123), channel_id=1, source_target_pairs={{0,2},{2,0},{1,3},{3,1},{4,6},{6,4},{5,7},{7,5},{8,10},{10,8},{9,1... | collective-permute-start | bytes 2162696 | tf_op jit(solution)/shard_map/ppermute | solution.py:62
  101.2 26.6 %collective-permute-start.26 = (bf16[256,1408]{1,0:T(8,128)(2,1)S(1)}, bf16[256,1408]{1,0:T(8,128)(2,1)S(1)}, u32[]{:S(2)}, u32[]{:S(2)}) collective-permute-start(bf16[256,1408]{1,0:T(8,128)(2,1)S(1)} %pad_maximum_fusion.4), channel_id=1, source_target_pairs={{0,16},{16,0},{1,17},{17,1},{2,18},{18,2},{3,19},{19,3},{4,20},{20... | collective-permute-start | bytes 2162696 | tf_op jit(solution)/shard_map/ppermute | solution.py:62
  112.4 19.0 %collective-permute-start.37 = (bf16[128,1152]{1,0:T(8,128)(2,1)S(1)}, bf16[128,1152]{1,0:T(8,128)(2,1)S(1)}, u32[]{:S(2)}, u32[]{:S(2)}) collective-permute-start(bf16[128,1152]{1,0:T(8,128)(2,1)S(1)} %split.141), channel_id=1, source_target_pairs={{0,2},{2,0},{1,3},{3,1},{4,6},{6,4},{5,7},{7,5},{8,10},{10,8},{9,1... | collective-permute-start | bytes 884744 | tf_op jit(solution)/shard_map/ppermute | solution.py:62
  113.0 21.0 %collective-permute-start.32 = (bf16[128,1152]{1,0:T(8,128)(2,1)S(1)}, bf16[128,1152]{1,0:T(8,128)(2,1)S(1)}, u32[]{:S(2)}, u32[]{:S(2)}) collective-permute-start(bf16[128,1152]{1,0:T(8,128)(2,1)S(1)} %split.135), channel_id=1, source_target_pairs={{0,16},{16,0},{1,17},{17,1},{2,18},{18,2},{3,19},{19,3},{4,20},{20... | collective-permute-start | bytes 884744 | tf_op jit(solution)/shard_map/ppermute | solution.py:62
  126.2 19.0 %collective-permute-start.22 = (bf16[128,1408]{1,0:T(8,128)(2,1)S(1)}, bf16[128,1408]{1,0:T(8,128)(2,1)S(1)}, u32[]{:S(2)}, u32[]{:S(2)}) collective-permute-start(bf16[128,1408]{1,0:T(8,128)(2,1)S(1)} %split.125), channel_id=1, source_target_pairs={{0,16},{16,0},{1,17},{17,1},{2,18},{18,2},{3,19},{19,3},{4,20},{20... | collective-permute-start | bytes 1081352 | tf_op jit(solution)/shard_map/ppermute | solution.py:62
  134.0 5.2 %collective-permute-start.38 = (bf16[64,1152]{1,0:T(8,128)(2,1)S(1)}, bf16[64,1152]{1,0:T(8,128)(2,1)S(1)}, u32[]{:S(2)}, u32[]{:S(2)}) collective-permute-start(bf16[64,1152]{1,0:T(8,128)(2,1)S(1)} %slice.190), channel_id=1, source_target_pairs={{0,4},{4,0},{8,12},{12,8},{1,5},{5,1},{9,13},{13,9},{2,6},{6,2},{1... | collective-permute-start | bytes 442376 | tf_op jit(solution)/shard_map/ppermute | solution.py:62
  135.9 7.1 %collective-permute-start.33 = (bf16[64,1152]{1,0:T(8,128)(2,1)S(1)}, bf16[64,1152]{1,0:T(8,128)(2,1)S(1)}, u32[]{:S(2)}, u32[]{:S(2)}) collective-permute-start(bf16[64,1152]{1,0:T(8,128)(2,1)S(1)} %slice.186), channel_id=1, source_target_pairs={{0,4},{4,0},{8,12},{12,8},{1,5},{5,1},{9,13},{13,9},{2,6},{6,2},{1... | collective-permute-start | bytes 442376 | tf_op jit(solution)/shard_map/ppermute | solution.py:62
  136.2 10.6 %collective-permute-start.27 = (bf16[128,1408]{1,0:T(8,128)(2,1)S(1)}, bf16[128,1408]{1,0:T(8,128)(2,1)S(1)}, u32[]{:S(2)}, u32[]{:S(2)}) collective-permute-start(bf16[128,1408]{1,0:T(8,128)(2,1)S(1)} %split.131), channel_id=1, source_target_pairs={{0,2},{2,0},{1,3},{3,1},{4,6},{6,4},{5,7},{7,5},{8,10},{10,8},{9,1... | collective-permute-start | bytes 1081352 | tf_op jit(solution)/shard_map/ppermute | solution.py:62
  139.3 16.9 %collective-permute-start.39 = (bf16[32,1152]{1,0:T(8,128)(2,1)S(1)}, bf16[32,1152]{1,0:T(8,128)(2,1)S(1)}, u32[]{:S(2)}, u32[]{:S(2)}) collective-permute-start(bf16[32,1152]{1,0:T(8,128)(2,1)S(1)} %slice.192), channel_id=1, source_target_pairs={{0,8},{4,12},{8,0},{12,4},{1,9},{5,13},{9,1},{13,5},{2,10},{6,14},... | collective-permute-start | bytes 221192 | tf_op jit(solution)/shard_map/ppermute | solution.py:62
  143.1 13.0 %collective-permute-start.34 = (bf16[32,1152]{1,0:T(8,128)(2,1)S(1)}, bf16[32,1152]{1,0:T(8,128)(2,1)S(1)}, u32[]{:S(2)}, u32[]{:S(2)}) collective-permute-start(bf16[32,1152]{1,0:T(8,128)(2,1)S(1)} %slice.188), channel_id=1, source_target_pairs={{0,8},{4,12},{8,0},{12,4},{1,9},{5,13},{9,1},{13,5},{2,10},{6,14},... | collective-permute-start | bytes 221192 | tf_op jit(solution)/shard_map/ppermute | solution.py:62
  145.3 10.8 %copy-start.2 = (bf16[1,32,5120]{2,1,0:T(8,128)(2,1)S(1)}, bf16[1,32,5120]{2,1,0:T(8,128)(2,1)}, u32[]{:S(2)}) copy-start(bf16[1,32,5120]{2,1,0:T(8,128)(2,1)} %param.6) | copy-start | bytes 983044
  145.4 6.9 %collective-permute-start.23 = (bf16[64,1408]{1,0:T(8,128)(2,1)S(1)}, bf16[64,1408]{1,0:T(8,128)(2,1)S(1)}, u32[]{:S(2)}, u32[]{:S(2)}) collective-permute-start(bf16[64,1408]{1,0:T(8,128)(2,1)S(1)} %slice.178), channel_id=1, source_target_pairs={{0,4},{4,0},{8,12},{12,8},{1,5},{5,1},{9,13},{13,9},{2,6},{6,2},{1... | collective-permute-start | bytes 540680 | tf_op jit(solution)/shard_map/ppermute | solution.py:62
  147.0 15.5 %copy-start.1 = (s32[1,64,6]{1,0,2:T(1,128)S(1)}, s32[1,64,6]{1,0,2:T(1,128)}, u32[]{:S(2)}) copy-start(s32[1,64,6]{1,0,2:T(1,128)} %param.7) | copy-start | bytes 4612
  147.0 8.1 %collective-permute-start.28 = (bf16[64,1408]{1,0:T(8,128)(2,1)S(1)}, bf16[64,1408]{1,0:T(8,128)(2,1)S(1)}, u32[]{:S(2)}, u32[]{:S(2)}) collective-permute-start(bf16[64,1408]{1,0:T(8,128)(2,1)S(1)} %slice.182), channel_id=1, source_target_pairs={{0,4},{4,0},{8,12},{12,8},{1,5},{5,1},{9,13},{13,9},{2,6},{6,2},{1... | collective-permute-start | bytes 540680 | tf_op jit(solution)/shard_map/ppermute | solution.py:62
  152.3 5.5 %collective-permute-start.24 = (bf16[32,1408]{1,0:T(8,128)(2,1)S(1)}, bf16[32,1408]{1,0:T(8,128)(2,1)S(1)}, u32[]{:S(2)}, u32[]{:S(2)}) collective-permute-start(bf16[32,1408]{1,0:T(8,128)(2,1)S(1)} %slice.180), channel_id=1, source_target_pairs={{0,8},{4,12},{8,0},{12,4},{1,9},{5,13},{9,1},{13,5},{2,10},{6,14},... | collective-permute-start | bytes 270344 | tf_op jit(solution)/shard_map/ppermute | solution.py:62
  155.2 6.5 %collective-permute-start.29 = (bf16[32,1408]{1,0:T(8,128)(2,1)S(1)}, bf16[32,1408]{1,0:T(8,128)(2,1)S(1)}, u32[]{:S(2)}, u32[]{:S(2)}) collective-permute-start(bf16[32,1408]{1,0:T(8,128)(2,1)S(1)} %slice.184), channel_id=1, source_target_pairs={{0,8},{4,12},{8,0},{12,4},{1,9},{5,13},{9,1},{13,5},{2,10},{6,14},... | collective-permute-start | bytes 270344 | tf_op jit(solution)/shard_map/ppermute | solution.py:62
  (2 other events, 4.3 us)

commit v2 on v1

--- a/solution.py
+++ b/solution.py
@@ -4,7 +4,6 @@
 from jax.sharding import Mesh, PartitionSpec as P
 
 CHUNK_EDGES = (0, 11, 22, 31, 40)
-SCATTER_ORDER = (2, 3, 0, 1)
 GAIN_CHUNK = 2
 LANES = 128
 
@@ -78,11 +77,24 @@
     return jnp.pad(columns, ((0, 0), (0, LANES - columns.shape[1])))
 
 
-def ordered(blocks, y_first):
-    return [blocks[0], blocks[2], blocks[1], blocks[3]] if y_first else blocks
-
-
-def grown(value, *flip):
+FAR, NEAR = ("z", 2), ("z", 1)
+STAGES = (
+    (FAR, NEAR, ("x",), ("y",)),
+    (FAR, NEAR, ("y",), ("x",)),
+    (("x",), FAR, NEAR, ("y",)),
+    (("y",), FAR, NEAR, ("x",)),
+)
+
+
+def ordered(value, old, new):
+    if old == new:
+        return value
+    blocks = value.reshape((2,) * len(old) + (-1, value.shape[1]))
+    axes = [old[::-1].index(flip) for flip in new[::-1]]
+    return jnp.transpose(blocks, axes + [len(old), len(old) + 1]).reshape(value.shape)
+
+
+def grown(value, flip):
     return jnp.concatenate([value, swap(value, *flip)], axis=0)
 
 
@@ -90,7 +102,7 @@
     return (a.astype(jnp.float32) + b.astype(jnp.float32)).astype(jnp.bfloat16)
 
 
-def halved(value, *flip):
+def halved(value, flip):
     cut = value.shape[0] // 2
     return added(value[:cut], swap(value[cut:], *flip))
 
@@ -109,33 +121,29 @@
     edges = [width * part // CHUNK_EDGES[-1] for part in CHUNK_EDGES]
     spans = [slice(start, stop) for start, stop in zip(edges, edges[1:])]
     n_chunks = len(spans)
-    planes = [("x", "y") if c % 2 == 0 else ("y", "x") for c in range(n_chunks)]
     dims = (((1,), (1,)), ((), ()))
 
-    far, in_z, in_first, received = {}, [], [], []
-    for c in range(n_chunks):
-        value = block[:, spans[c]]
-        if c == GAIN_CHUNK:
-            value = jnp.concatenate([value, columns], axis=1)
-        if c >= 2:
-            value = after(value, *in_z[:2])
-        far[c] = grown(value, "z", 2)
-        in_z.append(grown(after(far[c], *in_first[:2]) if c >= 2 else far[c], "z", 1))
-        value = grown(in_z[c], planes[c][0])
-        in_first.append(value)
-        if c < 2:
-            received.append(swap(value, planes[c][1]))
-    joined = lax.optimization_barrier(received + in_first[2:])
-    in_first[2:] = joined[2:]
-    received = joined[:2] + [swap(in_first[c], planes[c][1]) for c in (2, 3)]
+    chunks = [block[:, span] for span in spans]
+    one, two = (0, 1), (2, 3)
+    in_far = [grown(chunks[c], FAR) for c in one]
+    in_z = [grown(value, NEAR) for value in in_far]
+    before_last = [grown(value, STAGES[c][2]) for c, value in zip(one, in_z)]
+    flipped = [grown(after(chunks[c], *in_far), STAGES[c][0]) for c in two]
+    at = GAIN_CHUNK - two[0]
+    flipped[at] = jnp.concatenate([flipped[at], grown(after(columns, *in_far), STAGES[GAIN_CHUNK][0])], axis=1)
+    far = [grown(after(value, *in_z), FAR) for value in flipped]
+    near = [grown(after(value, *before_last), NEAR) for value in far]
+    received = [swap(value, *STAGES[c][3]) for c, value in zip(one, before_last)]
+    joined = lax.optimization_barrier(received + near)
+    before_last += joined[2:]
+    received = joined[:2] + [swap(before_last[c], *STAGES[c][3]) for c in two]
 
     halves = [{"gate": 0.0, "up": 0.0}, {"gate": 0.0, "up": 0.0}]
     for c in range(n_chunks):
         if c == 2:
             ties = [sums[name] for sums in halves for name in ("gate", "up")]
             received[2:] = lax.optimization_barrier(received[2:] + ties)[:2]
-        pieces = jnp.split(in_first[c], 2, axis=0) + jnp.split(received[c], 2, axis=0)
-        own = jnp.concatenate(ordered(pieces, c % 2 == 1), axis=0)
+        own = ordered(jnp.concatenate([before_last[c], received[c]], axis=0), STAGES[c], STAGES[0])
         for rows, sums in zip((own, swap(own, "core")), halves):
             if c == GAIN_CHUNK:
                 lane = lax.broadcasted_iota(jnp.int32, (rows.shape[0], LANES), 1)
@@ -154,27 +162,27 @@
         return jnp.dot(value, down_weight[0, :, spans[c]], preferred_element_type=jnp.float32)
 
     away = act(1)
-    to_core = {c: down(away, c).astype(jnp.bfloat16) for c in SCATTER_ORDER[:2]}
+    to_core = {c: down(ordered(away, STAGES[0], STAGES[c]), c).astype(jnp.bfloat16) for c in two}
     here = act(0, *to_core.values())
     away = after(away, *to_core.values())
-    to_core.update({c: down(away, c).astype(jnp.bfloat16) for c in SCATTER_ORDER[2:]})
-    parts, sent, kept = {}, {}, {}
-    for c in SCATTER_ORDER:
-        part = (down(here, c) + swap(to_core[c], "core").astype(jnp.float32)).astype(jnp.bfloat16)
-        parts[c] = jnp.concatenate(ordered(jnp.split(part, 4, axis=0), c % 2 == 1), axis=0)
+    to_core.update({c: down(ordered(away, STAGES[0], STAGES[c]), c).astype(jnp.bfloat16) for c in one})
+    parts, kept, sent = {}, {}, {}
+    for c in two + one:
+        parts[c] = added(down(ordered(here, STAGES[0], STAGES[c]), c), swap(to_core[c], "core"))
         kept[c], goes = jnp.split(parts[c], 2, axis=0)
-        sent[c] = swap(goes, planes[c][1])
-    following = {c: SCATTER_ORDER[i + 2 - i % 2:i + 4 - i % 2] for i, c in enumerate(SCATTER_ORDER)}
-    outs, first = {}, {}
-    for c in SCATTER_ORDER:
-        first[c] = added(kept[c], after(sent[c], *[parts[d] for d in following[c]]))
-    for c in SCATTER_ORDER:
-        stays, goes = jnp.split(first[c], 2, axis=0)
-        part = added(stays, after(swap(goes, planes[c][0]), *[first[d] for d in following[c]]))
-        part = halved(part, "z", 1)
-        total = block[:, spans[c]].astype(jnp.float32) + part[:half].astype(jnp.float32)
-        total += swap(part[half:], "z", 2).astype(jnp.float32)
-        outs[c] = total.astype(jnp.bfloat16)
+        sent[c] = swap(goes, *STAGES[c][3])
+    first = {c: added(kept[c], sent[c]) for c in one}
+    outs = {}
+    for c in two:
+        value = halved(added(kept[c], after(sent[c], *[parts[d] for d in one])), NEAR)
+        stays, goes = jnp.split(value, 2, axis=0)
+        value = added(stays, after(swap(goes, *FAR), *first.values()))
+        outs[c] = (value, STAGES[c][0])
+    for c in one:
+        outs[c] = (halved(halved(first[c], STAGES[c][2]), NEAR), FAR)
+    for c, (value, flip) in outs.items():
+        total = block[:, spans[c]].astype(jnp.float32) + value[:half].astype(jnp.float32)
+        outs[c] = (total + swap(value[half:], *flip).astype(jnp.float32)).astype(jnp.bfloat16)
     return jnp.concatenate([outs[c] for c in range(n_chunks)], axis=1)[None]
 
 

time: 163 us -> 157 us (0.963)
  waiting for transfers between devices: 74.7 us -> 64 us
  starting transfers between devices: 45.9 us -> 49.9 us
  local copies, waits for them, and re-layouts: 4.6 us -> 6.43 us
    ppermute x40 -> x41, waiting for transfers between devices: 74.7 us -> 64 us  [swap(): return lax.ppermute(value, axis, [(i, i ^ flip) for i in range(size)])]
    ppermute x40 -> x41, starting transfers between devices: 45.9 us -> 49.9 us  [swap(): return lax.ppermute(value, axis, [(i, i ^ flip) for i in range(size)])]
    unnamed x32 -> x29, local copies, waits for them, and re-layouts: 2.08 us -> 3.34 us
  transfers between devices with their start and end apart: 40 -> 41, of which waited for: 21 -> 20; matrix products, arithmetic and copies ran while one was open for 20% -> 20% of each run, Pallas kernels for 0% -> 0%
where the time goes in v2:
time: 157 us
  waiting for transfers between devices  64 us (41%)
  starting transfers between devices  49.9 us (32%)
  matrix products  32.6 us (21%)
  local copies, waits for them, and re-layouts  6.43 us (4%)
  other arithmetic  2.87 us (2%)
    ppermute x41, waiting for transfers between devices, swap(): return lax.ppermute(value, axis, [(i, i ^ flip) for i in range(size)])  64 us
    ppermute x41, starting transfers between devices, swap(): return lax.ppermute(value, axis, [(i, i ^ flip) for i in range(size)])  49.9 us
    dot_general x16, matrix products, ring_body(): lax.dot_general(rows, weight[0, :, spans[c]], dims, preferred_element_typ...  21.9 us
    dot_general x8, matrix products, down(): jnp.dot(value, down_weight[0, :, spans[c]], preferred_element_type=jnp.fl...  10.8 us
    unnamed x29, local copies, waits for them, and re-layouts  3.34 us
  transfers between devices with their start and end apart: 41, of which 20 were waited for; matrix products, arithmetic and copies ran while one was open for 20% of the time, Pallas kernels for 0%

profile of v2, /device:TPU:0, one launch (start us, length us, event | category | flops | bytes accessed | tf_op | source)
XLA Modules:
  0.0 156.7 jit_solution(17937959590809214208)
XLA Ops:
  0.0 1.6 %constant_dynamic-update-slice_fusion.4 = (bf16[512,1408]{1,0:T(8,128)(2,1)}, bf16[512,1408]{1,0:T(8,128)(2,1)S(1)}, bf16[32,1408]{1,0:T(8,128)(2,1)S(1)}, bf16[32,1408]{1,0:T(8,128)(2,1)S(1)}) fusion(bf16[32,5120]{1,0:T(8,128)(2,1)} %bitcast.160), kind=kLoop, calls=%fused_computation.133 | loop fusion | bytes 540672
  1.6 4.0 %collective-permute-start.4 = (bf16[32,1408]{1,0:T(8,128)(2,1)S(1)}, bf16[32,1408]{1,0:T(8,128)(2,1)S(1)}, u32[]{:S(2)}, u32[]{:S(2)}) collective-permute-start(bf16[32,1408]{1,0:T(8,128)(2,1)S(1)} %get-tuple-element.51), channel_id=1, source_target_pairs={{0,8},{4,12},{8,0},{12,4},{1,9},{5,13},{9,1},{13,5},{2,10},{6,14},... | collective-permute-start | bytes 270344 | tf_op jit(solution)/shard_map/ppermute | solution.py:61
  7.6 5.3 %collective-permute-done.4 = bf16[32,1408]{1,0:T(8,128)(2,1)S(1)} collective-permute-done((bf16[32,1408]{1,0:T(8,128)(2,1)S(1)}, bf16[32,1408]{1,0:T(8,128)(2,1)S(1)}, u32[]{:S(2)}, u32[]{:S(2)}) %collective-permute-start.4) | collective-permute-done | bytes 90144 | tf_op jit(solution)/shard_map/ppermute | solution.py:61
  15.0 1.7 %collective-permute-start.9 = (bf16[32,128]{0,1:T(8,128)(2,1)S(1)}, bf16[32,128]{0,1:T(8,128)(2,1)S(1)}, u32[]{:S(2)}, u32[]{:S(2)}) collective-permute-start(bf16[32,128]{0,1:T(8,128)(2,1)S(1)} %fusion.100), channel_id=1, source_target_pairs={{0,16},{16,0},{1,17},{17,1},{2,18},{18,2},{3,19},{19,3},{4,20},{20... | collective-permute-start | bytes 24584 | tf_op jit(solution)/shard_map/ppermute | solution.py:61
  17.0 1.7 %collective-permute-start.12 = (bf16[32,1152]{1,0:T(8,128)(2,1)S(1)}, bf16[32,1152]{1,0:T(8,128)(2,1)S(1)}, u32[]{:S(2)}, u32[]{:S(2)}) collective-permute-start(bf16[32,1152]{1,0:T(8,128)(2,1)S(1)} %get-tuple-element.28), channel_id=1, source_target_pairs={{0,2},{2,0},{1,3},{3,1},{4,6},{6,4},{5,7},{7,5},{8,10},{10,8},{9,1... | collective-permute-start | bytes 221192 | tf_op jit(solution)/shard_map/ppermute | solution.py:61
  19.6 1.8 %collective-permute-done.12 = bf16[32,1152]{1,0:T(8,128)(2,1)S(1)} collective-permute-done((bf16[32,1152]{1,0:T(8,128)(2,1)S(1)}, bf16[32,1152]{1,0:T(8,128)(2,1)S(1)}, u32[]{:S(2)}, u32[]{:S(2)}) %collective-permute-start.12) | collective-permute-done | bytes 73760 | tf_op jit(solution)/shard_map/ppermute | solution.py:61
  21.5 1.8 %collective-permute-start.6 = (bf16[128,1408]{1,0:T(8,128)(2,1)S(1)}, bf16[128,1408]{1,0:T(8,128)(2,1)S(1)}, u32[]{:S(2)}, u32[]{:S(2)}) collective-permute-start(bf16[128,1408]{1,0:T(8,128)(2,1)S(1)} %pad_maximum_fusion.7), channel_id=1, source_target_pairs={{0,2},{2,0},{1,3},{3,1},{4,6},{6,4},{5,7},{7,5},{8,10},{10,8},{9,1... | collective-permute-start | bytes 1081352 | tf_op jit(solution)/shard_map/ppermute | solution.py:61
  23.3 1.6 collective-permute-start.2
  24.9 3.0 %collective-permute-start.13 = (bf16[64,1152]{1,0:T(8,128)(2,1)S(1)}, bf16[64,1152]{1,0:T(8,128)(2,1)S(1)}, u32[]{:S(2)}, u32[]{:S(2)}) collective-permute-start(bf16[64,1152]{1,0:T(8,128)(2,1)S(1)} %pad_maximum_fusion.13), channel_id=1, source_target_pairs={{0,8},{4,12},{8,0},{12,4},{1,9},{5,13},{9,1},{13,5},{2,10},{6,14},... | collective-permute-start | bytes 442376 | tf_op jit(solution)/shard_map/ppermute | solution.py:61
  28.0 9.7 %collective-permute-done.13 = bf16[64,1152]{1,0:T(8,128)(2,1)S(1)} collective-permute-done((bf16[64,1152]{1,0:T(8,128)(2,1)S(1)}, bf16[64,1152]{1,0:T(8,128)(2,1)S(1)}, u32[]{:S(2)}, u32[]{:S(2)}) %collective-permute-start.13) | collective-permute-done | bytes 147488 | tf_op jit(solution)/shard_map/ppermute | solution.py:61
  37.8 2.1 %collective-permute-done.10 = bf16[64,1280]{1,0:T(8,128)(2,1)S(1)} collective-permute-done((bf16[64,1280]{1,0:T(8,128)(2,1)S(1)}, bf16[64,1280]{1,0:T(8,128)(2,1)S(1)}, u32[]{:S(2)}, u32[]{:S(2)}) %collective-permute-start.10) | collective-permute-done | bytes 163872 | tf_op jit(solution)/shard_map/ppermute | solution.py:61
  40.0 1.5 collective-permute-start.3
  44.3 7.8 %collective-permute-done.14 = bf16[128,1152]{1,0:T(8,128)(2,1)S(1)} collective-permute-done((bf16[128,1152]{1,0:T(8,128)(2,1)S(1)}, bf16[128,1152]{1,0:T(8,128)(2,1)S(1)}, u32[]{:S(2)}, u32[]{:S(2)}) %collective-permute-start.14) | collective-permute-done | bytes 294944 | tf_op jit(solution)/shard_map/ppermute | solution.py:61
  52.1 4.5 %collective-permute-done.11 = bf16[128,1280]{1,0:T(8,128)(2,1)S(1)} collective-permute-done((bf16[128,1280]{1,0:T(8,128)(2,1)S(1)}, bf16[128,1280]{1,0:T(8,128)(2,1)S(1)}, u32[]{:S(2)}, u32[]{:S(2)}) %collective-permute-start.11) | collective-permute-done | bytes 327712 | tf_op jit(solution)/shard_map/ppermute | solution.py:61
  56.9 1.6 %collective-permute-done.7 = bf16[256,1408]{1,0:T(8,128)(2,1)S(1)} collective-permute-done((bf16[256,1408]{1,0:T(8,128)(2,1)S(1)}, bf16[256,1408]{1,0:T(8,128)(2,1)S(1)}, u32[]{:S(2)}, u32[]{:S(2)}) %collective-permute-start.7) | collective-permute-done | bytes 720928 | tf_op jit(solution)/shard_map/ppermute | solution.py:61
  60.3 1.4 fusion.12
  62.1 1.4 fusion.20
  63.5 1.4 fusion.82
  64.9 1.4 fusion.76
  66.4 1.4 fusion.10
  67.8 1.4 fusion.85
  69.2 1.4 fusion.18
  70.7 1.4 fusion.79
  72.1 1.5 collective-permute-done.15
  75.8 1.4 fusion.52
  82.3 1.6 multiply_convert_fusion.1
  87.6 1.4 convolution_convert_fusion.3
  89.2 1.4 convolution_convert_fusion.2
  91.1 1.5 multiply_convert_fusion
  94.1 1.6 collective-permute-start.37
  95.7 1.5 add_convert_fusion.3
  97.7 1.4 add_convert_fusion.1
  99.2 1.7 %collective-permute-start.22 = (bf16[256,1408]{1,0:T(8,128)(2,1)S(1)}, bf16[256,1408]{1,0:T(8,128)(2,1)S(1)}, u32[]{:S(2)}, u32[]{:S(2)}) collective-permute-start(bf16[256,1408]{1,0:T(8,128)(2,1)S(1)} %split.49), channel_id=1, source_target_pairs={{0,2},{2,0},{1,3},{3,1},{4,6},{6,4},{5,7},{7,5},{8,10},{10,8},{9,1... | collective-permute-start | bytes 2162696 | tf_op jit(solution)/shard_map/ppermute | solution.py:61
  102.9 7.5 %collective-permute-done.37 = bf16[256,1152]{1,0:T(8,128)(2,1)S(1)} collective-permute-done((bf16[256,1152]{1,0:T(8,128)(2,1)S(1)}, bf16[256,1152]{1,0:T(8,128)(2,1)S(1)}, u32[]{:S(2)}, u32[]{:S(2)}) %collective-permute-start.37) | collective-permute-done | bytes 589856 | tf_op jit(solution)/shard_map/ppermute | solution.py:61
  110.5 2.5 %collective-permute-start.38 = (bf16[128,1152]{1,0:T(8,128)(2,1)S(1)}, bf16[128,1152]{1,0:T(8,128)(2,1)S(1)}, u32[]{:S(2)}, u32[]{:S(2)}) collective-permute-start(bf16[128,1152]{1,0:T(8,128)(2,1)S(1)} %slice.201), channel_id=1, source_target_pairs={{0,4},{4,0},{8,12},{12,8},{1,5},{5,1},{9,13},{13,9},{2,6},{6,2},{1... | collective-permute-start | bytes 884744 | tf_op jit(solution)/shard_map/ppermute | solution.py:61
  113.7 2.6 %collective-permute-start.33 = (bf16[128,1152]{1,0:T(8,128)(2,1)S(1)}, bf16[128,1152]{1,0:T(8,128)(2,1)S(1)}, u32[]{:S(2)}, u32[]{:S(2)}) collective-permute-start(bf16[128,1152]{1,0:T(8,128)(2,1)S(1)} %slice.197), channel_id=1, source_target_pairs={{0,4},{4,0},{8,12},{12,8},{1,5},{5,1},{9,13},{13,9},{2,6},{6,2},{1... | collective-permute-start | bytes 884744 | tf_op jit(solution)/shard_map/ppermute | solution.py:61
  116.2 6.4 %collective-permute-done.38 = bf16[128,1152]{1,0:T(8,128)(2,1)S(1)} collective-permute-done((bf16[128,1152]{1,0:T(8,128)(2,1)S(1)}, bf16[128,1152]{1,0:T(8,128)(2,1)S(1)}, u32[]{:S(2)}, u32[]{:S(2)}) %collective-permute-start.38) | collective-permute-done | bytes 294944 | tf_op jit(solution)/shard_map/ppermute | solution.py:61
  122.7 3.0 %collective-permute-start.39 = (bf16[64,1152]{1,0:T(8,128)(2,1)S(1)}, bf16[64,1152]{1,0:T(8,128)(2,1)S(1)}, u32[]{:S(2)}, u32[]{:S(2)}) collective-permute-start(bf16[64,1152]{1,0:T(8,128)(2,1)S(1)} %split.59), channel_id=1, source_target_pairs={{0,8},{4,12},{8,0},{12,4},{1,9},{5,13},{9,1},{13,5},{2,10},{6,14},... | collective-permute-start | bytes 442376 | tf_op jit(solution)/shard_map/ppermute | solution.py:61
  126.6 3.4 %collective-permute-start.34 = (bf16[64,1152]{1,0:T(8,128)(2,1)S(1)}, bf16[64,1152]{1,0:T(8,128)(2,1)S(1)}, u32[]{:S(2)}, u32[]{:S(2)}) collective-permute-start(bf16[64,1152]{1,0:T(8,128)(2,1)S(1)} %split.55), channel_id=1, source_target_pairs={{0,8},{4,12},{8,0},{12,4},{1,9},{5,13},{9,1},{13,5},{2,10},{6,14},... | collective-permute-start | bytes 442376 | tf_op jit(solution)/shard_map/ppermute | solution.py:61
  130.3 1.6 collective-permute-start.23
  132.7 2.8 %collective-permute-done.39 = bf16[64,1152]{1,0:T(8,128)(2,1)S(1)} collective-permute-done((bf16[64,1152]{1,0:T(8,128)(2,1)S(1)}, bf16[64,1152]{1,0:T(8,128)(2,1)S(1)}, u32[]{:S(2)}, u32[]{:S(2)}) %collective-permute-start.39) | collective-permute-done | bytes 147488 | tf_op jit(solution)/shard_map/ppermute | solution.py:61
  135.5 1.9 %collective-permute-done.34 = bf16[64,1152]{1,0:T(8,128)(2,1)S(1)} collective-permute-done((bf16[64,1152]{1,0:T(8,128)(2,1)S(1)}, bf16[64,1152]{1,0:T(8,128)(2,1)S(1)}, u32[]{:S(2)}, u32[]{:S(2)}) %collective-permute-start.34) | collective-permute-done | bytes 147488 | tf_op jit(solution)/shard_map/ppermute | solution.py:61
  138.0 1.5 collective-permute-start.35
  140.6 1.8 %collective-permute-start.29 = (bf16[64,1408]{1,0:T(8,128)(2,1)S(1)}, bf16[64,1408]{1,0:T(8,128)(2,1)S(1)}, u32[]{:S(2)}, u32[]{:S(2)}) collective-permute-start(bf16[64,1408]{1,0:T(8,128)(2,1)S(1)} %slice.193), channel_id=1, source_target_pairs={{0,4},{4,0},{8,12},{12,8},{1,5},{5,1},{9,13},{13,9},{2,6},{6,2},{1... | collective-permute-start | bytes 540680 | tf_op jit(solution)/shard_map/ppermute | solution.py:61
  142.3 4.7 %collective-permute-done.24 = bf16[64,1408]{1,0:T(8,128)(2,1)S(1)} collective-permute-done((bf16[64,1408]{1,0:T(8,128)(2,1)S(1)}, bf16[64,1408]{1,0:T(8,128)(2,1)S(1)}, u32[]{:S(2)}, u32[]{:S(2)}) %collective-permute-start.24) | collective-permute-done | bytes 180256 | tf_op jit(solution)/shard_map/ppermute | solution.py:61
  147.2 2.0 %collective-permute-start.25 = (bf16[32,1408]{1,0:T(8,128)(2,1)S(1)}, bf16[32,1408]{1,0:T(8,128)(2,1)S(1)}, u32[]{:S(2)}, u32[]{:S(2)}) collective-permute-start(bf16[32,1408]{1,0:T(8,128)(2,1)S(1)} %slice.189), channel_id=1, source_target_pairs={{0,8},{4,12},{8,0},{12,4},{1,9},{5,13},{9,1},{13,5},{2,10},{6,14},... | collective-permute-start | bytes 270344 | tf_op jit(solution)/shard_map/ppermute | solution.py:61
  149.4 2.7 %collective-permute-start.30 = (bf16[32,1408]{1,0:T(8,128)(2,1)S(1)}, bf16[32,1408]{1,0:T(8,128)(2,1)S(1)}, u32[]{:S(2)}, u32[]{:S(2)}) collective-permute-start(bf16[32,1408]{1,0:T(8,128)(2,1)S(1)} %slice.195), channel_id=1, source_target_pairs={{0,8},{4,12},{8,0},{12,4},{1,9},{5,13},{9,1},{13,5},{2,10},{6,14},... | collective-permute-start | bytes 270344 | tf_op jit(solution)/shard_map/ppermute | solution.py:61
  153.3 2.6 %collective-permute-done.30 = bf16[32,1408]{1,0:T(8,128)(2,1)S(1)} collective-permute-done((bf16[32,1408]{1,0:T(8,128)(2,1)S(1)}, bf16[32,1408]{1,0:T(8,128)(2,1)S(1)}, u32[]{:S(2)}, u32[]{:S(2)}) %collective-permute-start.30) | collective-permute-done | bytes 90144 | tf_op jit(solution)/shard_map/ppermute | solution.py:61
  (156 shorter events, 33.1 us)
Async XLA Ops:
  0.0 6.6 %copy-start = (s32[1,64,6]{1,0,2:T(1,128)S(1)}, s32[1,64,6]{1,0,2:T(1,128)}, u32[]{:S(2)}) copy-start(s32[1,64,6]{1,0,2:T(1,128)} %param.7) | copy-start | bytes 4612
  1.6 11.2 %collective-permute-start.4 = (bf16[32,1408]{1,0:T(8,128)(2,1)S(1)}, bf16[32,1408]{1,0:T(8,128)(2,1)S(1)}, u32[]{:S(2)}, u32[]{:S(2)}) collective-permute-start(bf16[32,1408]{1,0:T(8,128)(2,1)S(1)} %get-tuple-element.51), channel_id=1, source_target_pairs={{0,8},{4,12},{8,0},{12,4},{1,9},{5,13},{9,1},{13,5},{2,10},{6,14},... | collective-permute-start | bytes 270344 | tf_op jit(solution)/shard_map/ppermute | solution.py:61
  5.6 8.4 %collective-permute-start = (bf16[32,1408]{1,0:T(8,128)(2,1)S(1)}, bf16[32,1408]{1,0:T(8,128)(2,1)S(1)}, u32[]{:S(2)}, u32[]{:S(2)}) collective-permute-start(bf16[32,1408]{1,0:T(8,128)(2,1)S(1)} %get-tuple-element.52), channel_id=1, source_target_pairs={{0,8},{4,12},{8,0},{12,4},{1,9},{5,13},{9,1},{13,5},{2,10},{6,14},... | collective-permute-start | bytes 270344 | tf_op jit(solution)/shard_map/ppermute | solution.py:61
  12.8 8.6 %collective-permute-start.5 = (bf16[64,1408]{1,0:T(8,128)(2,1)S(1)}, bf16[64,1408]{1,0:T(8,128)(2,1)S(1)}, u32[]{:S(2)}, u32[]{:S(2)}) collective-permute-start(bf16[64,1408]{1,0:T(8,128)(2,1)S(1)} %pad_maximum_fusion.11), channel_id=1, source_target_pairs={{0,4},{4,0},{8,12},{12,8},{1,5},{5,1},{9,13},{13,9},{2,6},{6,2},{1... | collective-permute-start | bytes 540680 | tf_op jit(solution)/shard_map/ppermute | solution.py:61
  14.1 9.2 %collective-permute-start.1 = (bf16[64,1408]{1,0:T(8,128)(2,1)S(1)}, bf16[64,1408]{1,0:T(8,128)(2,1)S(1)}, u32[]{:S(2)}, u32[]{:S(2)}) collective-permute-start(bf16[64,1408]{1,0:T(8,128)(2,1)S(1)} %pad_maximum_fusion.10), channel_id=1, source_target_pairs={{0,4},{4,0},{8,12},{12,8},{1,5},{5,1},{9,13},{13,9},{2,6},{6,2},{1... | collective-permute-start | bytes 540680 | tf_op jit(solution)/shard_map/ppermute | solution.py:61
  15.0 4.4 %collective-permute-start.9 = (bf16[32,128]{0,1:T(8,128)(2,1)S(1)}, bf16[32,128]{0,1:T(8,128)(2,1)S(1)}, u32[]{:S(2)}, u32[]{:S(2)}) collective-permute-start(bf16[32,128]{0,1:T(8,128)(2,1)S(1)} %fusion.100), channel_id=1, source_target_pairs={{0,16},{16,0},{1,17},{17,1},{2,18},{18,2},{3,19},{19,3},{4,20},{20... | collective-permute-start | bytes 24584 | tf_op jit(solution)/shard_map/ppermute | solution.py:61
  16.7 4.7 %collective-permute-start.8 = (bf16[32,1152]{1,0:T(8,128)(2,1)S(1)}, bf16[32,1152]{1,0:T(8,128)(2,1)S(1)}, u32[]{:S(2)}, u32[]{:S(2)}) collective-permute-start(bf16[32,1152]{1,0:T(8,128)(2,1)S(1)} %get-tuple-element.24), channel_id=1, source_target_pairs={{0,16},{16,0},{1,17},{17,1},{2,18},{18,2},{3,19},{19,3},{4,20},{20... | collective-permute-start | bytes 221192 | tf_op jit(solution)/shard_map/ppermute | solution.py:61
  17.0 4.4 %collective-permute-start.12 = (bf16[32,1152]{1,0:T(8,128)(2,1)S(1)}, bf16[32,1152]{1,0:T(8,128)(2,1)S(1)}, u32[]{:S(2)}, u32[]{:S(2)}) collective-permute-start(bf16[32,1152]{1,0:T(8,128)(2,1)S(1)} %get-tuple-element.28), channel_id=1, source_target_pairs={{0,2},{2,0},{1,3},{3,1},{4,6},{6,4},{5,7},{7,5},{8,10},{10,8},{9,1... | collective-permute-start | bytes 221192 | tf_op jit(solution)/shard_map/ppermute | solution.py:61
  19.6 8.4 %copy-start.3 = (bf16[512,1408]{1,0:T(8,128)(2,1)S(1)}, bf16[512,1408]{1,0:T(8,128)(2,1)}, u32[]{:S(2)}) copy-start(bf16[512,1408]{1,0:T(8,128)(2,1)} %constant_dynamic-update-slice_fusion.3) | copy-start | bytes 4325380
  21.5 20.0 %collective-permute-start.6 = (bf16[128,1408]{1,0:T(8,128)(2,1)S(1)}, bf16[128,1408]{1,0:T(8,128)(2,1)S(1)}, u32[]{:S(2)}, u32[]{:S(2)}) collective-permute-start(bf16[128,1408]{1,0:T(8,128)(2,1)S(1)} %pad_maximum_fusion.7), channel_id=1, source_target_pairs={{0,2},{2,0},{1,3},{3,1},{4,6},{6,4},{5,7},{7,5},{8,10},{10,8},{9,1... | collective-permute-start | bytes 1081352 | tf_op jit(solution)/shard_map/ppermute | solution.py:61
  23.3 16.6 %collective-permute-start.2 = (bf16[128,1408]{1,0:T(8,128)(2,1)S(1)}, bf16[128,1408]{1,0:T(8,128)(2,1)S(1)}, u32[]{:S(2)}, u32[]{:S(2)}) collective-permute-start(bf16[128,1408]{1,0:T(8,128)(2,1)S(1)} %pad_maximum_fusion.6), channel_id=1, source_target_pairs={{0,16},{16,0},{1,17},{17,1},{2,18},{18,2},{3,19},{19,3},{4,20},{20... | collective-permute-start | bytes 1081352 | tf_op jit(solution)/shard_map/ppermute | solution.py:61
  24.9 12.9 %collective-permute-start.13 = (bf16[64,1152]{1,0:T(8,128)(2,1)S(1)}, bf16[64,1152]{1,0:T(8,128)(2,1)S(1)}, u32[]{:S(2)}, u32[]{:S(2)}) collective-permute-start(bf16[64,1152]{1,0:T(8,128)(2,1)S(1)} %pad_maximum_fusion.13), channel_id=1, source_target_pairs={{0,8},{4,12},{8,0},{12,4},{1,9},{5,13},{9,1},{13,5},{2,10},{6,14},... | collective-permute-start | bytes 442376 | tf_op jit(solution)/shard_map/ppermute | solution.py:61
  27.9 12.0 %collective-permute-start.10 = (bf16[64,1280]{1,0:T(8,128)(2,1)S(1)}, bf16[64,1280]{1,0:T(8,128)(2,1)S(1)}, u32[]{:S(2)}, u32[]{:S(2)}) collective-permute-start(bf16[64,1280]{1,0:T(8,128)(2,1)S(1)} %pad_maximum_fusion.12), channel_id=1, source_target_pairs={{0,8},{4,12},{8,0},{12,4},{1,9},{5,13},{9,1},{13,5},{2,10},{6,14},... | collective-permute-start | bytes 491528 | tf_op jit(solution)/shard_map/ppermute | solution.py:61
  28.0 32.3 %slice-start.2 = ((s8[7864320]{0:T(1024)(128)(4,1)}), s8[4194304]{0:T(1024)(128)(4,1)S(1)}, s32[]{:S(2)}) async-start(s8[7864320]{0:T(1024)(128)(4,1)} %bitcast.177), calls=%async_computation.2 | async-start | bytes 8388608
  40.0 16.9 %collective-permute-start.3 = (bf16[256,1408]{1,0:T(8,128)(2,1)S(1)}, bf16[256,1408]{1,0:T(8,128)(2,1)S(1)}, u32[]{:S(2)}, u32[]{:S(2)}) collective-permute-start(bf16[256,1408]{1,0:T(8,128)(2,1)S(1)} %pad_maximum_fusion.2), channel_id=1, source_target_pairs={{0,2},{2,0},{1,3},{3,1},{4,6},{6,4},{5,7},{7,5},{8,10},{10,8},{9,1... | collective-permute-start | bytes 2162696 | tf_op jit(solution)/shard_map/ppermute | solution.py:61
  41.5 16.9 %collective-permute-start.7 = (bf16[256,1408]{1,0:T(8,128)(2,1)S(1)}, bf16[256,1408]{1,0:T(8,128)(2,1)S(1)}, u32[]{:S(2)}, u32[]{:S(2)}) collective-permute-start(bf16[256,1408]{1,0:T(8,128)(2,1)S(1)} %pad_maximum_fusion.3), channel_id=1, source_target_pairs={{0,16},{16,0},{1,17},{17,1},{2,18},{18,2},{3,19},{19,3},{4,20},{20... | collective-permute-start | bytes 2162696 | tf_op jit(solution)/shard_map/ppermute | solution.py:61
  42.1 9.9 %collective-permute-start.14 = (bf16[128,1152]{1,0:T(8,128)(2,1)S(1)}, bf16[128,1152]{1,0:T(8,128)(2,1)S(1)}, u32[]{:S(2)}, u32[]{:S(2)}) collective-permute-start(bf16[128,1152]{1,0:T(8,128)(2,1)S(1)} %pad_maximum_fusion.9), channel_id=1, source_target_pairs={{0,4},{4,0},{8,12},{12,8},{1,5},{5,1},{9,13},{13,9},{2,6},{6,2},{1... | collective-permute-start | bytes 884744 | tf_op jit(solution)/shard_map/ppermute | solution.py:61
  42.8 13.8 %collective-permute-start.11 = (bf16[128,1280]{1,0:T(8,128)(2,1)S(1)}, bf16[128,1280]{1,0:T(8,128)(2,1)S(1)}, u32[]{:S(2)}, u32[]{:S(2)}) collective-permute-start(bf16[128,1280]{1,0:T(8,128)(2,1)S(1)} %pad_maximum_fusion.8), channel_id=1, source_target_pairs={{0,4},{4,0},{8,12},{12,8},{1,5},{5,1},{9,13},{13,9},{2,6},{6,2},{1... | collective-permute-start | bytes 983048 | tf_op jit(solution)/shard_map/ppermute | solution.py:61
  44.2 16.0 %slice-start.3 = ((s8[7864320]{0:T(1024)(128)(4,1)}), s8[3670016]{0:T(1024)(128)(4,1)S(1)}, s32[]{:S(2)}) async-start(s8[7864320]{0:T(1024)(128)(4,1)} %bitcast.177), calls=%async_computation.3 | async-start | bytes 7340032
  58.5 3.2 %slice-start = ((s8[7864320]{0:T(1024)(128)(4,1)}), s8[4194304]{0:T(1024)(128)(4,1)S(1)}, s32[]{:S(2)}) async-start(s8[7864320]{0:T(1024)(128)(4,1)} %bitcast.173), calls=%async_computation | async-start | bytes 8388608
  58.7 13.4 %collective-permute-start.16 = (bf16[256,1152]{1,0:T(8,128)(2,1)S(1)}, bf16[256,1152]{1,0:T(8,128)(2,1)S(1)}, u32[]{:S(2)}, u32[]{:S(2)}) collective-permute-start(bf16[256,1152]{1,0:T(8,128)(2,1)S(1)} %pad_maximum_fusion.5), channel_id=1, source_target_pairs={{0,16},{16,0},{1,17},{17,1},{2,18},{18,2},{3,19},{19,3},{4,20},{20... | collective-permute-start | bytes 1769480 | tf_op jit(solution)/shard_map/ppermute | solution.py:61
  59.3 14.2 %collective-permute-start.15 = (bf16[256,1280]{1,0:T(8,128)(2,1)S(1)}, bf16[256,1280]{1,0:T(8,128)(2,1)S(1)}, u32[]{:S(2)}, u32[]{:S(2)}) collective-permute-start(bf16[256,1280]{1,0:T(8,128)(2,1)S(1)} %pad_maximum_fusion.4), channel_id=1, source_target_pairs={{0,2},{2,0},{1,3},{3,1},{4,6},{6,4},{5,7},{7,5},{8,10},{10,8},{9,1... | collective-permute-start | bytes 1966088 | tf_op jit(solution)/shard_map/ppermute | solution.py:61
  59.6 6.8 %collective-permute-start.18 = (bf16[512,1408]{1,0:T(8,128)(2,1)S(1)}, bf16[512,1408]{1,0:T(8,128)(2,1)S(1)}, u32[]{:S(2)}, u32[]{:S(2)}) collective-permute-start(bf16[512,1408]{1,0:T(8,128)(2,1)S(1)} %bitcast.157), channel_id=1, source_target_pairs={{0,1},{1,0},{2,3},{3,2},{4,5},{5,4},{6,7},{7,6},{8,9},{9,8},{10,11... | collective-permute-start | bytes 4325384 | tf_op jit(solution)/shard_map/ppermute | solution.py:61
  59.7 8.1 %collective-permute-start.17 = (bf16[512,1408]{1,0:T(8,128)(2,1)S(1)}, bf16[512,1408]{1,0:T(8,128)(2,1)S(1)}, u32[]{:S(2)}, u32[]{:S(2)}) collective-permute-start(bf16[512,1408]{1,0:T(8,128)(2,1)S(1)} %constant_dynamic-update-slice_fusion), channel_id=1, source_target_pairs={{0,1},{1,0},{2,3},{3,2},{4,5},{5,4},{6,7},{7,6},{8,9},{9,8},{10,11... | collective-permute-start | bytes 4325384 | tf_op jit(solution)/shard_map/ppermute | solution.py:61
  73.8 4.7 %collective-permute-start.20 = (bf16[512,1152]{1,0:T(8,128)(2,1)S(1)}, bf16[512,1152]{1,0:T(8,128)(2,1)S(1)}, u32[]{:S(2)}, u32[]{:S(2)}) collective-permute-start(bf16[512,1152]{1,0:T(8,128)(2,1)S(1)} %bitcast.164), channel_id=1, source_target_pairs={{0,1},{1,0},{2,3},{3,2},{4,5},{5,4},{6,7},{7,6},{8,9},{9,8},{10,11... | collective-permute-start | bytes 3538952 | tf_op jit(solution)/shard_map/ppermute | solution.py:61
  74.0 5.7 %collective-permute-start.19 = (bf16[512,1280]{1,0:T(8,128)(2,1)S(1)}, bf16[512,1280]{1,0:T(8,128)(2,1)S(1)}, u32[]{:S(2)}, u32[]{:S(2)}) collective-permute-start(bf16[512,1280]{1,0:T(8,128)(2,1)S(1)} %bitcast.151), channel_id=1, source_target_pairs={{0,1},{1,0},{2,3},{3,2},{4,5},{5,4},{6,7},{7,6},{8,9},{9,8},{10,11... | collective-permute-start | bytes 3932168 | tf_op jit(solution)/shard_map/ppermute | solution.py:61
  87.0 8.7 %collective-permute-start.31 = (bf16[512,1152]{1,0:T(8,128)(2,1)S(1)}, bf16[512,1152]{1,0:T(8,128)(2,1)S(1)}, u32[]{:S(2)}, u32[]{:S(2)}) collective-permute-start(bf16[512,1152]{1,0:T(8,128)(2,1)S(1)} %convolution_convert_fusion.1), channel_id=1, source_target_pairs={{0,1},{1,0},{2,3},{3,2},{4,5},{5,4},{6,7},{7,6},{8,9},{9,8},{10,11... | collective-permute-start | bytes 3538952 | tf_op jit(solution)/shard_map/ppermute | solution.py:61
  87.1 5.8 %collective-permute-start.36 = (bf16[512,1152]{1,0:T(8,128)(2,1)S(1)}, bf16[512,1152]{1,0:T(8,128)(2,1)S(1)}, u32[]{:S(2)}, u32[]{:S(2)}) collective-permute-start(bf16[512,1152]{1,0:T(8,128)(2,1)S(1)} %convolution_convert_fusion), channel_id=1, source_target_pairs={{0,1},{1,0},{2,3},{3,2},{4,5},{5,4},{6,7},{7,6},{8,9},{9,8},{10,11... | collective-permute-start | bytes 3538952 | tf_op jit(solution)/shard_map/ppermute | solution.py:61
  89.0 8.6 %collective-permute-start.21 = (bf16[512,1408]{1,0:T(8,128)(2,1)S(1)}, bf16[512,1408]{1,0:T(8,128)(2,1)S(1)}, u32[]{:S(2)}, u32[]{:S(2)}) collective-permute-start(bf16[512,1408]{1,0:T(8,128)(2,1)S(1)} %convolution_convert_fusion.3), channel_id=1, source_target_pairs={{0,1},{1,0},{2,3},{3,2},{4,5},{5,4},{6,7},{7,6},{8,9},{9,8},{10,11... | collective-permute-start | bytes 4325384 | tf_op jit(solution)/shard_map/ppermute | solution.py:61
  90.6 10.2 %collective-permute-start.26 = (bf16[512,1408]{1,0:T(8,128)(2,1)S(1)}, bf16[512,1408]{1,0:T(8,128)(2,1)S(1)}, u32[]{:S(2)}, u32[]{:S(2)}) collective-permute-start(bf16[512,1408]{1,0:T(8,128)(2,1)S(1)} %convolution_convert_fusion.2), channel_id=1, source_target_pairs={{0,1},{1,0},{2,3},{3,2},{4,5},{5,4},{6,7},{7,6},{8,9},{9,8},{10,11... | collective-permute-start | bytes 4325384 | tf_op jit(solution)/shard_map/ppermute | solution.py:61
  94.1 16.3 %collective-permute-start.37 = (bf16[256,1152]{1,0:T(8,128)(2,1)S(1)}, bf16[256,1152]{1,0:T(8,128)(2,1)S(1)}, u32[]{:S(2)}, u32[]{:S(2)}) collective-permute-start(bf16[256,1152]{1,0:T(8,128)(2,1)S(1)} %split.57), channel_id=1, source_target_pairs={{0,16},{16,0},{1,17},{17,1},{2,18},{18,2},{3,19},{19,3},{4,20},{20... | collective-permute-start | bytes 1769480 | tf_op jit(solution)/shard_map/ppermute | solution.py:61
  97.2 16.3 %collective-permute-start.32 = (bf16[256,1152]{1,0:T(8,128)(2,1)S(1)}, bf16[256,1152]{1,0:T(8,128)(2,1)S(1)}, u32[]{:S(2)}, u32[]{:S(2)}) collective-permute-start(bf16[256,1152]{1,0:T(8,128)(2,1)S(1)} %split.53), channel_id=1, source_target_pairs={{0,2},{2,0},{1,3},{3,1},{4,6},{6,4},{5,7},{7,5},{8,10},{10,8},{9,1... | collective-permute-start | bytes 1769480 | tf_op jit(solution)/shard_map/ppermute | solution.py:61
  99.2 30.9 %collective-permute-start.22 = (bf16[256,1408]{1,0:T(8,128)(2,1)S(1)}, bf16[256,1408]{1,0:T(8,128)(2,1)S(1)}, u32[]{:S(2)}, u32[]{:S(2)}) collective-permute-start(bf16[256,1408]{1,0:T(8,128)(2,1)S(1)} %split.49), channel_id=1, source_target_pairs={{0,2},{2,0},{1,3},{3,1},{4,6},{6,4},{5,7},{7,5},{8,10},{10,8},{9,1... | collective-permute-start | bytes 2162696 | tf_op jit(solution)/shard_map/ppermute | solution.py:61
  102.3 29.6 %collective-permute-start.27 = (bf16[256,1408]{1,0:T(8,128)(2,1)S(1)}, bf16[256,1408]{1,0:T(8,128)(2,1)S(1)}, u32[]{:S(2)}, u32[]{:S(2)}) collective-permute-start(bf16[256,1408]{1,0:T(8,128)(2,1)S(1)} %split.51), channel_id=1, source_target_pairs={{0,16},{16,0},{1,17},{17,1},{2,18},{18,2},{3,19},{19,3},{4,20},{20... | collective-permute-start | bytes 2162696 | tf_op jit(solution)/shard_map/ppermute | solution.py:61
  110.5 12.0 %collective-permute-start.38 = (bf16[128,1152]{1,0:T(8,128)(2,1)S(1)}, bf16[128,1152]{1,0:T(8,128)(2,1)S(1)}, u32[]{:S(2)}, u32[]{:S(2)}) collective-permute-start(bf16[128,1152]{1,0:T(8,128)(2,1)S(1)} %slice.201), channel_id=1, source_target_pairs={{0,4},{4,0},{8,12},{12,8},{1,5},{5,1},{9,13},{13,9},{2,6},{6,2},{1... | collective-permute-start | bytes 884744 | tf_op jit(solution)/shard_map/ppermute | solution.py:61
  113.7 12.9 %collective-permute-start.33 = (bf16[128,1152]{1,0:T(8,128)(2,1)S(1)}, bf16[128,1152]{1,0:T(8,128)(2,1)S(1)}, u32[]{:S(2)}, u32[]{:S(2)}) collective-permute-start(bf16[128,1152]{1,0:T(8,128)(2,1)S(1)} %slice.197), channel_id=1, source_target_pairs={{0,4},{4,0},{8,12},{12,8},{1,5},{5,1},{9,13},{13,9},{2,6},{6,2},{1... | collective-permute-start | bytes 884744 | tf_op jit(solution)/shard_map/ppermute | solution.py:61
  122.7 12.8 %collective-permute-start.39 = (bf16[64,1152]{1,0:T(8,128)(2,1)S(1)}, bf16[64,1152]{1,0:T(8,128)(2,1)S(1)}, u32[]{:S(2)}, u32[]{:S(2)}) collective-permute-start(bf16[64,1152]{1,0:T(8,128)(2,1)S(1)} %split.59), channel_id=1, source_target_pairs={{0,8},{4,12},{8,0},{12,4},{1,9},{5,13},{9,1},{13,5},{2,10},{6,14},... | collective-permute-start | bytes 442376 | tf_op jit(solution)/shard_map/ppermute | solution.py:61
  126.6 10.7 %collective-permute-start.34 = (bf16[64,1152]{1,0:T(8,128)(2,1)S(1)}, bf16[64,1152]{1,0:T(8,128)(2,1)S(1)}, u32[]{:S(2)}, u32[]{:S(2)}) collective-permute-start(bf16[64,1152]{1,0:T(8,128)(2,1)S(1)} %split.55), channel_id=1, source_target_pairs={{0,8},{4,12},{8,0},{12,4},{1,9},{5,13},{9,1},{13,5},{2,10},{6,14},... | collective-permute-start | bytes 442376 | tf_op jit(solution)/shard_map/ppermute | solution.py:61
  130.3 9.2 %collective-permute-start.23 = (bf16[128,1408]{1,0:T(8,128)(2,1)S(1)}, bf16[128,1408]{1,0:T(8,128)(2,1)S(1)}, u32[]{:S(2)}, u32[]{:S(2)}) collective-permute-start(bf16[128,1408]{1,0:T(8,128)(2,1)S(1)} %slice.185), channel_id=1, source_target_pairs={{0,16},{16,0},{1,17},{17,1},{2,18},{18,2},{3,19},{19,3},{4,20},{20... | collective-permute-start | bytes 1081352 | tf_op jit(solution)/shard_map/ppermute | solution.py:61
  132.1 8.3 %collective-permute-start.28 = (bf16[128,1408]{1,0:T(8,128)(2,1)S(1)}, bf16[128,1408]{1,0:T(8,128)(2,1)S(1)}, u32[]{:S(2)}, u32[]{:S(2)}) collective-permute-start(bf16[128,1408]{1,0:T(8,128)(2,1)S(1)} %slice.191), channel_id=1, source_target_pairs={{0,2},{2,0},{1,3},{3,1},{4,6},{6,4},{5,7},{7,5},{8,10},{10,8},{9,1... | collective-permute-start | bytes 1081352 | tf_op jit(solution)/shard_map/ppermute | solution.py:61
  137.5 14.6 %collective-permute-start.40 = (bf16[32,1152]{1,0:T(8,128)(2,1)S(1)}, bf16[32,1152]{1,0:T(8,128)(2,1)S(1)}, u32[]{:S(2)}, u32[]{:S(2)}) collective-permute-start(bf16[32,1152]{1,0:T(8,128)(2,1)S(1)} %slice.203), channel_id=1, source_target_pairs={{0,2},{2,0},{1,3},{3,1},{4,6},{6,4},{5,7},{7,5},{8,10},{10,8},{9,1... | collective-permute-start | bytes 221192 | tf_op jit(solution)/shard_map/ppermute | solution.py:61
  138.0 14.0 %collective-permute-start.35 = (bf16[32,1152]{1,0:T(8,128)(2,1)S(1)}, bf16[32,1152]{1,0:T(8,128)(2,1)S(1)}, u32[]{:S(2)}, u32[]{:S(2)}) collective-permute-start(bf16[32,1152]{1,0:T(8,128)(2,1)S(1)} %slice.199), channel_id=1, source_target_pairs={{0,16},{16,0},{1,17},{17,1},{2,18},{18,2},{3,19},{19,3},{4,20},{20... | collective-permute-start | bytes 221192 | tf_op jit(solution)/shard_map/ppermute | solution.py:61
  139.6 12.4 %copy-start.2 = (bf16[1,32,5120]{2,1,0:T(8,128)(2,1)S(1)}, bf16[1,32,5120]{2,1,0:T(8,128)(2,1)}, u32[]{:S(2)}) copy-start(bf16[1,32,5120]{2,1,0:T(8,128)(2,1)} %param.6) | copy-start | bytes 983044
  139.7 7.4 %collective-permute-start.24 = (bf16[64,1408]{1,0:T(8,128)(2,1)S(1)}, bf16[64,1408]{1,0:T(8,128)(2,1)S(1)}, u32[]{:S(2)}, u32[]{:S(2)}) collective-permute-start(bf16[64,1408]{1,0:T(8,128)(2,1)S(1)} %slice.187), channel_id=1, source_target_pairs={{0,4},{4,0},{8,12},{12,8},{1,5},{5,1},{9,13},{13,9},{2,6},{6,2},{1... | collective-permute-start | bytes 540680 | tf_op jit(solution)/shard_map/ppermute | solution.py:61
  140.5 16.1 %copy-start.1 = (s32[1,64,6]{1,0,2:T(1,128)S(1)}, s32[1,64,6]{1,0,2:T(1,128)}, u32[]{:S(2)}) copy-start(s32[1,64,6]{1,0,2:T(1,128)} %param.7) | copy-start | bytes 4612
  140.6 8.7 %collective-permute-start.29 = (bf16[64,1408]{1,0:T(8,128)(2,1)S(1)}, bf16[64,1408]{1,0:T(8,128)(2,1)S(1)}, u32[]{:S(2)}, u32[]{:S(2)}) collective-permute-start(bf16[64,1408]{1,0:T(8,128)(2,1)S(1)} %slice.193), channel_id=1, source_target_pairs={{0,4},{4,0},{8,12},{12,8},{1,5},{5,1},{9,13},{13,9},{2,6},{6,2},{1... | collective-permute-start | bytes 540680 | tf_op jit(solution)/shard_map/ppermute | solution.py:61
  147.2 6.1 %collective-permute-start.25 = (bf16[32,1408]{1,0:T(8,128)(2,1)S(1)}, bf16[32,1408]{1,0:T(8,128)(2,1)S(1)}, u32[]{:S(2)}, u32[]{:S(2)}) collective-permute-start(bf16[32,1408]{1,0:T(8,128)(2,1)S(1)} %slice.189), channel_id=1, source_target_pairs={{0,8},{4,12},{8,0},{12,4},{1,9},{5,13},{9,1},{13,5},{2,10},{6,14},... | collective-permute-start | bytes 270344 | tf_op jit(solution)/shard_map/ppermute | solution.py:61
  149.4 6.5 %collective-permute-start.30 = (bf16[32,1408]{1,0:T(8,128)(2,1)S(1)}, bf16[32,1408]{1,0:T(8,128)(2,1)S(1)}, u32[]{:S(2)}, u32[]{:S(2)}) collective-permute-start(bf16[32,1408]{1,0:T(8,128)(2,1)S(1)} %slice.195), channel_id=1, source_target_pairs={{0,8},{4,12},{8,0},{12,4},{1,9},{5,13},{9,1},{13,5},{2,10},{6,14},... | collective-permute-start | bytes 270344 | tf_op jit(solution)/shard_map/ppermute | solution.py:61
  (3 other events, 7.7 us)

commit v3 on v2

--- a/solution.py
+++ b/solution.py
@@ -3,7 +3,8 @@
 from jax import lax
 from jax.sharding import Mesh, PartitionSpec as P
 
-CHUNK_EDGES = (0, 11, 22, 31, 40)
+GATHER_EDGES = (0, 12, 24, 32, 40)
+SCATTER_EDGES = (0, 11, 22, 31, 40)
 GAIN_CHUNK = 2
 LANES = 128
 
@@ -118,8 +119,12 @@
         lax.dynamic_slice_in_dim(route_gain[0], x * half, half, 0),
         n_lines,
     )
-    edges = [width * part // CHUNK_EDGES[-1] for part in CHUNK_EDGES]
-    spans = [slice(start, stop) for start, stop in zip(edges, edges[1:])]
+
+    def cut(edges):
+        edges = [width * part // edges[-1] for part in edges]
+        return [slice(start, stop) for start, stop in zip(edges, edges[1:])]
+
+    spans, back_spans = cut(GATHER_EDGES), cut(SCATTER_EDGES)
     n_chunks = len(spans)
     dims = (((1,), (1,)), ((), ()))
 
@@ -131,8 +136,9 @@
     flipped = [grown(after(chunks[c], *in_far), STAGES[c][0]) for c in two]
     at = GAIN_CHUNK - two[0]
     flipped[at] = jnp.concatenate([flipped[at], grown(after(columns, *in_far), STAGES[GAIN_CHUNK][0])], axis=1)
-    far = [grown(after(value, *in_z), FAR) for value in flipped]
-    near = [grown(after(value, *before_last), NEAR) for value in far]
+    flipped = [after(value, *in_z) for value in flipped]
+    far = [jnp.concatenate([value, after(swap(value, *FAR), *before_last)], axis=0) for value in flipped]
+    near = [grown(value, NEAR) for value in far]
     received = [swap(value, *STAGES[c][3]) for c, value in zip(one, before_last)]
     joined = lax.optimization_barrier(received + near)
     before_last += joined[2:]
@@ -159,7 +165,7 @@
         return lax.optimization_barrier(value)
 
     def down(value, c):
-        return jnp.dot(value, down_weight[0, :, spans[c]], preferred_element_type=jnp.float32)
+        return jnp.dot(value, down_weight[0, :, back_spans[c]], preferred_element_type=jnp.float32)
 
     away = act(1)
     to_core = {c: down(ordered(away, STAGES[0], STAGES[c]), c).astype(jnp.bfloat16) for c in two}
@@ -181,7 +187,7 @@
     for c in one:
         outs[c] = (halved(halved(first[c], STAGES[c][2]), NEAR), FAR)
     for c, (value, flip) in outs.items():
-        total = block[:, spans[c]].astype(jnp.float32) + value[:half].astype(jnp.float32)
+        total = block[:, back_spans[c]].astype(jnp.float32) + value[:half].astype(jnp.float32)
         outs[c] = (total + swap(value[half:], *flip).astype(jnp.float32)).astype(jnp.bfloat16)
     return jnp.concatenate([outs[c] for c in range(n_chunks)], axis=1)[None]
 

time: 157 us -> 153 us (0.975)
  starting transfers between devices: 49.9 us -> 42.7 us
  waiting for transfers between devices: 64 us -> 68.3 us
  matrix products: 32.6 us -> 30.9 us
    ppermute x41, starting transfers between devices: 49.9 us -> 42.7 us  [swap(): return lax.ppermute(value, axis, [(i, i ^ flip) for i in range(size)])]
    ppermute x41, waiting for transfers between devices: 64 us -> 68.3 us  [swap(): return lax.ppermute(value, axis, [(i, i ^ flip) for i in range(size)])]
    dot_general x16, matrix products: 21.9 us -> 20.2 us  [ring_body(): lax.dot_general(rows, weight[0, :, spans[c]], dims, preferred_element_typ...]
  transfers between devices with their start and end apart: 41 -> 41, of which waited for: 20 -> 24; matrix products, arithmetic and copies ran while one was open for 20% -> 20% of each run, Pallas kernels for 0% -> 0%
where the time goes in v3:
time: 153 us
  waiting for transfers between devices  68.3 us (45%)
  starting transfers between devices  42.7 us (28%)
  matrix products  30.9 us (20%)
  local copies, waits for them, and re-layouts  7.28 us (5%)
  other arithmetic  2.81 us (2%)
    ppermute x41, waiting for transfers between devices, swap(): return lax.ppermute(value, axis, [(i, i ^ flip) for i in range(size)])  68.3 us
    ppermute x41, starting transfers between devices, swap(): return lax.ppermute(value, axis, [(i, i ^ flip) for i in range(size)])  42.7 us
    dot_general x16, matrix products, ring_body(): lax.dot_general(rows, weight[0, :, spans[c]], dims, preferred_element_typ...  20.2 us
    dot_general x8, matrix products, down(): jnp.dot(value, down_weight[0, :, back_spans[c]], preferred_element_type=j...  10.7 us
    unnamed x29, local copies, waits for them, and re-layouts  4.32 us
  transfers between devices with their start and end apart: 41, of which 24 were waited for; matrix products, arithmetic and copies ran while one was open for 20% of the time, Pallas kernels for 0%

profile of v3, /device:TPU:0, one launch (start us, length us, event | category | flops | bytes accessed | tf_op | source)
XLA Modules:
  0.0 152.8 jit_solution(4613992635744371227)
XLA Ops:
  0.0 1.6 %constant_dynamic-update-slice_fusion.4 = (bf16[512,1536]{1,0:T(8,128)(2,1)}, bf16[512,1536]{1,0:T(8,128)(2,1)S(1)}, bf16[32,1536]{1,0:T(8,128)(2,1)S(1)}, bf16[32,1536]{1,0:T(8,128)(2,1)S(1)}) fusion(bf16[32,5120]{1,0:T(8,128)(2,1)} %bitcast.160), kind=kLoop, calls=%fused_computation.133 | loop fusion | bytes 589824
  1.6 4.0 %collective-permute-start = (bf16[32,1536]{1,0:T(8,128)(2,1)S(1)}, bf16[32,1536]{1,0:T(8,128)(2,1)S(1)}, u32[]{:S(2)}, u32[]{:S(2)}) collective-permute-start(bf16[32,1536]{1,0:T(8,128)(2,1)S(1)} %get-tuple-element.52), channel_id=1, source_target_pairs={{0,8},{4,12},{8,0},{12,4},{1,9},{5,13},{9,1},{13,5},{2,10},{6,14},... | collective-permute-start | bytes 294920 | tf_op jit(solution)/shard_map/ppermute | solution.py:62
  7.5 6.0 %collective-permute-done = bf16[32,1536]{1,0:T(8,128)(2,1)S(1)} collective-permute-done((bf16[32,1536]{1,0:T(8,128)(2,1)S(1)}, bf16[32,1536]{1,0:T(8,128)(2,1)S(1)}, u32[]{:S(2)}, u32[]{:S(2)}) %collective-permute-start) | collective-permute-done | bytes 98336 | tf_op jit(solution)/shard_map/ppermute | solution.py:62
  15.7 1.7 %collective-permute-start.12 = (bf16[32,1024]{1,0:T(8,128)(2,1)S(1)}, bf16[32,1024]{1,0:T(8,128)(2,1)S(1)}, u32[]{:S(2)}, u32[]{:S(2)}) collective-permute-start(bf16[32,1024]{1,0:T(8,128)(2,1)S(1)} %get-tuple-element.28), channel_id=1, source_target_pairs={{0,2},{2,0},{1,3},{3,1},{4,6},{6,4},{5,7},{7,5},{8,10},{10,8},{9,1... | collective-permute-start | bytes 196616 | tf_op jit(solution)/shard_map/ppermute | solution.py:62
  17.4 1.5 collective-permute-start.9
  20.1 1.3 collective-permute-done.9
  21.6 1.5 %collective-permute-done.8 = bf16[32,1024]{1,0:T(8,128)(2,1)S(1)} collective-permute-done((bf16[32,1024]{1,0:T(8,128)(2,1)S(1)}, bf16[32,1024]{1,0:T(8,128)(2,1)S(1)}, u32[]{:S(2)}, u32[]{:S(2)}) %collective-permute-start.8) | collective-permute-done | bytes 65568 | tf_op jit(solution)/shard_map/ppermute | solution.py:62
  23.2 1.6 %collective-permute-start.6 = (bf16[128,1536]{1,0:T(8,128)(2,1)S(1)}, bf16[128,1536]{1,0:T(8,128)(2,1)S(1)}, u32[]{:S(2)}, u32[]{:S(2)}) collective-permute-start(bf16[128,1536]{1,0:T(8,128)(2,1)S(1)} %pad_maximum_fusion.7), channel_id=1, source_target_pairs={{0,2},{2,0},{1,3},{3,1},{4,6},{6,4},{5,7},{7,5},{8,10},{10,8},{9,1... | collective-permute-start | bytes 1179656 | tf_op jit(solution)/shard_map/ppermute | solution.py:62
  24.9 1.6 %collective-permute-start.2 = (bf16[128,1536]{1,0:T(8,128)(2,1)S(1)}, bf16[128,1536]{1,0:T(8,128)(2,1)S(1)}, u32[]{:S(2)}, u32[]{:S(2)}) collective-permute-start(bf16[128,1536]{1,0:T(8,128)(2,1)S(1)} %pad_maximum_fusion.6), channel_id=1, source_target_pairs={{0,16},{16,0},{1,17},{17,1},{2,18},{18,2},{3,19},{19,3},{4,20},{20... | collective-permute-start | bytes 1179656 | tf_op jit(solution)/shard_map/ppermute | solution.py:62
  26.5 2.9 %collective-permute-start.13 = (bf16[64,1024]{1,0:T(8,128)(2,1)S(1)}, bf16[64,1024]{1,0:T(8,128)(2,1)S(1)}, u32[]{:S(2)}, u32[]{:S(2)}) collective-permute-start(bf16[64,1024]{1,0:T(8,128)(2,1)S(1)} %pad_maximum_fusion.13), channel_id=1, source_target_pairs={{0,8},{4,12},{8,0},{12,4},{1,9},{5,13},{9,1},{13,5},{2,10},{6,14},... | collective-permute-start | bytes 393224 | tf_op jit(solution)/shard_map/ppermute | solution.py:62
  29.4 3.0 %collective-permute-done.6 = bf16[128,1536]{1,0:T(8,128)(2,1)S(1)} collective-permute-done((bf16[128,1536]{1,0:T(8,128)(2,1)S(1)}, bf16[128,1536]{1,0:T(8,128)(2,1)S(1)}, u32[]{:S(2)}, u32[]{:S(2)}) %collective-permute-start.6) | collective-permute-done | bytes 393248 | tf_op jit(solution)/shard_map/ppermute | solution.py:62
  34.3 1.6 %collective-permute-start.3 = (bf16[256,1536]{1,0:T(8,128)(2,1)S(1)}, bf16[256,1536]{1,0:T(8,128)(2,1)S(1)}, u32[]{:S(2)}, u32[]{:S(2)}) collective-permute-start(bf16[256,1536]{1,0:T(8,128)(2,1)S(1)} %pad_maximum_fusion.2), channel_id=1, source_target_pairs={{0,2},{2,0},{1,3},{3,1},{4,6},{6,4},{5,7},{7,5},{8,10},{10,8},{9,1... | collective-permute-start | bytes 2359304 | tf_op jit(solution)/shard_map/ppermute | solution.py:62
  35.8 3.0 %collective-permute-done.13 = bf16[64,1024]{1,0:T(8,128)(2,1)S(1)} collective-permute-done((bf16[64,1024]{1,0:T(8,128)(2,1)S(1)}, bf16[64,1024]{1,0:T(8,128)(2,1)S(1)}, u32[]{:S(2)}, u32[]{:S(2)}) %collective-permute-start.13) | collective-permute-done | bytes 131104 | tf_op jit(solution)/shard_map/ppermute | solution.py:62
  38.9 2.1 %collective-permute-done.10 = bf16[64,1152]{1,0:T(8,128)(2,1)S(1)} collective-permute-done((bf16[64,1152]{1,0:T(8,128)(2,1)S(1)}, bf16[64,1152]{1,0:T(8,128)(2,1)S(1)}, u32[]{:S(2)}, u32[]{:S(2)}) %collective-permute-start.10) | collective-permute-done | bytes 147488 | tf_op jit(solution)/shard_map/ppermute | solution.py:62
  41.8 6.3 %collective-permute-done.14 = bf16[128,1024]{1,0:T(8,128)(2,1)S(1)} collective-permute-done((bf16[128,1024]{1,0:T(8,128)(2,1)S(1)}, bf16[128,1024]{1,0:T(8,128)(2,1)S(1)}, u32[]{:S(2)}, u32[]{:S(2)}) %collective-permute-start.14) | collective-permute-done | bytes 262176 | tf_op jit(solution)/shard_map/ppermute | solution.py:62
  48.2 4.7 %collective-permute-done.11 = bf16[128,1152]{1,0:T(8,128)(2,1)S(1)} collective-permute-done((bf16[128,1152]{1,0:T(8,128)(2,1)S(1)}, bf16[128,1152]{1,0:T(8,128)(2,1)S(1)}, u32[]{:S(2)}, u32[]{:S(2)}) %collective-permute-start.11) | collective-permute-done | bytes 294944 | tf_op jit(solution)/shard_map/ppermute | solution.py:62
  53.9 1.4 fusion.2
  56.4 1.4 fusion.10
  58.9 1.4 fusion.78
  60.3 1.4 fusion.72
  61.8 1.4 fusion.8
  63.2 1.4 fusion.75
  64.6 1.4 fusion
  66.0 1.4 fusion.81
  67.4 3.9 %collective-permute-done.16 = bf16[256,1024]{1,0:T(8,128)(2,1)S(1)} collective-permute-done((bf16[256,1024]{1,0:T(8,128)(2,1)S(1)}, bf16[256,1024]{1,0:T(8,128)(2,1)S(1)}, u32[]{:S(2)}, u32[]{:S(2)}) %collective-permute-start.16) | collective-permute-done | bytes 524320 | tf_op jit(solution)/shard_map/ppermute | solution.py:62
  80.4 1.4 multiply_convert_fusion.1
  85.9 1.4 convolution_convert_fusion.2
  87.5 1.4 convolution_convert_fusion.3
  89.4 1.2 multiply_convert_fusion
  92.7 1.4 add_convert_fusion.3
  94.8 1.4 add_convert_fusion
  96.2 1.6 %collective-permute-start.27 = (bf16[256,1408]{1,0:T(8,128)(2,1)S(1)}, bf16[256,1408]{1,0:T(8,128)(2,1)S(1)}, u32[]{:S(2)}, u32[]{:S(2)}) collective-permute-start(bf16[256,1408]{1,0:T(8,128)(2,1)S(1)} %split.51), channel_id=1, source_target_pairs={{0,16},{16,0},{1,17},{17,1},{2,18},{18,2},{3,19},{19,3},{4,20},{20... | collective-permute-start | bytes 2162696 | tf_op jit(solution)/shard_map/ppermute | solution.py:62
  97.8 1.4 add_convert_fusion.1
  99.3 1.6 %collective-permute-start.22 = (bf16[256,1408]{1,0:T(8,128)(2,1)S(1)}, bf16[256,1408]{1,0:T(8,128)(2,1)S(1)}, u32[]{:S(2)}, u32[]{:S(2)}) collective-permute-start(bf16[256,1408]{1,0:T(8,128)(2,1)S(1)} %split.49), channel_id=1, source_target_pairs={{0,2},{2,0},{1,3},{3,1},{4,6},{6,4},{5,7},{7,5},{8,10},{10,8},{9,1... | collective-permute-start | bytes 2162696 | tf_op jit(solution)/shard_map/ppermute | solution.py:62
  100.8 7.5 %collective-permute-done.37 = bf16[256,1152]{1,0:T(8,128)(2,1)S(1)} collective-permute-done((bf16[256,1152]{1,0:T(8,128)(2,1)S(1)}, bf16[256,1152]{1,0:T(8,128)(2,1)S(1)}, u32[]{:S(2)}, u32[]{:S(2)}) %collective-permute-start.37) | collective-permute-done | bytes 589856 | tf_op jit(solution)/shard_map/ppermute | solution.py:62
  108.8 1.7 %collective-permute-done.32 = bf16[256,1152]{1,0:T(8,128)(2,1)S(1)} collective-permute-done((bf16[256,1152]{1,0:T(8,128)(2,1)S(1)}, bf16[256,1152]{1,0:T(8,128)(2,1)S(1)}, u32[]{:S(2)}, u32[]{:S(2)}) %collective-permute-start.32) | collective-permute-done | bytes 589856 | tf_op jit(solution)/shard_map/ppermute | solution.py:62
  111.6 8.5 %collective-permute-done.38 = bf16[128,1152]{1,0:T(8,128)(2,1)S(1)} collective-permute-done((bf16[128,1152]{1,0:T(8,128)(2,1)S(1)}, bf16[128,1152]{1,0:T(8,128)(2,1)S(1)}, u32[]{:S(2)}, u32[]{:S(2)}) %collective-permute-start.38) | collective-permute-done | bytes 294944 | tf_op jit(solution)/shard_map/ppermute | solution.py:62
  120.2 1.8 %collective-permute-start.39 = (bf16[64,1152]{1,0:T(8,128)(2,1)S(1)}, bf16[64,1152]{1,0:T(8,128)(2,1)S(1)}, u32[]{:S(2)}, u32[]{:S(2)}) collective-permute-start(bf16[64,1152]{1,0:T(8,128)(2,1)S(1)} %split.59), channel_id=1, source_target_pairs={{0,8},{4,12},{8,0},{12,4},{1,9},{5,13},{9,1},{13,5},{2,10},{6,14},... | collective-permute-start | bytes 442376 | tf_op jit(solution)/shard_map/ppermute | solution.py:62
  122.0 1.9 %collective-permute-done.33 = bf16[128,1152]{1,0:T(8,128)(2,1)S(1)} collective-permute-done((bf16[128,1152]{1,0:T(8,128)(2,1)S(1)}, bf16[128,1152]{1,0:T(8,128)(2,1)S(1)}, u32[]{:S(2)}, u32[]{:S(2)}) %collective-permute-start.33) | collective-permute-done | bytes 294944 | tf_op jit(solution)/shard_map/ppermute | solution.py:62
  124.0 3.2 %collective-permute-start.34 = (bf16[64,1152]{1,0:T(8,128)(2,1)S(1)}, bf16[64,1152]{1,0:T(8,128)(2,1)S(1)}, u32[]{:S(2)}, u32[]{:S(2)}) collective-permute-start(bf16[64,1152]{1,0:T(8,128)(2,1)S(1)} %split.55), channel_id=1, source_target_pairs={{0,8},{4,12},{8,0},{12,4},{1,9},{5,13},{9,1},{13,5},{2,10},{6,14},... | collective-permute-start | bytes 442376 | tf_op jit(solution)/shard_map/ppermute | solution.py:62
  127.4 1.7 %collective-permute-start.28 = (bf16[128,1408]{1,0:T(8,128)(2,1)S(1)}, bf16[128,1408]{1,0:T(8,128)(2,1)S(1)}, u32[]{:S(2)}, u32[]{:S(2)}) collective-permute-start(bf16[128,1408]{1,0:T(8,128)(2,1)S(1)} %slice.205), channel_id=1, source_target_pairs={{0,2},{2,0},{1,3},{3,1},{4,6},{6,4},{5,7},{7,5},{8,10},{10,8},{9,1... | collective-permute-start | bytes 1081352 | tf_op jit(solution)/shard_map/ppermute | solution.py:62
  130.0 2.8 %collective-permute-done.39 = bf16[64,1152]{1,0:T(8,128)(2,1)S(1)} collective-permute-done((bf16[64,1152]{1,0:T(8,128)(2,1)S(1)}, bf16[64,1152]{1,0:T(8,128)(2,1)S(1)}, u32[]{:S(2)}, u32[]{:S(2)}) %collective-permute-start.39) | collective-permute-done | bytes 147488 | tf_op jit(solution)/shard_map/ppermute | solution.py:62
  135.7 1.5 collective-permute-start.29
  138.7 4.0 %collective-permute-done.29 = bf16[64,1408]{1,0:T(8,128)(2,1)S(1)} collective-permute-done((bf16[64,1408]{1,0:T(8,128)(2,1)S(1)}, bf16[64,1408]{1,0:T(8,128)(2,1)S(1)}, u32[]{:S(2)}, u32[]{:S(2)}) %collective-permute-start.29) | collective-permute-done | bytes 180256 | tf_op jit(solution)/shard_map/ppermute | solution.py:62
  142.7 1.9 %collective-permute-start.30 = (bf16[32,1408]{1,0:T(8,128)(2,1)S(1)}, bf16[32,1408]{1,0:T(8,128)(2,1)S(1)}, u32[]{:S(2)}, u32[]{:S(2)}) collective-permute-start(bf16[32,1408]{1,0:T(8,128)(2,1)S(1)} %slice.209), channel_id=1, source_target_pairs={{0,8},{4,12},{8,0},{12,4},{1,9},{5,13},{9,1},{13,5},{2,10},{6,14},... | collective-permute-start | bytes 270344 | tf_op jit(solution)/shard_map/ppermute | solution.py:62
  145.5 2.0 %collective-permute-start.25 = (bf16[32,1408]{1,0:T(8,128)(2,1)S(1)}, bf16[32,1408]{1,0:T(8,128)(2,1)S(1)}, u32[]{:S(2)}, u32[]{:S(2)}) collective-permute-start(bf16[32,1408]{1,0:T(8,128)(2,1)S(1)} %slice.202), channel_id=1, source_target_pairs={{0,8},{4,12},{8,0},{12,4},{1,9},{5,13},{9,1},{13,5},{2,10},{6,14},... | collective-permute-start | bytes 270344 | tf_op jit(solution)/shard_map/ppermute | solution.py:62
  147.6 1.7 %collective-permute-done.30 = bf16[32,1408]{1,0:T(8,128)(2,1)S(1)} collective-permute-done((bf16[32,1408]{1,0:T(8,128)(2,1)S(1)}, bf16[32,1408]{1,0:T(8,128)(2,1)S(1)}, u32[]{:S(2)}, u32[]{:S(2)}) %collective-permute-start.30) | collective-permute-done | bytes 90144 | tf_op jit(solution)/shard_map/ppermute | solution.py:62
  149.3 2.7 %collective-permute-done.25 = bf16[32,1408]{1,0:T(8,128)(2,1)S(1)} collective-permute-done((bf16[32,1408]{1,0:T(8,128)(2,1)S(1)}, bf16[32,1408]{1,0:T(8,128)(2,1)S(1)}, u32[]{:S(2)}, u32[]{:S(2)}) %collective-permute-start.25) | collective-permute-done | bytes 90144 | tf_op jit(solution)/shard_map/ppermute | solution.py:62
  (156 shorter events, 36.6 us)
Async XLA Ops:
  0.0 6.6 %copy-start = (f32[1,64,6]{1,0,2:T(1,128)S(1)}, f32[1,64,6]{1,0,2:T(1,128)}, u32[]{:S(2)}) copy-start(f32[1,64,6]{1,0,2:T(1,128)} %param.8) | copy-start | bytes 4612
  1.6 11.9 %collective-permute-start = (bf16[32,1536]{1,0:T(8,128)(2,1)S(1)}, bf16[32,1536]{1,0:T(8,128)(2,1)S(1)}, u32[]{:S(2)}, u32[]{:S(2)}) collective-permute-start(bf16[32,1536]{1,0:T(8,128)(2,1)S(1)} %get-tuple-element.52), channel_id=1, source_target_pairs={{0,8},{4,12},{8,0},{12,4},{1,9},{5,13},{9,1},{13,5},{2,10},{6,14},... | collective-permute-start | bytes 294920 | tf_op jit(solution)/shard_map/ppermute | solution.py:62
  5.7 9.2 %collective-permute-start.4 = (bf16[32,1536]{1,0:T(8,128)(2,1)S(1)}, bf16[32,1536]{1,0:T(8,128)(2,1)S(1)}, u32[]{:S(2)}, u32[]{:S(2)}) collective-permute-start(bf16[32,1536]{1,0:T(8,128)(2,1)S(1)} %get-tuple-element.51), channel_id=1, source_target_pairs={{0,8},{4,12},{8,0},{12,4},{1,9},{5,13},{9,1},{13,5},{2,10},{6,14},... | collective-permute-start | bytes 294920 | tf_op jit(solution)/shard_map/ppermute | solution.py:62
  13.5 11.4 %collective-permute-start.1 = (bf16[64,1536]{1,0:T(8,128)(2,1)S(1)}, bf16[64,1536]{1,0:T(8,128)(2,1)S(1)}, u32[]{:S(2)}, u32[]{:S(2)}) collective-permute-start(bf16[64,1536]{1,0:T(8,128)(2,1)S(1)} %pad_maximum_fusion.10), channel_id=1, source_target_pairs={{0,4},{4,0},{8,12},{12,8},{1,5},{5,1},{9,13},{13,9},{2,6},{6,2},{1... | collective-permute-start | bytes 589832 | tf_op jit(solution)/shard_map/ppermute | solution.py:62
  14.8 8.4 %collective-permute-start.5 = (bf16[64,1536]{1,0:T(8,128)(2,1)S(1)}, bf16[64,1536]{1,0:T(8,128)(2,1)S(1)}, u32[]{:S(2)}, u32[]{:S(2)}) collective-permute-start(bf16[64,1536]{1,0:T(8,128)(2,1)S(1)} %pad_maximum_fusion.11), channel_id=1, source_target_pairs={{0,4},{4,0},{8,12},{12,8},{1,5},{5,1},{9,13},{13,9},{2,6},{6,2},{1... | collective-permute-start | bytes 589832 | tf_op jit(solution)/shard_map/ppermute | solution.py:62
  15.7 5.9 %collective-permute-start.12 = (bf16[32,1024]{1,0:T(8,128)(2,1)S(1)}, bf16[32,1024]{1,0:T(8,128)(2,1)S(1)}, u32[]{:S(2)}, u32[]{:S(2)}) collective-permute-start(bf16[32,1024]{1,0:T(8,128)(2,1)S(1)} %get-tuple-element.28), channel_id=1, source_target_pairs={{0,2},{2,0},{1,3},{3,1},{4,6},{6,4},{5,7},{7,5},{8,10},{10,8},{9,1... | collective-permute-start | bytes 196616 | tf_op jit(solution)/shard_map/ppermute | solution.py:62
  17.4 4.0 %collective-permute-start.9 = (bf16[32,128]{0,1:T(8,128)(2,1)S(1)}, bf16[32,128]{0,1:T(8,128)(2,1)S(1)}, u32[]{:S(2)}, u32[]{:S(2)}) collective-permute-start(bf16[32,128]{0,1:T(8,128)(2,1)S(1)} %fusion.100), channel_id=1, source_target_pairs={{0,16},{16,0},{1,17},{17,1},{2,18},{18,2},{3,19},{19,3},{4,20},{20... | collective-permute-start | bytes 24584 | tf_op jit(solution)/shard_map/ppermute | solution.py:62
  18.9 4.3 %collective-permute-start.8 = (bf16[32,1024]{1,0:T(8,128)(2,1)S(1)}, bf16[32,1024]{1,0:T(8,128)(2,1)S(1)}, u32[]{:S(2)}, u32[]{:S(2)}) collective-permute-start(bf16[32,1024]{1,0:T(8,128)(2,1)S(1)} %get-tuple-element.24), channel_id=1, source_target_pairs={{0,16},{16,0},{1,17},{17,1},{2,18},{18,2},{3,19},{19,3},{4,20},{20... | collective-permute-start | bytes 196616 | tf_op jit(solution)/shard_map/ppermute | solution.py:62
  21.6 7.8 %copy-start.3 = (bf16[512,1536]{1,0:T(8,128)(2,1)S(1)}, bf16[512,1536]{1,0:T(8,128)(2,1)}, u32[]{:S(2)}) copy-start(bf16[512,1536]{1,0:T(8,128)(2,1)} %constant_dynamic-update-slice_fusion.3) | copy-start | bytes 4718596
  23.2 9.2 %collective-permute-start.6 = (bf16[128,1536]{1,0:T(8,128)(2,1)S(1)}, bf16[128,1536]{1,0:T(8,128)(2,1)S(1)}, u32[]{:S(2)}, u32[]{:S(2)}) collective-permute-start(bf16[128,1536]{1,0:T(8,128)(2,1)S(1)} %pad_maximum_fusion.7), channel_id=1, source_target_pairs={{0,2},{2,0},{1,3},{3,1},{4,6},{6,4},{5,7},{7,5},{8,10},{10,8},{9,1... | collective-permute-start | bytes 1179656 | tf_op jit(solution)/shard_map/ppermute | solution.py:62
  24.9 9.3 %collective-permute-start.2 = (bf16[128,1536]{1,0:T(8,128)(2,1)S(1)}, bf16[128,1536]{1,0:T(8,128)(2,1)S(1)}, u32[]{:S(2)}, u32[]{:S(2)}) collective-permute-start(bf16[128,1536]{1,0:T(8,128)(2,1)S(1)} %pad_maximum_fusion.6), channel_id=1, source_target_pairs={{0,16},{16,0},{1,17},{17,1},{2,18},{18,2},{3,19},{19,3},{4,20},{20... | collective-permute-start | bytes 1179656 | tf_op jit(solution)/shard_map/ppermute | solution.py:62
  26.5 12.4 %collective-permute-start.13 = (bf16[64,1024]{1,0:T(8,128)(2,1)S(1)}, bf16[64,1024]{1,0:T(8,128)(2,1)S(1)}, u32[]{:S(2)}, u32[]{:S(2)}) collective-permute-start(bf16[64,1024]{1,0:T(8,128)(2,1)S(1)} %pad_maximum_fusion.13), channel_id=1, source_target_pairs={{0,8},{4,12},{8,0},{12,4},{1,9},{5,13},{9,1},{13,5},{2,10},{6,14},... | collective-permute-start | bytes 393224 | tf_op jit(solution)/shard_map/ppermute | solution.py:62
  29.4 11.7 %collective-permute-start.10 = (bf16[64,1152]{1,0:T(8,128)(2,1)S(1)}, bf16[64,1152]{1,0:T(8,128)(2,1)S(1)}, u32[]{:S(2)}, u32[]{:S(2)}) collective-permute-start(bf16[64,1152]{1,0:T(8,128)(2,1)S(1)} %pad_maximum_fusion.12), channel_id=1, source_target_pairs={{0,8},{4,12},{8,0},{12,4},{1,9},{5,13},{9,1},{13,5},{2,10},{6,14},... | collective-permute-start | bytes 442376 | tf_op jit(solution)/shard_map/ppermute | solution.py:62
  29.4 24.5 %slice-start.2 = ((s8[7864320]{0:T(1024)(128)(4,1)}), s8[4194304]{0:T(1024)(128)(4,1)S(1)}, s32[]{:S(2)}) async-start(s8[7864320]{0:T(1024)(128)(4,1)} %bitcast.177), calls=%async_computation.2 | async-start | bytes 8388608
  32.5 20.4 %collective-permute-start.7 = (bf16[256,1536]{1,0:T(8,128)(2,1)S(1)}, bf16[256,1536]{1,0:T(8,128)(2,1)S(1)}, u32[]{:S(2)}, u32[]{:S(2)}) collective-permute-start(bf16[256,1536]{1,0:T(8,128)(2,1)S(1)} %pad_maximum_fusion.3), channel_id=1, source_target_pairs={{0,16},{16,0},{1,17},{17,1},{2,18},{18,2},{3,19},{19,3},{4,20},{20... | collective-permute-start | bytes 2359304 | tf_op jit(solution)/shard_map/ppermute | solution.py:62
  34.3 18.7 %collective-permute-start.3 = (bf16[256,1536]{1,0:T(8,128)(2,1)S(1)}, bf16[256,1536]{1,0:T(8,128)(2,1)S(1)}, u32[]{:S(2)}, u32[]{:S(2)}) collective-permute-start(bf16[256,1536]{1,0:T(8,128)(2,1)S(1)} %pad_maximum_fusion.2), channel_id=1, source_target_pairs={{0,2},{2,0},{1,3},{3,1},{4,6},{6,4},{5,7},{7,5},{8,10},{10,8},{9,1... | collective-permute-start | bytes 2359304 | tf_op jit(solution)/shard_map/ppermute | solution.py:62
  38.8 9.3 %collective-permute-start.14 = (bf16[128,1024]{1,0:T(8,128)(2,1)S(1)}, bf16[128,1024]{1,0:T(8,128)(2,1)S(1)}, u32[]{:S(2)}, u32[]{:S(2)}) collective-permute-start(bf16[128,1024]{1,0:T(8,128)(2,1)S(1)} %pad_maximum_fusion.9), channel_id=1, source_target_pairs={{0,4},{4,0},{8,12},{12,8},{1,5},{5,1},{9,13},{13,9},{2,6},{6,2},{1... | collective-permute-start | bytes 786440 | tf_op jit(solution)/shard_map/ppermute | solution.py:62
  41.1 11.8 %collective-permute-start.11 = (bf16[128,1152]{1,0:T(8,128)(2,1)S(1)}, bf16[128,1152]{1,0:T(8,128)(2,1)S(1)}, u32[]{:S(2)}, u32[]{:S(2)}) collective-permute-start(bf16[128,1152]{1,0:T(8,128)(2,1)S(1)} %pad_maximum_fusion.8), channel_id=1, source_target_pairs={{0,4},{4,0},{8,12},{12,8},{1,5},{5,1},{9,13},{13,9},{2,6},{6,2},{1... | collective-permute-start | bytes 884744 | tf_op jit(solution)/shard_map/ppermute | solution.py:62
  41.8 12.1 %slice-start.3 = ((s8[7864320]{0:T(1024)(128)(4,1)}), s8[3670016]{0:T(1024)(128)(4,1)S(1)}, s32[]{:S(2)}) async-start(s8[7864320]{0:T(1024)(128)(4,1)} %bitcast.177), calls=%async_computation.3 | async-start | bytes 7340032
  53.0 10.1 %collective-permute-start.17 = (bf16[512,1536]{1,0:T(8,128)(2,1)S(1)}, bf16[512,1536]{1,0:T(8,128)(2,1)S(1)}, u32[]{:S(2)}, u32[]{:S(2)}) collective-permute-start(bf16[512,1536]{1,0:T(8,128)(2,1)S(1)} %constant_dynamic-update-slice_fusion), channel_id=1, source_target_pairs={{0,1},{1,0},{2,3},{3,2},{4,5},{5,4},{6,7},{7,6},{8,9},{9,8},{10,11... | collective-permute-start | bytes 4718600 | tf_op jit(solution)/shard_map/ppermute | solution.py:62
  53.3 3.1 %slice-start.1 = ((s8[7864320]{0:T(1024)(128)(4,1)}), s8[3670016]{0:T(1024)(128)(4,1)S(1)}, s32[]{:S(2)}) async-start(s8[7864320]{0:T(1024)(128)(4,1)} %bitcast.173), calls=%async_computation.1 | async-start | bytes 7340032
  53.3 8.4 %collective-permute-start.18 = (bf16[512,1536]{1,0:T(8,128)(2,1)S(1)}, bf16[512,1536]{1,0:T(8,128)(2,1)S(1)}, u32[]{:S(2)}, u32[]{:S(2)}) collective-permute-start(bf16[512,1536]{1,0:T(8,128)(2,1)S(1)} %bitcast.157), channel_id=1, source_target_pairs={{0,1},{1,0},{2,3},{3,2},{4,5},{5,4},{6,7},{7,6},{8,9},{9,8},{10,11... | collective-permute-start | bytes 4718600 | tf_op jit(solution)/shard_map/ppermute | solution.py:62
  57.8 14.8 %collective-permute-start.15 = (bf16[256,1152]{1,0:T(8,128)(2,1)S(1)}, bf16[256,1152]{1,0:T(8,128)(2,1)S(1)}, u32[]{:S(2)}, u32[]{:S(2)}) collective-permute-start(bf16[256,1152]{1,0:T(8,128)(2,1)S(1)} %pad_maximum_fusion.4), channel_id=1, source_target_pairs={{0,2},{2,0},{1,3},{3,1},{4,6},{6,4},{5,7},{7,5},{8,10},{10,8},{9,1... | collective-permute-start | bytes 1769480 | tf_op jit(solution)/shard_map/ppermute | solution.py:62
  58.4 13.0 %collective-permute-start.16 = (bf16[256,1024]{1,0:T(8,128)(2,1)S(1)}, bf16[256,1024]{1,0:T(8,128)(2,1)S(1)}, u32[]{:S(2)}, u32[]{:S(2)}) collective-permute-start(bf16[256,1024]{1,0:T(8,128)(2,1)S(1)} %pad_maximum_fusion.5), channel_id=1, source_target_pairs={{0,16},{16,0},{1,17},{17,1},{2,18},{18,2},{3,19},{19,3},{4,20},{20... | collective-permute-start | bytes 1572872 | tf_op jit(solution)/shard_map/ppermute | solution.py:62
  72.8 5.4 %collective-permute-start.19 = (bf16[512,1152]{1,0:T(8,128)(2,1)S(1)}, bf16[512,1152]{1,0:T(8,128)(2,1)S(1)}, u32[]{:S(2)}, u32[]{:S(2)}) collective-permute-start(bf16[512,1152]{1,0:T(8,128)(2,1)S(1)} %bitcast.150), channel_id=1, source_target_pairs={{0,1},{1,0},{2,3},{3,2},{4,5},{5,4},{6,7},{7,6},{8,9},{9,8},{10,11... | collective-permute-start | bytes 3538952 | tf_op jit(solution)/shard_map/ppermute | solution.py:62
  73.0 4.2 %collective-permute-start.20 = (bf16[512,1024]{1,0:T(8,128)(2,1)S(1)}, bf16[512,1024]{1,0:T(8,128)(2,1)S(1)}, u32[]{:S(2)}, u32[]{:S(2)}) collective-permute-start(bf16[512,1024]{1,0:T(8,128)(2,1)S(1)} %bitcast.164), channel_id=1, source_target_pairs={{0,1},{1,0},{2,3},{3,2},{4,5},{5,4},{6,7},{7,6},{8,9},{9,8},{10,11... | collective-permute-start | bytes 3145736 | tf_op jit(solution)/shard_map/ppermute | solution.py:62
  85.2 5.6 %collective-permute-start.36 = (bf16[512,1152]{1,0:T(8,128)(2,1)S(1)}, bf16[512,1152]{1,0:T(8,128)(2,1)S(1)}, u32[]{:S(2)}, u32[]{:S(2)}) collective-permute-start(bf16[512,1152]{1,0:T(8,128)(2,1)S(1)} %convolution_convert_fusion), channel_id=1, source_target_pairs={{0,1},{1,0},{2,3},{3,2},{4,5},{5,4},{6,7},{7,6},{8,9},{9,8},{10,11... | collective-permute-start | bytes 3538952 | tf_op jit(solution)/shard_map/ppermute | solution.py:62
  85.4 7.3 %collective-permute-start.31 = (bf16[512,1152]{1,0:T(8,128)(2,1)S(1)}, bf16[512,1152]{1,0:T(8,128)(2,1)S(1)}, u32[]{:S(2)}, u32[]{:S(2)}) collective-permute-start(bf16[512,1152]{1,0:T(8,128)(2,1)S(1)} %convolution_convert_fusion.1), channel_id=1, source_target_pairs={{0,1},{1,0},{2,3},{3,2},{4,5},{5,4},{6,7},{7,6},{8,9},{9,8},{10,11... | collective-permute-start | bytes 3538952 | tf_op jit(solution)/shard_map/ppermute | solution.py:62
  87.3 7.5 %collective-permute-start.26 = (bf16[512,1408]{1,0:T(8,128)(2,1)S(1)}, bf16[512,1408]{1,0:T(8,128)(2,1)S(1)}, u32[]{:S(2)}, u32[]{:S(2)}) collective-permute-start(bf16[512,1408]{1,0:T(8,128)(2,1)S(1)} %convolution_convert_fusion.2), channel_id=1, source_target_pairs={{0,1},{1,0},{2,3},{3,2},{4,5},{5,4},{6,7},{7,6},{8,9},{9,8},{10,11... | collective-permute-start | bytes 4325384 | tf_op jit(solution)/shard_map/ppermute | solution.py:62
  88.9 8.9 %collective-permute-start.21 = (bf16[512,1408]{1,0:T(8,128)(2,1)S(1)}, bf16[512,1408]{1,0:T(8,128)(2,1)S(1)}, u32[]{:S(2)}, u32[]{:S(2)}) collective-permute-start(bf16[512,1408]{1,0:T(8,128)(2,1)S(1)} %convolution_convert_fusion.3), channel_id=1, source_target_pairs={{0,1},{1,0},{2,3},{3,2},{4,5},{5,4},{6,7},{7,6},{8,9},{9,8},{10,11... | collective-permute-start | bytes 4325384 | tf_op jit(solution)/shard_map/ppermute | solution.py:62
  92.1 16.2 %collective-permute-start.37 = (bf16[256,1152]{1,0:T(8,128)(2,1)S(1)}, bf16[256,1152]{1,0:T(8,128)(2,1)S(1)}, u32[]{:S(2)}, u32[]{:S(2)}) collective-permute-start(bf16[256,1152]{1,0:T(8,128)(2,1)S(1)} %split.57), channel_id=1, source_target_pairs={{0,16},{16,0},{1,17},{17,1},{2,18},{18,2},{3,19},{19,3},{4,20},{20... | collective-permute-start | bytes 1769480 | tf_op jit(solution)/shard_map/ppermute | solution.py:62
  94.2 16.3 %collective-permute-start.32 = (bf16[256,1152]{1,0:T(8,128)(2,1)S(1)}, bf16[256,1152]{1,0:T(8,128)(2,1)S(1)}, u32[]{:S(2)}, u32[]{:S(2)}) collective-permute-start(bf16[256,1152]{1,0:T(8,128)(2,1)S(1)} %split.53), channel_id=1, source_target_pairs={{0,2},{2,0},{1,3},{3,1},{4,6},{6,4},{5,7},{7,5},{8,10},{10,8},{9,1... | collective-permute-start | bytes 1769480 | tf_op jit(solution)/shard_map/ppermute | solution.py:62
  96.2 30.9 %collective-permute-start.27 = (bf16[256,1408]{1,0:T(8,128)(2,1)S(1)}, bf16[256,1408]{1,0:T(8,128)(2,1)S(1)}, u32[]{:S(2)}, u32[]{:S(2)}) collective-permute-start(bf16[256,1408]{1,0:T(8,128)(2,1)S(1)} %split.51), channel_id=1, source_target_pairs={{0,16},{16,0},{1,17},{17,1},{2,18},{18,2},{3,19},{19,3},{4,20},{20... | collective-permute-start | bytes 2162696 | tf_op jit(solution)/shard_map/ppermute | solution.py:62
  99.3 29.8 %collective-permute-start.22 = (bf16[256,1408]{1,0:T(8,128)(2,1)S(1)}, bf16[256,1408]{1,0:T(8,128)(2,1)S(1)}, u32[]{:S(2)}, u32[]{:S(2)}) collective-permute-start(bf16[256,1408]{1,0:T(8,128)(2,1)S(1)} %split.49), channel_id=1, source_target_pairs={{0,2},{2,0},{1,3},{3,1},{4,6},{6,4},{5,7},{7,5},{8,10},{10,8},{9,1... | collective-permute-start | bytes 2162696 | tf_op jit(solution)/shard_map/ppermute | solution.py:62
  108.5 11.6 %collective-permute-start.38 = (bf16[128,1152]{1,0:T(8,128)(2,1)S(1)}, bf16[128,1152]{1,0:T(8,128)(2,1)S(1)}, u32[]{:S(2)}, u32[]{:S(2)}) collective-permute-start(bf16[128,1152]{1,0:T(8,128)(2,1)S(1)} %slice.217), channel_id=1, source_target_pairs={{0,4},{4,0},{8,12},{12,8},{1,5},{5,1},{9,13},{13,9},{2,6},{6,2},{1... | collective-permute-start | bytes 884744 | tf_op jit(solution)/shard_map/ppermute | solution.py:62
  110.7 13.2 %collective-permute-start.33 = (bf16[128,1152]{1,0:T(8,128)(2,1)S(1)}, bf16[128,1152]{1,0:T(8,128)(2,1)S(1)}, u32[]{:S(2)}, u32[]{:S(2)}) collective-permute-start(bf16[128,1152]{1,0:T(8,128)(2,1)S(1)} %slice.212), channel_id=1, source_target_pairs={{0,4},{4,0},{8,12},{12,8},{1,5},{5,1},{9,13},{13,9},{2,6},{6,2},{1... | collective-permute-start | bytes 884744 | tf_op jit(solution)/shard_map/ppermute | solution.py:62
  120.2 12.6 %collective-permute-start.39 = (bf16[64,1152]{1,0:T(8,128)(2,1)S(1)}, bf16[64,1152]{1,0:T(8,128)(2,1)S(1)}, u32[]{:S(2)}, u32[]{:S(2)}) collective-permute-start(bf16[64,1152]{1,0:T(8,128)(2,1)S(1)} %split.59), channel_id=1, source_target_pairs={{0,8},{4,12},{8,0},{12,4},{1,9},{5,13},{9,1},{13,5},{2,10},{6,14},... | collective-permute-start | bytes 442376 | tf_op jit(solution)/shard_map/ppermute | solution.py:62
  124.0 10.6 %collective-permute-start.34 = (bf16[64,1152]{1,0:T(8,128)(2,1)S(1)}, bf16[64,1152]{1,0:T(8,128)(2,1)S(1)}, u32[]{:S(2)}, u32[]{:S(2)}) collective-permute-start(bf16[64,1152]{1,0:T(8,128)(2,1)S(1)} %split.55), channel_id=1, source_target_pairs={{0,8},{4,12},{8,0},{12,4},{1,9},{5,13},{9,1},{13,5},{2,10},{6,14},... | collective-permute-start | bytes 442376 | tf_op jit(solution)/shard_map/ppermute | solution.py:62
  127.4 8.2 %collective-permute-start.28 = (bf16[128,1408]{1,0:T(8,128)(2,1)S(1)}, bf16[128,1408]{1,0:T(8,128)(2,1)S(1)}, u32[]{:S(2)}, u32[]{:S(2)}) collective-permute-start(bf16[128,1408]{1,0:T(8,128)(2,1)S(1)} %slice.205), channel_id=1, source_target_pairs={{0,2},{2,0},{1,3},{3,1},{4,6},{6,4},{5,7},{7,5},{8,10},{10,8},{9,1... | collective-permute-start | bytes 1081352 | tf_op jit(solution)/shard_map/ppermute | solution.py:62
  129.3 8.2 %collective-permute-start.23 = (bf16[128,1408]{1,0:T(8,128)(2,1)S(1)}, bf16[128,1408]{1,0:T(8,128)(2,1)S(1)}, u32[]{:S(2)}, u32[]{:S(2)}) collective-permute-start(bf16[128,1408]{1,0:T(8,128)(2,1)S(1)} %slice.198), channel_id=1, source_target_pairs={{0,16},{16,0},{1,17},{17,1},{2,18},{18,2},{3,19},{19,3},{4,20},{20... | collective-permute-start | bytes 1081352 | tf_op jit(solution)/shard_map/ppermute | solution.py:62
  132.8 14.7 %collective-permute-start.40 = (bf16[32,1152]{1,0:T(8,128)(2,1)S(1)}, bf16[32,1152]{1,0:T(8,128)(2,1)S(1)}, u32[]{:S(2)}, u32[]{:S(2)}) collective-permute-start(bf16[32,1152]{1,0:T(8,128)(2,1)S(1)} %slice.219), channel_id=1, source_target_pairs={{0,2},{2,0},{1,3},{3,1},{4,6},{6,4},{5,7},{7,5},{8,10},{10,8},{9,1... | collective-permute-start | bytes 221192 | tf_op jit(solution)/shard_map/ppermute | solution.py:62
  134.6 12.9 %collective-permute-start.35 = (bf16[32,1152]{1,0:T(8,128)(2,1)S(1)}, bf16[32,1152]{1,0:T(8,128)(2,1)S(1)}, u32[]{:S(2)}, u32[]{:S(2)}) collective-permute-start(bf16[32,1152]{1,0:T(8,128)(2,1)S(1)} %slice.214), channel_id=1, source_target_pairs={{0,16},{16,0},{1,17},{17,1},{2,18},{18,2},{3,19},{19,3},{4,20},{20... | collective-permute-start | bytes 221192 | tf_op jit(solution)/shard_map/ppermute | solution.py:62
  135.6 11.9 %copy-start.2 = (bf16[1,32,5120]{2,1,0:T(8,128)(2,1)S(1)}, bf16[1,32,5120]{2,1,0:T(8,128)(2,1)}, u32[]{:S(2)}) copy-start(bf16[1,32,5120]{2,1,0:T(8,128)(2,1)} %param.6) | copy-start | bytes 983044
  135.7 7.0 %collective-permute-start.29 = (bf16[64,1408]{1,0:T(8,128)(2,1)S(1)}, bf16[64,1408]{1,0:T(8,128)(2,1)S(1)}, u32[]{:S(2)}, u32[]{:S(2)}) collective-permute-start(bf16[64,1408]{1,0:T(8,128)(2,1)S(1)} %slice.207), channel_id=1, source_target_pairs={{0,4},{4,0},{8,12},{12,8},{1,5},{5,1},{9,13},{13,9},{2,6},{6,2},{1... | collective-permute-start | bytes 540680 | tf_op jit(solution)/shard_map/ppermute | solution.py:62
  137.6 15.1 %copy-start.1 = (f32[1,64,6]{1,0,2:T(1,128)S(1)}, f32[1,64,6]{1,0,2:T(1,128)}, u32[]{:S(2)}) copy-start(f32[1,64,6]{1,0,2:T(1,128)} %param.8) | copy-start | bytes 4612
  137.7 7.8 %collective-permute-start.24 = (bf16[64,1408]{1,0:T(8,128)(2,1)S(1)}, bf16[64,1408]{1,0:T(8,128)(2,1)S(1)}, u32[]{:S(2)}, u32[]{:S(2)}) collective-permute-start(bf16[64,1408]{1,0:T(8,128)(2,1)S(1)} %slice.200), channel_id=1, source_target_pairs={{0,4},{4,0},{8,12},{12,8},{1,5},{5,1},{9,13},{13,9},{2,6},{6,2},{1... | collective-permute-start | bytes 540680 | tf_op jit(solution)/shard_map/ppermute | solution.py:62
  142.7 6.5 %collective-permute-start.30 = (bf16[32,1408]{1,0:T(8,128)(2,1)S(1)}, bf16[32,1408]{1,0:T(8,128)(2,1)S(1)}, u32[]{:S(2)}, u32[]{:S(2)}) collective-permute-start(bf16[32,1408]{1,0:T(8,128)(2,1)S(1)} %slice.209), channel_id=1, source_target_pairs={{0,8},{4,12},{8,0},{12,4},{1,9},{5,13},{9,1},{13,5},{2,10},{6,14},... | collective-permute-start | bytes 270344 | tf_op jit(solution)/shard_map/ppermute | solution.py:62
  145.5 6.4 %collective-permute-start.25 = (bf16[32,1408]{1,0:T(8,128)(2,1)S(1)}, bf16[32,1408]{1,0:T(8,128)(2,1)S(1)}, u32[]{:S(2)}, u32[]{:S(2)}) collective-permute-start(bf16[32,1408]{1,0:T(8,128)(2,1)S(1)} %slice.202), channel_id=1, source_target_pairs={{0,8},{4,12},{8,0},{12,4},{1,9},{5,13},{9,1},{13,5},{2,10},{6,14},... | collective-permute-start | bytes 270344 | tf_op jit(solution)/shard_map/ppermute | solution.py:62
  (3 other events, 7.4 us)

commit v4 on v3

--- a/solution.py
+++ b/solution.py
@@ -146,8 +146,10 @@
 
     halves = [{"gate": 0.0, "up": 0.0}, {"gate": 0.0, "up": 0.0}]
     for c in range(n_chunks):
+        if c == 1:
+            partial = halves[1]["up"]
         if c == 2:
-            ties = [sums[name] for sums in halves for name in ("gate", "up")]
+            ties = [halves[0]["gate"], halves[0]["up"], halves[1]["gate"], partial]
             received[2:] = lax.optimization_barrier(received[2:] + ties)[:2]
         own = ordered(jnp.concatenate([before_last[c], received[c]], axis=0), STAGES[c], STAGES[0])
         for rows, sums in zip((own, swap(own, "core")), halves):
@@ -180,7 +182,10 @@
     first = {c: added(kept[c], sent[c]) for c in one}
     outs = {}
     for c in two:
-        value = halved(added(kept[c], after(sent[c], *[parts[d] for d in one])), NEAR)
+        value = added(kept[c], after(sent[c], *[parts[d] for d in one]))
+        stays, goes = jnp.split(value, 2, axis=0)
+        goes = swap(goes, *NEAR)
+        value = added(stays, after(goes, *first.values()) if c == two[0] else goes)
         stays, goes = jnp.split(value, 2, axis=0)
         value = added(stays, after(swap(goes, *FAR), *first.values()))
         outs[c] = (value, STAGES[c][0])

time: 153 us -> 152 us (level)
  waiting for transfers between devices: 68.3 us -> 58.5 us
  starting transfers between devices: 42.7 us -> 52.4 us
    ppermute x41, waiting for transfers between devices: 68.3 us -> 58.5 us  [swap(): return lax.ppermute(value, axis, [(i, i ^ flip) for i in range(size)])]
    ppermute x41, starting transfers between devices: 42.7 us -> 52.4 us  [swap(): return lax.ppermute(value, axis, [(i, i ^ flip) for i in range(size)])]
    unnamed x29 -> x27, local copies, waits for them, and re-layouts: 4.32 us -> 3.17 us
  transfers between devices with their start and end apart: 41 -> 41, of which waited for: 24 -> 19; matrix products, arithmetic and copies ran while one was open for 20% -> 20% of each run, Pallas kernels for 0% -> 0%
where the time goes in v4:
time: 152 us
  waiting for transfers between devices  58.5 us (38%)
  starting transfers between devices  52.4 us (34%)
  matrix products  31 us (20%)
  local copies, waits for them, and re-layouts  6.13 us (4%)
  other arithmetic  2.79 us (2%)
    ppermute x41, waiting for transfers between devices, swap(): return lax.ppermute(value, axis, [(i, i ^ flip) for i in range(size)])  58.5 us
    ppermute x41, starting transfers between devices, swap(): return lax.ppermute(value, axis, [(i, i ^ flip) for i in range(size)])  52.4 us
    dot_general x16, matrix products, ring_body(): lax.dot_general(rows, weight[0, :, spans[c]], dims, preferred_element_typ...  20.3 us
    dot_general x8, matrix products, down(): jnp.dot(value, down_weight[0, :, back_spans[c]], preferred_element_type=j...  10.7 us
    unnamed x27, local copies, waits for them, and re-layouts  3.17 us
  transfers between devices with their start and end apart: 41, of which 19 were waited for; matrix products, arithmetic and copies ran while one was open for 20% of the time, Pallas kernels for 0%

profile of v4, /device:TPU:0, one launch (start us, length us, event | category | flops | bytes accessed | tf_op | source)
XLA Modules:
  0.0 151.6 jit_solution(15033328298630837985)
XLA Ops:
  0.0 1.6 %constant_dynamic-update-slice_fusion.4 = (bf16[512,1536]{1,0:T(8,128)(2,1)}, bf16[512,1536]{1,0:T(8,128)(2,1)S(1)}, bf16[32,1536]{1,0:T(8,128)(2,1)S(1)}, bf16[32,1536]{1,0:T(8,128)(2,1)S(1)}) fusion(bf16[32,5120]{1,0:T(8,128)(2,1)} %bitcast.158), kind=kLoop, calls=%fused_computation.132 | loop fusion | bytes 589824
  1.6 4.0 %collective-permute-start.4 = (bf16[32,1536]{1,0:T(8,128)(2,1)S(1)}, bf16[32,1536]{1,0:T(8,128)(2,1)S(1)}, u32[]{:S(2)}, u32[]{:S(2)}) collective-permute-start(bf16[32,1536]{1,0:T(8,128)(2,1)S(1)} %get-tuple-element.53), channel_id=1, source_target_pairs={{0,8},{4,12},{8,0},{12,4},{1,9},{5,13},{9,1},{13,5},{2,10},{6,14},... | collective-permute-start | bytes 294920 | tf_op jit(solution)/shard_map/ppermute | solution.py:62
  7.5 6.0 %collective-permute-done.4 = bf16[32,1536]{1,0:T(8,128)(2,1)S(1)} collective-permute-done((bf16[32,1536]{1,0:T(8,128)(2,1)S(1)}, bf16[32,1536]{1,0:T(8,128)(2,1)S(1)}, u32[]{:S(2)}, u32[]{:S(2)}) %collective-permute-start.4) | collective-permute-done | bytes 98336 | tf_op jit(solution)/shard_map/ppermute | solution.py:62
  15.7 1.7 %collective-permute-start.9 = (bf16[32,128]{0,1:T(8,128)(2,1)S(1)}, bf16[32,128]{0,1:T(8,128)(2,1)S(1)}, u32[]{:S(2)}, u32[]{:S(2)}) collective-permute-start(bf16[32,128]{0,1:T(8,128)(2,1)S(1)} %fusion.97), channel_id=1, source_target_pairs={{0,16},{16,0},{1,17},{17,1},{2,18},{18,2},{3,19},{19,3},{4,20},{20... | collective-permute-start | bytes 24584 | tf_op jit(solution)/shard_map/ppermute | solution.py:62
  17.7 1.7 %collective-permute-start.12 = (bf16[32,1024]{1,0:T(8,128)(2,1)S(1)}, bf16[32,1024]{1,0:T(8,128)(2,1)S(1)}, u32[]{:S(2)}, u32[]{:S(2)}) collective-permute-start(bf16[32,1024]{1,0:T(8,128)(2,1)S(1)} %get-tuple-element.29), channel_id=1, source_target_pairs={{0,2},{2,0},{1,3},{3,1},{4,6},{6,4},{5,7},{7,5},{8,10},{10,8},{9,1... | collective-permute-start | bytes 196616 | tf_op jit(solution)/shard_map/ppermute | solution.py:62
  20.3 1.7 %collective-permute-done.12 = bf16[32,1024]{1,0:T(8,128)(2,1)S(1)} collective-permute-done((bf16[32,1024]{1,0:T(8,128)(2,1)S(1)}, bf16[32,1024]{1,0:T(8,128)(2,1)S(1)}, u32[]{:S(2)}, u32[]{:S(2)}) %collective-permute-start.12) | collective-permute-done | bytes 65568 | tf_op jit(solution)/shard_map/ppermute | solution.py:62
  22.1 1.8 %collective-permute-start.6 = (bf16[128,1536]{1,0:T(8,128)(2,1)S(1)}, bf16[128,1536]{1,0:T(8,128)(2,1)S(1)}, u32[]{:S(2)}, u32[]{:S(2)}) collective-permute-start(bf16[128,1536]{1,0:T(8,128)(2,1)S(1)} %pad_maximum_fusion.7), channel_id=1, source_target_pairs={{0,2},{2,0},{1,3},{3,1},{4,6},{6,4},{5,7},{7,5},{8,10},{10,8},{9,1... | collective-permute-start | bytes 1179656 | tf_op jit(solution)/shard_map/ppermute | solution.py:62
  23.9 1.6 %collective-permute-start.2 = (bf16[128,1536]{1,0:T(8,128)(2,1)S(1)}, bf16[128,1536]{1,0:T(8,128)(2,1)S(1)}, u32[]{:S(2)}, u32[]{:S(2)}) collective-permute-start(bf16[128,1536]{1,0:T(8,128)(2,1)S(1)} %pad_maximum_fusion.6), channel_id=1, source_target_pairs={{0,16},{16,0},{1,17},{17,1},{2,18},{18,2},{3,19},{19,3},{4,20},{20... | collective-permute-start | bytes 1179656 | tf_op jit(solution)/shard_map/ppermute | solution.py:62
  25.5 3.1 %collective-permute-start.13 = (bf16[64,1024]{1,0:T(8,128)(2,1)S(1)}, bf16[64,1024]{1,0:T(8,128)(2,1)S(1)}, u32[]{:S(2)}, u32[]{:S(2)}) collective-permute-start(bf16[64,1024]{1,0:T(8,128)(2,1)S(1)} %pad_maximum_fusion.13), channel_id=1, source_target_pairs={{0,8},{4,12},{8,0},{12,4},{1,9},{5,13},{9,1},{13,5},{2,10},{6,14},... | collective-permute-start | bytes 393224 | tf_op jit(solution)/shard_map/ppermute | solution.py:62
  28.6 4.2 %collective-permute-done.2 = bf16[128,1536]{1,0:T(8,128)(2,1)S(1)} collective-permute-done((bf16[128,1536]{1,0:T(8,128)(2,1)S(1)}, bf16[128,1536]{1,0:T(8,128)(2,1)S(1)}, u32[]{:S(2)}, u32[]{:S(2)}) %collective-permute-start.2) | collective-permute-done | bytes 393248 | tf_op jit(solution)/shard_map/ppermute | solution.py:62
  33.6 1.6 %collective-permute-start.7 = (bf16[256,1536]{1,0:T(8,128)(2,1)S(1)}, bf16[256,1536]{1,0:T(8,128)(2,1)S(1)}, u32[]{:S(2)}, u32[]{:S(2)}) collective-permute-start(bf16[256,1536]{1,0:T(8,128)(2,1)S(1)} %pad_maximum_fusion.3), channel_id=1, source_target_pairs={{0,16},{16,0},{1,17},{17,1},{2,18},{18,2},{3,19},{19,3},{4,20},{20... | collective-permute-start | bytes 2359304 | tf_op jit(solution)/shard_map/ppermute | solution.py:62
  35.2 2.3 %collective-permute-done.13 = bf16[64,1024]{1,0:T(8,128)(2,1)S(1)} collective-permute-done((bf16[64,1024]{1,0:T(8,128)(2,1)S(1)}, bf16[64,1024]{1,0:T(8,128)(2,1)S(1)}, u32[]{:S(2)}, u32[]{:S(2)}) %collective-permute-start.13) | collective-permute-done | bytes 131104 | tf_op jit(solution)/shard_map/ppermute | solution.py:62
  37.5 2.1 %collective-permute-done.10 = bf16[64,1152]{1,0:T(8,128)(2,1)S(1)} collective-permute-done((bf16[64,1152]{1,0:T(8,128)(2,1)S(1)}, bf16[64,1152]{1,0:T(8,128)(2,1)S(1)}, u32[]{:S(2)}, u32[]{:S(2)}) %collective-permute-start.10) | collective-permute-done | bytes 147488 | tf_op jit(solution)/shard_map/ppermute | solution.py:62
  40.4 1.4 collective-permute-start.11
  41.9 7.1 %collective-permute-done.14 = bf16[128,1024]{1,0:T(8,128)(2,1)S(1)} collective-permute-done((bf16[128,1024]{1,0:T(8,128)(2,1)S(1)}, bf16[128,1024]{1,0:T(8,128)(2,1)S(1)}, u32[]{:S(2)}, u32[]{:S(2)}) %collective-permute-start.14) | collective-permute-done | bytes 262176 | tf_op jit(solution)/shard_map/ppermute | solution.py:62
  49.0 4.3 %collective-permute-done.11 = bf16[128,1152]{1,0:T(8,128)(2,1)S(1)} collective-permute-done((bf16[128,1152]{1,0:T(8,128)(2,1)S(1)}, bf16[128,1152]{1,0:T(8,128)(2,1)S(1)}, u32[]{:S(2)}, u32[]{:S(2)}) %collective-permute-start.11) | collective-permute-done | bytes 294944 | tf_op jit(solution)/shard_map/ppermute | solution.py:62
  54.2 1.5 %collective-permute-start.15 = (bf16[256,1152]{1,0:T(8,128)(2,1)S(1)}, bf16[256,1152]{1,0:T(8,128)(2,1)S(1)}, u32[]{:S(2)}, u32[]{:S(2)}) collective-permute-start(bf16[256,1152]{1,0:T(8,128)(2,1)S(1)} %pad_maximum_fusion.4), channel_id=1, source_target_pairs={{0,2},{2,0},{1,3},{3,1},{4,6},{6,4},{5,7},{7,5},{8,10},{10,8},{9,1... | collective-permute-start | bytes 1769480 | tf_op jit(solution)/shard_map/ppermute | solution.py:62
  55.7 1.4 fusion.2
  57.8 1.4 fusion.10
  59.2 1.4 fusion.78
  60.6 1.4 fusion.72
  62.1 1.4 fusion.8
  63.5 1.4 fusion.4
  64.9 1.4 fusion.75
  70.4 1.6 %fusion = f32[512,768]{1,0:T(8,128)S(1)} fusion(bf16[512,1536]{1,0:T(8,128)(2,1)S(1)} %collective-permute-done.18, bf16[1,768,5120]{2,1,0:T(8,128)(2,1)S(1)} %copy-done.4), kind=kOutput, calls=%fused_computation.6 | convolution fusion | flops 1207959552 | bytes 5505024 | tf_op jit(solution)/shard_map/dot_general | solution.py:162
  76.3 1.5 multiply_convert_fusion.1
  81.7 1.4 convolution_convert_fusion.3
  83.3 1.4 convolution_convert_fusion.2
  87.9 1.6 %collective-permute-start.37 = (bf16[256,1152]{1,0:T(8,128)(2,1)S(1)}, bf16[256,1152]{1,0:T(8,128)(2,1)S(1)}, u32[]{:S(2)}, u32[]{:S(2)}) collective-permute-start(bf16[256,1152]{1,0:T(8,128)(2,1)S(1)} %split.75), channel_id=1, source_target_pairs={{0,16},{16,0},{1,17},{17,1},{2,18},{18,2},{3,19},{19,3},{4,20},{20... | collective-permute-start | bytes 1769480 | tf_op jit(solution)/shard_map/ppermute | solution.py:62
  89.5 1.5 add_convert_fusion.3
  91.0 1.6 %collective-permute-start.32 = (bf16[256,1152]{1,0:T(8,128)(2,1)S(1)}, bf16[256,1152]{1,0:T(8,128)(2,1)S(1)}, u32[]{:S(2)}, u32[]{:S(2)}) collective-permute-start(bf16[256,1152]{1,0:T(8,128)(2,1)S(1)} %split.69), channel_id=1, source_target_pairs={{0,2},{2,0},{1,3},{3,1},{4,6},{6,4},{5,7},{7,5},{8,10},{10,8},{9,1... | collective-permute-start | bytes 1769480 | tf_op jit(solution)/shard_map/ppermute | solution.py:62
  92.6 1.4 add_convert_fusion.1
  94.6 1.4 add_convert_fusion
  96.7 7.5 %collective-permute-done.37 = bf16[256,1152]{1,0:T(8,128)(2,1)S(1)} collective-permute-done((bf16[256,1152]{1,0:T(8,128)(2,1)S(1)}, bf16[256,1152]{1,0:T(8,128)(2,1)S(1)}, u32[]{:S(2)}, u32[]{:S(2)}) %collective-permute-start.37) | collective-permute-done | bytes 589856 | tf_op jit(solution)/shard_map/ppermute | solution.py:62
  104.3 2.5 %collective-permute-start.38 = (bf16[128,1152]{1,0:T(8,128)(2,1)S(1)}, bf16[128,1152]{1,0:T(8,128)(2,1)S(1)}, u32[]{:S(2)}, u32[]{:S(2)}) collective-permute-start(bf16[128,1152]{1,0:T(8,128)(2,1)S(1)} %split.77), channel_id=1, source_target_pairs={{0,4},{4,0},{8,12},{12,8},{1,5},{5,1},{9,13},{13,9},{2,6},{6,2},{1... | collective-permute-start | bytes 884744 | tf_op jit(solution)/shard_map/ppermute | solution.py:62
  107.4 2.5 %collective-permute-start.33 = (bf16[128,1152]{1,0:T(8,128)(2,1)S(1)}, bf16[128,1152]{1,0:T(8,128)(2,1)S(1)}, u32[]{:S(2)}, u32[]{:S(2)}) collective-permute-start(bf16[128,1152]{1,0:T(8,128)(2,1)S(1)} %split.71), channel_id=1, source_target_pairs={{0,4},{4,0},{8,12},{12,8},{1,5},{5,1},{9,13},{13,9},{2,6},{6,2},{1... | collective-permute-start | bytes 884744 | tf_op jit(solution)/shard_map/ppermute | solution.py:62
  110.0 6.4 %collective-permute-done.38 = bf16[128,1152]{1,0:T(8,128)(2,1)S(1)} collective-permute-done((bf16[128,1152]{1,0:T(8,128)(2,1)S(1)}, bf16[128,1152]{1,0:T(8,128)(2,1)S(1)}, u32[]{:S(2)}, u32[]{:S(2)}) %collective-permute-start.38) | collective-permute-done | bytes 294944 | tf_op jit(solution)/shard_map/ppermute | solution.py:62
  116.5 3.0 %collective-permute-start.39 = (bf16[64,1152]{1,0:T(8,128)(2,1)S(1)}, bf16[64,1152]{1,0:T(8,128)(2,1)S(1)}, u32[]{:S(2)}, u32[]{:S(2)}) collective-permute-start(bf16[64,1152]{1,0:T(8,128)(2,1)S(1)} %split.79), channel_id=1, source_target_pairs={{0,8},{4,12},{8,0},{12,4},{1,9},{5,13},{9,1},{13,5},{2,10},{6,14},... | collective-permute-start | bytes 442376 | tf_op jit(solution)/shard_map/ppermute | solution.py:62
  119.4 2.1 %collective-permute-done.22 = bf16[256,1408]{1,0:T(8,128)(2,1)S(1)} collective-permute-done((bf16[256,1408]{1,0:T(8,128)(2,1)S(1)}, bf16[256,1408]{1,0:T(8,128)(2,1)S(1)}, u32[]{:S(2)}, u32[]{:S(2)}) %collective-permute-start.22) | collective-permute-done | bytes 720928 | tf_op jit(solution)/shard_map/ppermute | solution.py:62
  122.7 4.5 %collective-permute-start.34 = (bf16[64,1152]{1,0:T(8,128)(2,1)S(1)}, bf16[64,1152]{1,0:T(8,128)(2,1)S(1)}, u32[]{:S(2)}, u32[]{:S(2)}) collective-permute-start(bf16[64,1152]{1,0:T(8,128)(2,1)S(1)} %split.73), channel_id=1, source_target_pairs={{0,8},{4,12},{8,0},{12,4},{1,9},{5,13},{9,1},{13,5},{2,10},{6,14},... | collective-permute-start | bytes 442376 | tf_op jit(solution)/shard_map/ppermute | solution.py:62
  127.2 1.5 collective-permute-start.28
  129.4 3.7 %collective-permute-done.34 = bf16[64,1152]{1,0:T(8,128)(2,1)S(1)} collective-permute-done((bf16[64,1152]{1,0:T(8,128)(2,1)S(1)}, bf16[64,1152]{1,0:T(8,128)(2,1)S(1)}, u32[]{:S(2)}, u32[]{:S(2)}) %collective-permute-start.34) | collective-permute-done | bytes 147488 | tf_op jit(solution)/shard_map/ppermute | solution.py:62
  133.1 1.5 %collective-permute-start.35 = (bf16[32,1152]{1,0:T(8,128)(2,1)S(1)}, bf16[32,1152]{1,0:T(8,128)(2,1)S(1)}, u32[]{:S(2)}, u32[]{:S(2)}) collective-permute-start(bf16[32,1152]{1,0:T(8,128)(2,1)S(1)} %slice.196), channel_id=1, source_target_pairs={{0,16},{16,0},{1,17},{17,1},{2,18},{18,2},{3,19},{19,3},{4,20},{20... | collective-permute-start | bytes 221192 | tf_op jit(solution)/shard_map/ppermute | solution.py:62
  136.8 1.5 collective-permute-start.29
  138.3 3.8 %collective-permute-done.24 = bf16[64,1408]{1,0:T(8,128)(2,1)S(1)} collective-permute-done((bf16[64,1408]{1,0:T(8,128)(2,1)S(1)}, bf16[64,1408]{1,0:T(8,128)(2,1)S(1)}, u32[]{:S(2)}, u32[]{:S(2)}) %collective-permute-start.24) | collective-permute-done | bytes 180256 | tf_op jit(solution)/shard_map/ppermute | solution.py:62
  142.1 2.4 %collective-permute-start.25 = (bf16[32,1408]{1,0:T(8,128)(2,1)S(1)}, bf16[32,1408]{1,0:T(8,128)(2,1)S(1)}, u32[]{:S(2)}, u32[]{:S(2)}) collective-permute-start(bf16[32,1408]{1,0:T(8,128)(2,1)S(1)} %slice.186), channel_id=1, source_target_pairs={{0,8},{4,12},{8,0},{12,4},{1,9},{5,13},{9,1},{13,5},{2,10},{6,14},... | collective-permute-start | bytes 270344 | tf_op jit(solution)/shard_map/ppermute | solution.py:62
  145.0 2.6 %collective-permute-start.30 = (bf16[32,1408]{1,0:T(8,128)(2,1)S(1)}, bf16[32,1408]{1,0:T(8,128)(2,1)S(1)}, u32[]{:S(2)}, u32[]{:S(2)}) collective-permute-start(bf16[32,1408]{1,0:T(8,128)(2,1)S(1)} %slice.193), channel_id=1, source_target_pairs={{0,8},{4,12},{8,0},{12,4},{1,9},{5,13},{9,1},{13,5},{2,10},{6,14},... | collective-permute-start | bytes 270344 | tf_op jit(solution)/shard_map/ppermute | solution.py:62
  147.6 2.2 %collective-permute-done.25 = bf16[32,1408]{1,0:T(8,128)(2,1)S(1)} collective-permute-done((bf16[32,1408]{1,0:T(8,128)(2,1)S(1)}, bf16[32,1408]{1,0:T(8,128)(2,1)S(1)}, u32[]{:S(2)}, u32[]{:S(2)}) %collective-permute-start.25) | collective-permute-done | bytes 90144 | tf_op jit(solution)/shard_map/ppermute | solution.py:62
  (153 shorter events, 32.4 us)
Async XLA Ops:
  0.0 6.6 %copy-start = (s32[1,64,6]{1,0,2:T(1,128)S(1)}, s32[1,64,6]{1,0,2:T(1,128)}, u32[]{:S(2)}) copy-start(s32[1,64,6]{1,0,2:T(1,128)} %param.7) | copy-start | bytes 4612
  1.6 11.9 %collective-permute-start.4 = (bf16[32,1536]{1,0:T(8,128)(2,1)S(1)}, bf16[32,1536]{1,0:T(8,128)(2,1)S(1)}, u32[]{:S(2)}, u32[]{:S(2)}) collective-permute-start(bf16[32,1536]{1,0:T(8,128)(2,1)S(1)} %get-tuple-element.53), channel_id=1, source_target_pairs={{0,8},{4,12},{8,0},{12,4},{1,9},{5,13},{9,1},{13,5},{2,10},{6,14},... | collective-permute-start | bytes 294920 | tf_op jit(solution)/shard_map/ppermute | solution.py:62
  5.6 9.2 %collective-permute-start = (bf16[32,1536]{1,0:T(8,128)(2,1)S(1)}, bf16[32,1536]{1,0:T(8,128)(2,1)S(1)}, u32[]{:S(2)}, u32[]{:S(2)}) collective-permute-start(bf16[32,1536]{1,0:T(8,128)(2,1)S(1)} %get-tuple-element.54), channel_id=1, source_target_pairs={{0,8},{4,12},{8,0},{12,4},{1,9},{5,13},{9,1},{13,5},{2,10},{6,14},... | collective-permute-start | bytes 294920 | tf_op jit(solution)/shard_map/ppermute | solution.py:62
  13.5 8.5 %collective-permute-start.5 = (bf16[64,1536]{1,0:T(8,128)(2,1)S(1)}, bf16[64,1536]{1,0:T(8,128)(2,1)S(1)}, u32[]{:S(2)}, u32[]{:S(2)}) collective-permute-start(bf16[64,1536]{1,0:T(8,128)(2,1)S(1)} %pad_maximum_fusion.11), channel_id=1, source_target_pairs={{0,4},{4,0},{8,12},{12,8},{1,5},{5,1},{9,13},{13,9},{2,6},{6,2},{1... | collective-permute-start | bytes 589832 | tf_op jit(solution)/shard_map/ppermute | solution.py:62
  14.8 9.0 %collective-permute-start.1 = (bf16[64,1536]{1,0:T(8,128)(2,1)S(1)}, bf16[64,1536]{1,0:T(8,128)(2,1)S(1)}, u32[]{:S(2)}, u32[]{:S(2)}) collective-permute-start(bf16[64,1536]{1,0:T(8,128)(2,1)S(1)} %pad_maximum_fusion.10), channel_id=1, source_target_pairs={{0,4},{4,0},{8,12},{12,8},{1,5},{5,1},{9,13},{13,9},{2,6},{6,2},{1... | collective-permute-start | bytes 589832 | tf_op jit(solution)/shard_map/ppermute | solution.py:62
  15.7 4.4 %collective-permute-start.9 = (bf16[32,128]{0,1:T(8,128)(2,1)S(1)}, bf16[32,128]{0,1:T(8,128)(2,1)S(1)}, u32[]{:S(2)}, u32[]{:S(2)}) collective-permute-start(bf16[32,128]{0,1:T(8,128)(2,1)S(1)} %fusion.97), channel_id=1, source_target_pairs={{0,16},{16,0},{1,17},{17,1},{2,18},{18,2},{3,19},{19,3},{4,20},{20... | collective-permute-start | bytes 24584 | tf_op jit(solution)/shard_map/ppermute | solution.py:62
  17.4 4.6 %collective-permute-start.8 = (bf16[32,1024]{1,0:T(8,128)(2,1)S(1)}, bf16[32,1024]{1,0:T(8,128)(2,1)S(1)}, u32[]{:S(2)}, u32[]{:S(2)}) collective-permute-start(bf16[32,1024]{1,0:T(8,128)(2,1)S(1)} %get-tuple-element.25), channel_id=1, source_target_pairs={{0,16},{16,0},{1,17},{17,1},{2,18},{18,2},{3,19},{19,3},{4,20},{20... | collective-permute-start | bytes 196616 | tf_op jit(solution)/shard_map/ppermute | solution.py:62
  17.7 4.3 %collective-permute-start.12 = (bf16[32,1024]{1,0:T(8,128)(2,1)S(1)}, bf16[32,1024]{1,0:T(8,128)(2,1)S(1)}, u32[]{:S(2)}, u32[]{:S(2)}) collective-permute-start(bf16[32,1024]{1,0:T(8,128)(2,1)S(1)} %get-tuple-element.29), channel_id=1, source_target_pairs={{0,2},{2,0},{1,3},{3,1},{4,6},{6,4},{5,7},{7,5},{8,10},{10,8},{9,1... | collective-permute-start | bytes 196616 | tf_op jit(solution)/shard_map/ppermute | solution.py:62
  20.3 8.3 %copy-start.3 = (bf16[512,1536]{1,0:T(8,128)(2,1)S(1)}, bf16[512,1536]{1,0:T(8,128)(2,1)}, u32[]{:S(2)}) copy-start(bf16[512,1536]{1,0:T(8,128)(2,1)} %constant_dynamic-update-slice_fusion.3) | copy-start | bytes 4718596
  22.1 11.5 %collective-permute-start.6 = (bf16[128,1536]{1,0:T(8,128)(2,1)S(1)}, bf16[128,1536]{1,0:T(8,128)(2,1)S(1)}, u32[]{:S(2)}, u32[]{:S(2)}) collective-permute-start(bf16[128,1536]{1,0:T(8,128)(2,1)S(1)} %pad_maximum_fusion.7), channel_id=1, source_target_pairs={{0,2},{2,0},{1,3},{3,1},{4,6},{6,4},{5,7},{7,5},{8,10},{10,8},{9,1... | collective-permute-start | bytes 1179656 | tf_op jit(solution)/shard_map/ppermute | solution.py:62
  23.9 8.9 %collective-permute-start.2 = (bf16[128,1536]{1,0:T(8,128)(2,1)S(1)}, bf16[128,1536]{1,0:T(8,128)(2,1)S(1)}, u32[]{:S(2)}, u32[]{:S(2)}) collective-permute-start(bf16[128,1536]{1,0:T(8,128)(2,1)S(1)} %pad_maximum_fusion.6), channel_id=1, source_target_pairs={{0,16},{16,0},{1,17},{17,1},{2,18},{18,2},{3,19},{19,3},{4,20},{20... | collective-permute-start | bytes 1179656 | tf_op jit(solution)/shard_map/ppermute | solution.py:62
  25.5 12.0 %collective-permute-start.13 = (bf16[64,1024]{1,0:T(8,128)(2,1)S(1)}, bf16[64,1024]{1,0:T(8,128)(2,1)S(1)}, u32[]{:S(2)}, u32[]{:S(2)}) collective-permute-start(bf16[64,1024]{1,0:T(8,128)(2,1)S(1)} %pad_maximum_fusion.13), channel_id=1, source_target_pairs={{0,8},{4,12},{8,0},{12,4},{1,9},{5,13},{9,1},{13,5},{2,10},{6,14},... | collective-permute-start | bytes 393224 | tf_op jit(solution)/shard_map/ppermute | solution.py:62
  28.5 11.1 %collective-permute-start.10 = (bf16[64,1152]{1,0:T(8,128)(2,1)S(1)}, bf16[64,1152]{1,0:T(8,128)(2,1)S(1)}, u32[]{:S(2)}, u32[]{:S(2)}) collective-permute-start(bf16[64,1152]{1,0:T(8,128)(2,1)S(1)} %pad_maximum_fusion.12), channel_id=1, source_target_pairs={{0,8},{4,12},{8,0},{12,4},{1,9},{5,13},{9,1},{13,5},{2,10},{6,14},... | collective-permute-start | bytes 442376 | tf_op jit(solution)/shard_map/ppermute | solution.py:62
  32.9 20.5 %collective-permute-start.3 = (bf16[256,1536]{1,0:T(8,128)(2,1)S(1)}, bf16[256,1536]{1,0:T(8,128)(2,1)S(1)}, u32[]{:S(2)}, u32[]{:S(2)}) collective-permute-start(bf16[256,1536]{1,0:T(8,128)(2,1)S(1)} %pad_maximum_fusion.2), channel_id=1, source_target_pairs={{0,2},{2,0},{1,3},{3,1},{4,6},{6,4},{5,7},{7,5},{8,10},{10,8},{9,1... | collective-permute-start | bytes 2359304 | tf_op jit(solution)/shard_map/ppermute | solution.py:62
  33.6 19.7 %collective-permute-start.7 = (bf16[256,1536]{1,0:T(8,128)(2,1)S(1)}, bf16[256,1536]{1,0:T(8,128)(2,1)S(1)}, u32[]{:S(2)}, u32[]{:S(2)}) collective-permute-start(bf16[256,1536]{1,0:T(8,128)(2,1)S(1)} %pad_maximum_fusion.3), channel_id=1, source_target_pairs={{0,16},{16,0},{1,17},{17,1},{2,18},{18,2},{3,19},{19,3},{4,20},{20... | collective-permute-start | bytes 2359304 | tf_op jit(solution)/shard_map/ppermute | solution.py:62
  39.6 9.3 %collective-permute-start.14 = (bf16[128,1024]{1,0:T(8,128)(2,1)S(1)}, bf16[128,1024]{1,0:T(8,128)(2,1)S(1)}, u32[]{:S(2)}, u32[]{:S(2)}) collective-permute-start(bf16[128,1024]{1,0:T(8,128)(2,1)S(1)} %pad_maximum_fusion.9), channel_id=1, source_target_pairs={{0,4},{4,0},{8,12},{12,8},{1,5},{5,1},{9,13},{13,9},{2,6},{6,2},{1... | collective-permute-start | bytes 786440 | tf_op jit(solution)/shard_map/ppermute | solution.py:62
  40.4 12.9 %collective-permute-start.11 = (bf16[128,1152]{1,0:T(8,128)(2,1)S(1)}, bf16[128,1152]{1,0:T(8,128)(2,1)S(1)}, u32[]{:S(2)}, u32[]{:S(2)}) collective-permute-start(bf16[128,1152]{1,0:T(8,128)(2,1)S(1)} %pad_maximum_fusion.8), channel_id=1, source_target_pairs={{0,4},{4,0},{8,12},{12,8},{1,5},{5,1},{9,13},{13,9},{2,6},{6,2},{1... | collective-permute-start | bytes 884744 | tf_op jit(solution)/shard_map/ppermute | solution.py:62
  41.8 13.9 %copy-start.4 = (bf16[1,768,5120]{2,1,0:T(8,128)(2,1)S(1)}, bf16[1,768,5120]{2,1,0:T(8,128)(2,1)}, u32[]{:S(2)}) copy-start(bf16[1,768,5120]{2,1,0:T(8,128)(2,1)} %param.10) | copy-start | bytes 23592964
  53.4 4.4 %slice-start = ((s8[7864320]{0:T(1024)(128)(4,1)}), s8[4194304]{0:T(1024)(128)(4,1)S(1)}, s32[]{:S(2)}) async-start(s8[7864320]{0:T(1024)(128)(4,1)} %bitcast.171), calls=%async_computation | async-start | bytes 8388608
  53.6 12.8 %collective-permute-start.16 = (bf16[256,1024]{1,0:T(8,128)(2,1)S(1)}, bf16[256,1024]{1,0:T(8,128)(2,1)S(1)}, u32[]{:S(2)}, u32[]{:S(2)}) collective-permute-start(bf16[256,1024]{1,0:T(8,128)(2,1)S(1)} %pad_maximum_fusion.5), channel_id=1, source_target_pairs={{0,16},{16,0},{1,17},{17,1},{2,18},{18,2},{3,19},{19,3},{4,20},{20... | collective-permute-start | bytes 1572872 | tf_op jit(solution)/shard_map/ppermute | solution.py:62
  54.2 13.2 %collective-permute-start.15 = (bf16[256,1152]{1,0:T(8,128)(2,1)S(1)}, bf16[256,1152]{1,0:T(8,128)(2,1)S(1)}, u32[]{:S(2)}, u32[]{:S(2)}) collective-permute-start(bf16[256,1152]{1,0:T(8,128)(2,1)S(1)} %pad_maximum_fusion.4), channel_id=1, source_target_pairs={{0,2},{2,0},{1,3},{3,1},{4,6},{6,4},{5,7},{7,5},{8,10},{10,8},{9,1... | collective-permute-start | bytes 1769480 | tf_op jit(solution)/shard_map/ppermute | solution.py:62
  55.7 6.3 %collective-permute-start.18 = (bf16[512,1536]{1,0:T(8,128)(2,1)S(1)}, bf16[512,1536]{1,0:T(8,128)(2,1)S(1)}, u32[]{:S(2)}, u32[]{:S(2)}) collective-permute-start(bf16[512,1536]{1,0:T(8,128)(2,1)S(1)} %bitcast.155), channel_id=1, source_target_pairs={{0,1},{1,0},{2,3},{3,2},{4,5},{5,4},{6,7},{7,6},{8,9},{9,8},{10,11... | collective-permute-start | bytes 4718600 | tf_op jit(solution)/shard_map/ppermute | solution.py:62
  57.2 6.3 %collective-permute-start.17 = (bf16[512,1536]{1,0:T(8,128)(2,1)S(1)}, bf16[512,1536]{1,0:T(8,128)(2,1)S(1)}, u32[]{:S(2)}, u32[]{:S(2)}) collective-permute-start(bf16[512,1536]{1,0:T(8,128)(2,1)S(1)} %constant_dynamic-update-slice_fusion), channel_id=1, source_target_pairs={{0,1},{1,0},{2,3},{3,2},{4,5},{5,4},{6,7},{7,6},{8,9},{9,8},{10,11... | collective-permute-start | bytes 4718600 | tf_op jit(solution)/shard_map/ppermute | solution.py:62
  67.5 5.5 %collective-permute-start.20 = (bf16[512,1024]{1,0:T(8,128)(2,1)S(1)}, bf16[512,1024]{1,0:T(8,128)(2,1)S(1)}, u32[]{:S(2)}, u32[]{:S(2)}) collective-permute-start(bf16[512,1024]{1,0:T(8,128)(2,1)S(1)} %bitcast.162), channel_id=1, source_target_pairs={{0,1},{1,0},{2,3},{3,2},{4,5},{5,4},{6,7},{7,6},{8,9},{9,8},{10,11... | collective-permute-start | bytes 3145736 | tf_op jit(solution)/shard_map/ppermute | solution.py:62
  68.9 5.3 %collective-permute-start.19 = (bf16[512,1152]{1,0:T(8,128)(2,1)S(1)}, bf16[512,1152]{1,0:T(8,128)(2,1)S(1)}, u32[]{:S(2)}, u32[]{:S(2)}) collective-permute-start(bf16[512,1152]{1,0:T(8,128)(2,1)S(1)} %bitcast.148), channel_id=1, source_target_pairs={{0,1},{1,0},{2,3},{3,2},{4,5},{5,4},{6,7},{7,6},{8,9},{9,8},{10,11... | collective-permute-start | bytes 3538952 | tf_op jit(solution)/shard_map/ppermute | solution.py:62
  75.1 2.8 %slice-start.2 = ((s8[7864320]{0:T(1024)(128)(4,1)}), s8[4194304]{0:T(1024)(128)(4,1)S(1)}, s32[]{:S(2)}) async-start(s8[7864320]{0:T(1024)(128)(4,1)} %bitcast.175), calls=%async_computation.2 | async-start | bytes 8388608
  81.1 8.4 %collective-permute-start.31 = (bf16[512,1152]{1,0:T(8,128)(2,1)S(1)}, bf16[512,1152]{1,0:T(8,128)(2,1)S(1)}, u32[]{:S(2)}, u32[]{:S(2)}) collective-permute-start(bf16[512,1152]{1,0:T(8,128)(2,1)S(1)} %convolution_convert_fusion.1), channel_id=1, source_target_pairs={{0,1},{1,0},{2,3},{3,2},{4,5},{5,4},{6,7},{7,6},{8,9},{9,8},{10,11... | collective-permute-start | bytes 3538952 | tf_op jit(solution)/shard_map/ppermute | solution.py:62
  81.2 5.4 %collective-permute-start.36 = (bf16[512,1152]{1,0:T(8,128)(2,1)S(1)}, bf16[512,1152]{1,0:T(8,128)(2,1)S(1)}, u32[]{:S(2)}, u32[]{:S(2)}) collective-permute-start(bf16[512,1152]{1,0:T(8,128)(2,1)S(1)} %convolution_convert_fusion), channel_id=1, source_target_pairs={{0,1},{1,0},{2,3},{3,2},{4,5},{5,4},{6,7},{7,6},{8,9},{9,8},{10,11... | collective-permute-start | bytes 3538952 | tf_op jit(solution)/shard_map/ppermute | solution.py:62
  83.2 9.4 %collective-permute-start.21 = (bf16[512,1408]{1,0:T(8,128)(2,1)S(1)}, bf16[512,1408]{1,0:T(8,128)(2,1)S(1)}, u32[]{:S(2)}, u32[]{:S(2)}) collective-permute-start(bf16[512,1408]{1,0:T(8,128)(2,1)S(1)} %convolution_convert_fusion.3), channel_id=1, source_target_pairs={{0,1},{1,0},{2,3},{3,2},{4,5},{5,4},{6,7},{7,6},{8,9},{9,8},{10,11... | collective-permute-start | bytes 4325384 | tf_op jit(solution)/shard_map/ppermute | solution.py:62
  84.7 9.9 %collective-permute-start.26 = (bf16[512,1408]{1,0:T(8,128)(2,1)S(1)}, bf16[512,1408]{1,0:T(8,128)(2,1)S(1)}, u32[]{:S(2)}, u32[]{:S(2)}) collective-permute-start(bf16[512,1408]{1,0:T(8,128)(2,1)S(1)} %convolution_convert_fusion.2), channel_id=1, source_target_pairs={{0,1},{1,0},{2,3},{3,2},{4,5},{5,4},{6,7},{7,6},{8,9},{9,8},{10,11... | collective-permute-start | bytes 4325384 | tf_op jit(solution)/shard_map/ppermute | solution.py:62
  87.9 16.3 %collective-permute-start.37 = (bf16[256,1152]{1,0:T(8,128)(2,1)S(1)}, bf16[256,1152]{1,0:T(8,128)(2,1)S(1)}, u32[]{:S(2)}, u32[]{:S(2)}) collective-permute-start(bf16[256,1152]{1,0:T(8,128)(2,1)S(1)} %split.75), channel_id=1, source_target_pairs={{0,16},{16,0},{1,17},{17,1},{2,18},{18,2},{3,19},{19,3},{4,20},{20... | collective-permute-start | bytes 1769480 | tf_op jit(solution)/shard_map/ppermute | solution.py:62
  91.0 16.3 %collective-permute-start.32 = (bf16[256,1152]{1,0:T(8,128)(2,1)S(1)}, bf16[256,1152]{1,0:T(8,128)(2,1)S(1)}, u32[]{:S(2)}, u32[]{:S(2)}) collective-permute-start(bf16[256,1152]{1,0:T(8,128)(2,1)S(1)} %split.69), channel_id=1, source_target_pairs={{0,2},{2,0},{1,3},{3,1},{4,6},{6,4},{5,7},{7,5},{8,10},{10,8},{9,1... | collective-permute-start | bytes 1769480 | tf_op jit(solution)/shard_map/ppermute | solution.py:62
  94.0 27.5 %collective-permute-start.22 = (bf16[256,1408]{1,0:T(8,128)(2,1)S(1)}, bf16[256,1408]{1,0:T(8,128)(2,1)S(1)}, u32[]{:S(2)}, u32[]{:S(2)}) collective-permute-start(bf16[256,1408]{1,0:T(8,128)(2,1)S(1)} %split.65), channel_id=1, source_target_pairs={{0,2},{2,0},{1,3},{3,1},{4,6},{6,4},{5,7},{7,5},{8,10},{10,8},{9,1... | collective-permute-start | bytes 2162696 | tf_op jit(solution)/shard_map/ppermute | solution.py:62
  96.1 26.3 %collective-permute-start.27 = (bf16[256,1408]{1,0:T(8,128)(2,1)S(1)}, bf16[256,1408]{1,0:T(8,128)(2,1)S(1)}, u32[]{:S(2)}, u32[]{:S(2)}) collective-permute-start(bf16[256,1408]{1,0:T(8,128)(2,1)S(1)} %split.67), channel_id=1, source_target_pairs={{0,16},{16,0},{1,17},{17,1},{2,18},{18,2},{3,19},{19,3},{4,20},{20... | collective-permute-start | bytes 2162696 | tf_op jit(solution)/shard_map/ppermute | solution.py:62
  104.3 12.0 %collective-permute-start.38 = (bf16[128,1152]{1,0:T(8,128)(2,1)S(1)}, bf16[128,1152]{1,0:T(8,128)(2,1)S(1)}, u32[]{:S(2)}, u32[]{:S(2)}) collective-permute-start(bf16[128,1152]{1,0:T(8,128)(2,1)S(1)} %split.77), channel_id=1, source_target_pairs={{0,4},{4,0},{8,12},{12,8},{1,5},{5,1},{9,13},{13,9},{2,6},{6,2},{1... | collective-permute-start | bytes 884744 | tf_op jit(solution)/shard_map/ppermute | solution.py:62
  107.4 15.1 %collective-permute-start.33 = (bf16[128,1152]{1,0:T(8,128)(2,1)S(1)}, bf16[128,1152]{1,0:T(8,128)(2,1)S(1)}, u32[]{:S(2)}, u32[]{:S(2)}) collective-permute-start(bf16[128,1152]{1,0:T(8,128)(2,1)S(1)} %split.71), channel_id=1, source_target_pairs={{0,4},{4,0},{8,12},{12,8},{1,5},{5,1},{9,13},{13,9},{2,6},{6,2},{1... | collective-permute-start | bytes 884744 | tf_op jit(solution)/shard_map/ppermute | solution.py:62
  116.5 12.3 %collective-permute-start.39 = (bf16[64,1152]{1,0:T(8,128)(2,1)S(1)}, bf16[64,1152]{1,0:T(8,128)(2,1)S(1)}, u32[]{:S(2)}, u32[]{:S(2)}) collective-permute-start(bf16[64,1152]{1,0:T(8,128)(2,1)S(1)} %split.79), channel_id=1, source_target_pairs={{0,8},{4,12},{8,0},{12,4},{1,9},{5,13},{9,1},{13,5},{2,10},{6,14},... | collective-permute-start | bytes 442376 | tf_op jit(solution)/shard_map/ppermute | solution.py:62
  121.7 12.9 %collective-permute-start.23 = (bf16[128,1408]{1,0:T(8,128)(2,1)S(1)}, bf16[128,1408]{1,0:T(8,128)(2,1)S(1)}, u32[]{:S(2)}, u32[]{:S(2)}) collective-permute-start(bf16[128,1408]{1,0:T(8,128)(2,1)S(1)} %slice.182), channel_id=1, source_target_pairs={{0,16},{16,0},{1,17},{17,1},{2,18},{18,2},{3,19},{19,3},{4,20},{20... | collective-permute-start | bytes 1081352 | tf_op jit(solution)/shard_map/ppermute | solution.py:62
  122.7 10.3 %collective-permute-start.34 = (bf16[64,1152]{1,0:T(8,128)(2,1)S(1)}, bf16[64,1152]{1,0:T(8,128)(2,1)S(1)}, u32[]{:S(2)}, u32[]{:S(2)}) collective-permute-start(bf16[64,1152]{1,0:T(8,128)(2,1)S(1)} %split.73), channel_id=1, source_target_pairs={{0,8},{4,12},{8,0},{12,4},{1,9},{5,13},{9,1},{13,5},{2,10},{6,14},... | collective-permute-start | bytes 442376 | tf_op jit(solution)/shard_map/ppermute | solution.py:62
  127.2 9.5 %collective-permute-start.28 = (bf16[128,1408]{1,0:T(8,128)(2,1)S(1)}, bf16[128,1408]{1,0:T(8,128)(2,1)S(1)}, u32[]{:S(2)}, u32[]{:S(2)}) collective-permute-start(bf16[128,1408]{1,0:T(8,128)(2,1)S(1)} %slice.189), channel_id=1, source_target_pairs={{0,2},{2,0},{1,3},{3,1},{4,6},{6,4},{5,7},{7,5},{8,10},{10,8},{9,1... | collective-permute-start | bytes 1081352 | tf_op jit(solution)/shard_map/ppermute | solution.py:62
  128.8 18.8 %collective-permute-start.40 = (bf16[32,1152]{1,0:T(8,128)(2,1)S(1)}, bf16[32,1152]{1,0:T(8,128)(2,1)S(1)}, u32[]{:S(2)}, u32[]{:S(2)}) collective-permute-start(bf16[32,1152]{1,0:T(8,128)(2,1)S(1)} %slice.199), channel_id=1, source_target_pairs={{0,2},{2,0},{1,3},{3,1},{4,6},{6,4},{5,7},{7,5},{8,10},{10,8},{9,1... | collective-permute-start | bytes 221192 | tf_op jit(solution)/shard_map/ppermute | solution.py:62
  133.1 14.5 %collective-permute-start.35 = (bf16[32,1152]{1,0:T(8,128)(2,1)S(1)}, bf16[32,1152]{1,0:T(8,128)(2,1)S(1)}, u32[]{:S(2)}, u32[]{:S(2)}) collective-permute-start(bf16[32,1152]{1,0:T(8,128)(2,1)S(1)} %slice.196), channel_id=1, source_target_pairs={{0,16},{16,0},{1,17},{17,1},{2,18},{18,2},{3,19},{19,3},{4,20},{20... | collective-permute-start | bytes 221192 | tf_op jit(solution)/shard_map/ppermute | solution.py:62
  134.7 12.9 %copy-start.2 = (bf16[1,32,5120]{2,1,0:T(8,128)(2,1)S(1)}, bf16[1,32,5120]{2,1,0:T(8,128)(2,1)}, u32[]{:S(2)}) copy-start(bf16[1,32,5120]{2,1,0:T(8,128)(2,1)} %param.6) | copy-start | bytes 983044
  134.8 7.3 %collective-permute-start.24 = (bf16[64,1408]{1,0:T(8,128)(2,1)S(1)}, bf16[64,1408]{1,0:T(8,128)(2,1)S(1)}, u32[]{:S(2)}, u32[]{:S(2)}) collective-permute-start(bf16[64,1408]{1,0:T(8,128)(2,1)S(1)} %slice.184), channel_id=1, source_target_pairs={{0,4},{4,0},{8,12},{12,8},{1,5},{5,1},{9,13},{13,9},{2,6},{6,2},{1... | collective-permute-start | bytes 540680 | tf_op jit(solution)/shard_map/ppermute | solution.py:62
  136.8 14.8 %copy-start.1 = (s32[1,64,6]{1,0,2:T(1,128)S(1)}, s32[1,64,6]{1,0,2:T(1,128)}, u32[]{:S(2)}) copy-start(s32[1,64,6]{1,0,2:T(1,128)} %param.7) | copy-start | bytes 4612
  136.8 8.1 %collective-permute-start.29 = (bf16[64,1408]{1,0:T(8,128)(2,1)S(1)}, bf16[64,1408]{1,0:T(8,128)(2,1)S(1)}, u32[]{:S(2)}, u32[]{:S(2)}) collective-permute-start(bf16[64,1408]{1,0:T(8,128)(2,1)S(1)} %slice.191), channel_id=1, source_target_pairs={{0,4},{4,0},{8,12},{12,8},{1,5},{5,1},{9,13},{13,9},{2,6},{6,2},{1... | collective-permute-start | bytes 540680 | tf_op jit(solution)/shard_map/ppermute | solution.py:62
  142.1 7.7 %collective-permute-start.25 = (bf16[32,1408]{1,0:T(8,128)(2,1)S(1)}, bf16[32,1408]{1,0:T(8,128)(2,1)S(1)}, u32[]{:S(2)}, u32[]{:S(2)}) collective-permute-start(bf16[32,1408]{1,0:T(8,128)(2,1)S(1)} %slice.186), channel_id=1, source_target_pairs={{0,8},{4,12},{8,0},{12,4},{1,9},{5,13},{9,1},{13,5},{2,10},{6,14},... | collective-permute-start | bytes 270344 | tf_op jit(solution)/shard_map/ppermute | solution.py:62
  145.0 5.8 %collective-permute-start.30 = (bf16[32,1408]{1,0:T(8,128)(2,1)S(1)}, bf16[32,1408]{1,0:T(8,128)(2,1)S(1)}, u32[]{:S(2)}, u32[]{:S(2)}) collective-permute-start(bf16[32,1408]{1,0:T(8,128)(2,1)S(1)} %slice.193), channel_id=1, source_target_pairs={{0,8},{4,12},{8,0},{12,4},{1,9},{5,13},{9,1},{13,5},{2,10},{6,14},... | collective-permute-start | bytes 270344 | tf_op jit(solution)/shard_map/ppermute | solution.py:62
  (2 other events, 4.4 us)

commit v5 on v4

--- a/solution.py
+++ b/solution.py
@@ -180,6 +180,7 @@
         kept[c], goes = jnp.split(parts[c], 2, axis=0)
         sent[c] = swap(goes, *STAGES[c][3])
     first = {c: added(kept[c], sent[c]) for c in one}
+    second = {c: halved(first[c], STAGES[c][2]) for c in one}
     outs = {}
     for c in two:
         value = added(kept[c], after(sent[c], *[parts[d] for d in one]))
@@ -187,10 +188,10 @@
         goes = swap(goes, *NEAR)
         value = added(stays, after(goes, *first.values()) if c == two[0] else goes)
         stays, goes = jnp.split(value, 2, axis=0)
-        value = added(stays, after(swap(goes, *FAR), *first.values()))
+        value = added(stays, after(swap(goes, *FAR), second[one[0]] if c == two[0] else first[one[0]]))
         outs[c] = (value, STAGES[c][0])
     for c in one:
-        outs[c] = (halved(halved(first[c], STAGES[c][2]), NEAR), FAR)
+        outs[c] = (halved(second[c], NEAR), FAR)
     for c, (value, flip) in outs.items():
         total = block[:, back_spans[c]].astype(jnp.float32) + value[:half].astype(jnp.float32)
         outs[c] = (total + swap(value[half:], *flip).astype(jnp.float32)).astype(jnp.bfloat16)

time: 152 us -> 150 us (0.987)
  waiting for transfers between devices: 58.5 us -> 53.1 us
  starting transfers between devices: 52.4 us -> 55.8 us
    ppermute x41, waiting for transfers between devices: 58.5 us -> 53.1 us  [swap(): return lax.ppermute(value, axis, [(i, i ^ flip) for i in range(size)])]
    ppermute x41, starting transfers between devices: 52.4 us -> 55.8 us  [swap(): return lax.ppermute(value, axis, [(i, i ^ flip) for i in range(size)])]
  transfers between devices with their start and end apart: 41 -> 41, of which waited for: 19 -> 17; matrix products, arithmetic and copies ran while one was open for 20% -> 20% of each run, Pallas kernels for 0% -> 0%
where the time goes in v5:
time: 150 us
  starting transfers between devices  55.8 us (37%)
  waiting for transfers between devices  53.1 us (35%)
  matrix products  31 us (21%)
  local copies, waits for them, and re-layouts  6.13 us (4%)
  other arithmetic  2.81 us (2%)
    ppermute x41, starting transfers between devices, swap(): return lax.ppermute(value, axis, [(i, i ^ flip) for i in range(size)])  55.8 us
    ppermute x41, waiting for transfers between devices, swap(): return lax.ppermute(value, axis, [(i, i ^ flip) for i in range(size)])  53.1 us
    dot_general x16, matrix products, ring_body(): lax.dot_general(rows, weight[0, :, spans[c]], dims, preferred_element_typ...  20.3 us
    dot_general x8, matrix products, down(): jnp.dot(value, down_weight[0, :, back_spans[c]], preferred_element_type=j...  10.7 us
    unnamed x27, local copies, waits for them, and re-layouts  3.17 us
  transfers between devices with their start and end apart: 41, of which 17 were waited for; matrix products, arithmetic and copies ran while one was open for 20% of the time, Pallas kernels for 0%

profile of v5, /device:TPU:0, one launch (start us, length us, event | category | flops | bytes accessed | tf_op | source)
XLA Modules:
  0.0 149.6 jit_solution(901525227943717347)
XLA Ops:
  0.0 1.6 %constant_dynamic-update-slice_fusion.4 = (bf16[512,1536]{1,0:T(8,128)(2,1)}, bf16[512,1536]{1,0:T(8,128)(2,1)S(1)}, bf16[32,1536]{1,0:T(8,128)(2,1)S(1)}, bf16[32,1536]{1,0:T(8,128)(2,1)S(1)}) fusion(bf16[32,5120]{1,0:T(8,128)(2,1)} %bitcast.158), kind=kLoop, calls=%fused_computation.132 | loop fusion | bytes 589824
  1.6 4.0 %collective-permute-start.4 = (bf16[32,1536]{1,0:T(8,128)(2,1)S(1)}, bf16[32,1536]{1,0:T(8,128)(2,1)S(1)}, u32[]{:S(2)}, u32[]{:S(2)}) collective-permute-start(bf16[32,1536]{1,0:T(8,128)(2,1)S(1)} %get-tuple-element.53), channel_id=1, source_target_pairs={{0,8},{4,12},{8,0},{12,4},{1,9},{5,13},{9,1},{13,5},{2,10},{6,14},... | collective-permute-start | bytes 294920 | tf_op jit(solution)/shard_map/ppermute | solution.py:62
  7.5 6.0 %collective-permute-done.4 = bf16[32,1536]{1,0:T(8,128)(2,1)S(1)} collective-permute-done((bf16[32,1536]{1,0:T(8,128)(2,1)S(1)}, bf16[32,1536]{1,0:T(8,128)(2,1)S(1)}, u32[]{:S(2)}, u32[]{:S(2)}) %collective-permute-start.4) | collective-permute-done | bytes 98336 | tf_op jit(solution)/shard_map/ppermute | solution.py:62
  15.7 1.7 %collective-permute-start.9 = (bf16[32,128]{0,1:T(8,128)(2,1)S(1)}, bf16[32,128]{0,1:T(8,128)(2,1)S(1)}, u32[]{:S(2)}, u32[]{:S(2)}) collective-permute-start(bf16[32,128]{0,1:T(8,128)(2,1)S(1)} %fusion.97), channel_id=1, source_target_pairs={{0,16},{16,0},{1,17},{17,1},{2,18},{18,2},{3,19},{19,3},{4,20},{20... | collective-permute-start | bytes 24584 | tf_op jit(solution)/shard_map/ppermute | solution.py:62
  17.7 1.7 %collective-permute-start.12 = (bf16[32,1024]{1,0:T(8,128)(2,1)S(1)}, bf16[32,1024]{1,0:T(8,128)(2,1)S(1)}, u32[]{:S(2)}, u32[]{:S(2)}) collective-permute-start(bf16[32,1024]{1,0:T(8,128)(2,1)S(1)} %get-tuple-element.29), channel_id=1, source_target_pairs={{0,2},{2,0},{1,3},{3,1},{4,6},{6,4},{5,7},{7,5},{8,10},{10,8},{9,1... | collective-permute-start | bytes 196616 | tf_op jit(solution)/shard_map/ppermute | solution.py:62
  20.3 1.7 %collective-permute-done.12 = bf16[32,1024]{1,0:T(8,128)(2,1)S(1)} collective-permute-done((bf16[32,1024]{1,0:T(8,128)(2,1)S(1)}, bf16[32,1024]{1,0:T(8,128)(2,1)S(1)}, u32[]{:S(2)}, u32[]{:S(2)}) %collective-permute-start.12) | collective-permute-done | bytes 65568 | tf_op jit(solution)/shard_map/ppermute | solution.py:62
  22.1 1.8 %collective-permute-start.6 = (bf16[128,1536]{1,0:T(8,128)(2,1)S(1)}, bf16[128,1536]{1,0:T(8,128)(2,1)S(1)}, u32[]{:S(2)}, u32[]{:S(2)}) collective-permute-start(bf16[128,1536]{1,0:T(8,128)(2,1)S(1)} %pad_maximum_fusion.7), channel_id=1, source_target_pairs={{0,2},{2,0},{1,3},{3,1},{4,6},{6,4},{5,7},{7,5},{8,10},{10,8},{9,1... | collective-permute-start | bytes 1179656 | tf_op jit(solution)/shard_map/ppermute | solution.py:62
  23.9 1.6 %collective-permute-start.2 = (bf16[128,1536]{1,0:T(8,128)(2,1)S(1)}, bf16[128,1536]{1,0:T(8,128)(2,1)S(1)}, u32[]{:S(2)}, u32[]{:S(2)}) collective-permute-start(bf16[128,1536]{1,0:T(8,128)(2,1)S(1)} %pad_maximum_fusion.6), channel_id=1, source_target_pairs={{0,16},{16,0},{1,17},{17,1},{2,18},{18,2},{3,19},{19,3},{4,20},{20... | collective-permute-start | bytes 1179656 | tf_op jit(solution)/shard_map/ppermute | solution.py:62
  25.5 3.1 %collective-permute-start.13 = (bf16[64,1024]{1,0:T(8,128)(2,1)S(1)}, bf16[64,1024]{1,0:T(8,128)(2,1)S(1)}, u32[]{:S(2)}, u32[]{:S(2)}) collective-permute-start(bf16[64,1024]{1,0:T(8,128)(2,1)S(1)} %pad_maximum_fusion.13), channel_id=1, source_target_pairs={{0,8},{4,12},{8,0},{12,4},{1,9},{5,13},{9,1},{13,5},{2,10},{6,14},... | collective-permute-start | bytes 393224 | tf_op jit(solution)/shard_map/ppermute | solution.py:62
  28.6 4.2 %collective-permute-done.2 = bf16[128,1536]{1,0:T(8,128)(2,1)S(1)} collective-permute-done((bf16[128,1536]{1,0:T(8,128)(2,1)S(1)}, bf16[128,1536]{1,0:T(8,128)(2,1)S(1)}, u32[]{:S(2)}, u32[]{:S(2)}) %collective-permute-start.2) | collective-permute-done | bytes 393248 | tf_op jit(solution)/shard_map/ppermute | solution.py:62
  33.6 1.6 %collective-permute-start.7 = (bf16[256,1536]{1,0:T(8,128)(2,1)S(1)}, bf16[256,1536]{1,0:T(8,128)(2,1)S(1)}, u32[]{:S(2)}, u32[]{:S(2)}) collective-permute-start(bf16[256,1536]{1,0:T(8,128)(2,1)S(1)} %pad_maximum_fusion.3), channel_id=1, source_target_pairs={{0,16},{16,0},{1,17},{17,1},{2,18},{18,2},{3,19},{19,3},{4,20},{20... | collective-permute-start | bytes 2359304 | tf_op jit(solution)/shard_map/ppermute | solution.py:62
  35.2 2.3 %collective-permute-done.13 = bf16[64,1024]{1,0:T(8,128)(2,1)S(1)} collective-permute-done((bf16[64,1024]{1,0:T(8,128)(2,1)S(1)}, bf16[64,1024]{1,0:T(8,128)(2,1)S(1)}, u32[]{:S(2)}, u32[]{:S(2)}) %collective-permute-start.13) | collective-permute-done | bytes 131104 | tf_op jit(solution)/shard_map/ppermute | solution.py:62
  37.5 2.1 %collective-permute-done.10 = bf16[64,1152]{1,0:T(8,128)(2,1)S(1)} collective-permute-done((bf16[64,1152]{1,0:T(8,128)(2,1)S(1)}, bf16[64,1152]{1,0:T(8,128)(2,1)S(1)}, u32[]{:S(2)}, u32[]{:S(2)}) %collective-permute-start.10) | collective-permute-done | bytes 147488 | tf_op jit(solution)/shard_map/ppermute | solution.py:62
  40.4 1.4 collective-permute-start.11
  41.9 7.1 %collective-permute-done.14 = bf16[128,1024]{1,0:T(8,128)(2,1)S(1)} collective-permute-done((bf16[128,1024]{1,0:T(8,128)(2,1)S(1)}, bf16[128,1024]{1,0:T(8,128)(2,1)S(1)}, u32[]{:S(2)}, u32[]{:S(2)}) %collective-permute-start.14) | collective-permute-done | bytes 262176 | tf_op jit(solution)/shard_map/ppermute | solution.py:62
  49.0 4.3 %collective-permute-done.11 = bf16[128,1152]{1,0:T(8,128)(2,1)S(1)} collective-permute-done((bf16[128,1152]{1,0:T(8,128)(2,1)S(1)}, bf16[128,1152]{1,0:T(8,128)(2,1)S(1)}, u32[]{:S(2)}, u32[]{:S(2)}) %collective-permute-start.11) | collective-permute-done | bytes 294944 | tf_op jit(solution)/shard_map/ppermute | solution.py:62
  54.2 1.5 %collective-permute-start.15 = (bf16[256,1152]{1,0:T(8,128)(2,1)S(1)}, bf16[256,1152]{1,0:T(8,128)(2,1)S(1)}, u32[]{:S(2)}, u32[]{:S(2)}) collective-permute-start(bf16[256,1152]{1,0:T(8,128)(2,1)S(1)} %pad_maximum_fusion.4), channel_id=1, source_target_pairs={{0,2},{2,0},{1,3},{3,1},{4,6},{6,4},{5,7},{7,5},{8,10},{10,8},{9,1... | collective-permute-start | bytes 1769480 | tf_op jit(solution)/shard_map/ppermute | solution.py:62
  55.7 1.4 fusion.2
  57.8 1.4 fusion.10
  59.2 1.4 fusion.78
  60.6 1.4 fusion.72
  62.1 1.4 fusion.8
  63.5 1.4 fusion.4
  64.9 1.4 fusion.75
  70.4 1.6 %fusion = f32[512,768]{1,0:T(8,128)S(1)} fusion(bf16[512,1536]{1,0:T(8,128)(2,1)S(1)} %collective-permute-done.18, bf16[1,768,5120]{2,1,0:T(8,128)(2,1)S(1)} %copy-done.4), kind=kOutput, calls=%fused_computation.6 | convolution fusion | flops 1207959552 | bytes 5505024 | tf_op jit(solution)/shard_map/dot_general | solution.py:162
  76.3 1.5 multiply_convert_fusion.1
  81.7 1.4 convolution_convert_fusion.3
  83.3 1.4 convolution_convert_fusion.2
  87.9 1.6 %collective-permute-start.37 = (bf16[256,1152]{1,0:T(8,128)(2,1)S(1)}, bf16[256,1152]{1,0:T(8,128)(2,1)S(1)}, u32[]{:S(2)}, u32[]{:S(2)}) collective-permute-start(bf16[256,1152]{1,0:T(8,128)(2,1)S(1)} %split.75), channel_id=1, source_target_pairs={{0,16},{16,0},{1,17},{17,1},{2,18},{18,2},{3,19},{19,3},{4,20},{20... | collective-permute-start | bytes 1769480 | tf_op jit(solution)/shard_map/ppermute | solution.py:62
  89.5 1.5 add_convert_fusion.3
  91.0 1.6 %collective-permute-start.32 = (bf16[256,1152]{1,0:T(8,128)(2,1)S(1)}, bf16[256,1152]{1,0:T(8,128)(2,1)S(1)}, u32[]{:S(2)}, u32[]{:S(2)}) collective-permute-start(bf16[256,1152]{1,0:T(8,128)(2,1)S(1)} %split.69), channel_id=1, source_target_pairs={{0,2},{2,0},{1,3},{3,1},{4,6},{6,4},{5,7},{7,5},{8,10},{10,8},{9,1... | collective-permute-start | bytes 1769480 | tf_op jit(solution)/shard_map/ppermute | solution.py:62
  92.6 1.4 add_convert_fusion.1
  94.6 1.4 add_convert_fusion
  96.7 7.5 %collective-permute-done.37 = bf16[256,1152]{1,0:T(8,128)(2,1)S(1)} collective-permute-done((bf16[256,1152]{1,0:T(8,128)(2,1)S(1)}, bf16[256,1152]{1,0:T(8,128)(2,1)S(1)}, u32[]{:S(2)}, u32[]{:S(2)}) %collective-permute-start.37) | collective-permute-done | bytes 589856 | tf_op jit(solution)/shard_map/ppermute | solution.py:62
  104.3 2.5 %collective-permute-start.38 = (bf16[128,1152]{1,0:T(8,128)(2,1)S(1)}, bf16[128,1152]{1,0:T(8,128)(2,1)S(1)}, u32[]{:S(2)}, u32[]{:S(2)}) collective-permute-start(bf16[128,1152]{1,0:T(8,128)(2,1)S(1)} %split.77), channel_id=1, source_target_pairs={{0,4},{4,0},{8,12},{12,8},{1,5},{5,1},{9,13},{13,9},{2,6},{6,2},{1... | collective-permute-start | bytes 884744 | tf_op jit(solution)/shard_map/ppermute | solution.py:62
  107.4 2.5 %collective-permute-start.33 = (bf16[128,1152]{1,0:T(8,128)(2,1)S(1)}, bf16[128,1152]{1,0:T(8,128)(2,1)S(1)}, u32[]{:S(2)}, u32[]{:S(2)}) collective-permute-start(bf16[128,1152]{1,0:T(8,128)(2,1)S(1)} %split.71), channel_id=1, source_target_pairs={{0,4},{4,0},{8,12},{12,8},{1,5},{5,1},{9,13},{13,9},{2,6},{6,2},{1... | collective-permute-start | bytes 884744 | tf_op jit(solution)/shard_map/ppermute | solution.py:62
  110.0 6.4 %collective-permute-done.38 = bf16[128,1152]{1,0:T(8,128)(2,1)S(1)} collective-permute-done((bf16[128,1152]{1,0:T(8,128)(2,1)S(1)}, bf16[128,1152]{1,0:T(8,128)(2,1)S(1)}, u32[]{:S(2)}, u32[]{:S(2)}) %collective-permute-start.38) | collective-permute-done | bytes 294944 | tf_op jit(solution)/shard_map/ppermute | solution.py:62
  116.5 3.0 %collective-permute-start.39 = (bf16[64,1152]{1,0:T(8,128)(2,1)S(1)}, bf16[64,1152]{1,0:T(8,128)(2,1)S(1)}, u32[]{:S(2)}, u32[]{:S(2)}) collective-permute-start(bf16[64,1152]{1,0:T(8,128)(2,1)S(1)} %split.79), channel_id=1, source_target_pairs={{0,8},{4,12},{8,0},{12,4},{1,9},{5,13},{9,1},{13,5},{2,10},{6,14},... | collective-permute-start | bytes 442376 | tf_op jit(solution)/shard_map/ppermute | solution.py:62
  119.4 2.1 %collective-permute-done.22 = bf16[256,1408]{1,0:T(8,128)(2,1)S(1)} collective-permute-done((bf16[256,1408]{1,0:T(8,128)(2,1)S(1)}, bf16[256,1408]{1,0:T(8,128)(2,1)S(1)}, u32[]{:S(2)}, u32[]{:S(2)}) %collective-permute-start.22) | collective-permute-done | bytes 720928 | tf_op jit(solution)/shard_map/ppermute | solution.py:62
  122.7 4.5 %collective-permute-start.34 = (bf16[64,1152]{1,0:T(8,128)(2,1)S(1)}, bf16[64,1152]{1,0:T(8,128)(2,1)S(1)}, u32[]{:S(2)}, u32[]{:S(2)}) collective-permute-start(bf16[64,1152]{1,0:T(8,128)(2,1)S(1)} %split.73), channel_id=1, source_target_pairs={{0,8},{4,12},{8,0},{12,4},{1,9},{5,13},{9,1},{13,5},{2,10},{6,14},... | collective-permute-start | bytes 442376 | tf_op jit(solution)/shard_map/ppermute | solution.py:62
  127.2 1.5 %collective-permute-start.28 = (bf16[128,1408]{1,0:T(8,128)(2,1)S(1)}, bf16[128,1408]{1,0:T(8,128)(2,1)S(1)}, u32[]{:S(2)}, u32[]{:S(2)}) collective-permute-start(bf16[128,1408]{1,0:T(8,128)(2,1)S(1)} %slice.189), channel_id=1, source_target_pairs={{0,2},{2,0},{1,3},{3,1},{4,6},{6,4},{5,7},{7,5},{8,10},{10,8},{9,1... | collective-permute-start | bytes 1081352 | tf_op jit(solution)/shard_map/ppermute | solution.py:62
  129.4 1.7 %collective-permute-done.23 = bf16[128,1408]{1,0:T(8,128)(2,1)S(1)} collective-permute-done((bf16[128,1408]{1,0:T(8,128)(2,1)S(1)}, bf16[128,1408]{1,0:T(8,128)(2,1)S(1)}, u32[]{:S(2)}, u32[]{:S(2)}) %collective-permute-start.23) | collective-permute-done | bytes 360480 | tf_op jit(solution)/shard_map/ppermute | solution.py:62
  131.2 2.5 %collective-permute-start.24 = (bf16[64,1408]{1,0:T(8,128)(2,1)S(1)}, bf16[64,1408]{1,0:T(8,128)(2,1)S(1)}, u32[]{:S(2)}, u32[]{:S(2)}) collective-permute-start(bf16[64,1408]{1,0:T(8,128)(2,1)S(1)} %slice.184), channel_id=1, source_target_pairs={{0,4},{4,0},{8,12},{12,8},{1,5},{5,1},{9,13},{13,9},{2,6},{6,2},{1... | collective-permute-start | bytes 540680 | tf_op jit(solution)/shard_map/ppermute | solution.py:62
  134.7 1.9 %collective-permute-done.28 = bf16[128,1408]{1,0:T(8,128)(2,1)S(1)} collective-permute-done((bf16[128,1408]{1,0:T(8,128)(2,1)S(1)}, bf16[128,1408]{1,0:T(8,128)(2,1)S(1)}, u32[]{:S(2)}, u32[]{:S(2)}) %collective-permute-start.28) | collective-permute-done | bytes 360480 | tf_op jit(solution)/shard_map/ppermute | solution.py:62
  136.8 1.5 collective-permute-start.29
  138.5 4.7 %collective-permute-start.25 = (bf16[32,1408]{1,0:T(8,128)(2,1)S(1)}, bf16[32,1408]{1,0:T(8,128)(2,1)S(1)}, u32[]{:S(2)}, u32[]{:S(2)}) collective-permute-start(bf16[32,1408]{1,0:T(8,128)(2,1)S(1)} %slice.186), channel_id=1, source_target_pairs={{0,8},{4,12},{8,0},{12,4},{1,9},{5,13},{9,1},{13,5},{2,10},{6,14},... | collective-permute-start | bytes 270344 | tf_op jit(solution)/shard_map/ppermute | solution.py:62
  143.2 2.4 %collective-permute-start.30 = (bf16[32,1408]{1,0:T(8,128)(2,1)S(1)}, bf16[32,1408]{1,0:T(8,128)(2,1)S(1)}, u32[]{:S(2)}, u32[]{:S(2)}) collective-permute-start(bf16[32,1408]{1,0:T(8,128)(2,1)S(1)} %slice.193), channel_id=1, source_target_pairs={{0,8},{4,12},{8,0},{12,4},{1,9},{5,13},{9,1},{13,5},{2,10},{6,14},... | collective-permute-start | bytes 270344 | tf_op jit(solution)/shard_map/ppermute | solution.py:62
  145.7 3.0 %collective-permute-done.30 = bf16[32,1408]{1,0:T(8,128)(2,1)S(1)} collective-permute-done((bf16[32,1408]{1,0:T(8,128)(2,1)S(1)}, bf16[32,1408]{1,0:T(8,128)(2,1)S(1)}, u32[]{:S(2)}, u32[]{:S(2)}) %collective-permute-start.30) | collective-permute-done | bytes 90144 | tf_op jit(solution)/shard_map/ppermute | solution.py:62
  (153 shorter events, 30.2 us)
Async XLA Ops:
  0.0 6.6 %copy-start = (s32[1,64,6]{1,0,2:T(1,128)S(1)}, s32[1,64,6]{1,0,2:T(1,128)}, u32[]{:S(2)}) copy-start(s32[1,64,6]{1,0,2:T(1,128)} %param.7) | copy-start | bytes 4612
  1.6 11.9 %collective-permute-start.4 = (bf16[32,1536]{1,0:T(8,128)(2,1)S(1)}, bf16[32,1536]{1,0:T(8,128)(2,1)S(1)}, u32[]{:S(2)}, u32[]{:S(2)}) collective-permute-start(bf16[32,1536]{1,0:T(8,128)(2,1)S(1)} %get-tuple-element.53), channel_id=1, source_target_pairs={{0,8},{4,12},{8,0},{12,4},{1,9},{5,13},{9,1},{13,5},{2,10},{6,14},... | collective-permute-start | bytes 294920 | tf_op jit(solution)/shard_map/ppermute | solution.py:62
  5.6 9.2 %collective-permute-start = (bf16[32,1536]{1,0:T(8,128)(2,1)S(1)}, bf16[32,1536]{1,0:T(8,128)(2,1)S(1)}, u32[]{:S(2)}, u32[]{:S(2)}) collective-permute-start(bf16[32,1536]{1,0:T(8,128)(2,1)S(1)} %get-tuple-element.54), channel_id=1, source_target_pairs={{0,8},{4,12},{8,0},{12,4},{1,9},{5,13},{9,1},{13,5},{2,10},{6,14},... | collective-permute-start | bytes 294920 | tf_op jit(solution)/shard_map/ppermute | solution.py:62
  13.5 8.5 %collective-permute-start.5 = (bf16[64,1536]{1,0:T(8,128)(2,1)S(1)}, bf16[64,1536]{1,0:T(8,128)(2,1)S(1)}, u32[]{:S(2)}, u32[]{:S(2)}) collective-permute-start(bf16[64,1536]{1,0:T(8,128)(2,1)S(1)} %pad_maximum_fusion.11), channel_id=1, source_target_pairs={{0,4},{4,0},{8,12},{12,8},{1,5},{5,1},{9,13},{13,9},{2,6},{6,2},{1... | collective-permute-start | bytes 589832 | tf_op jit(solution)/shard_map/ppermute | solution.py:62
  14.8 9.0 %collective-permute-start.1 = (bf16[64,1536]{1,0:T(8,128)(2,1)S(1)}, bf16[64,1536]{1,0:T(8,128)(2,1)S(1)}, u32[]{:S(2)}, u32[]{:S(2)}) collective-permute-start(bf16[64,1536]{1,0:T(8,128)(2,1)S(1)} %pad_maximum_fusion.10), channel_id=1, source_target_pairs={{0,4},{4,0},{8,12},{12,8},{1,5},{5,1},{9,13},{13,9},{2,6},{6,2},{1... | collective-permute-start | bytes 589832 | tf_op jit(solution)/shard_map/ppermute | solution.py:62
  15.7 4.4 %collective-permute-start.9 = (bf16[32,128]{0,1:T(8,128)(2,1)S(1)}, bf16[32,128]{0,1:T(8,128)(2,1)S(1)}, u32[]{:S(2)}, u32[]{:S(2)}) collective-permute-start(bf16[32,128]{0,1:T(8,128)(2,1)S(1)} %fusion.97), channel_id=1, source_target_pairs={{0,16},{16,0},{1,17},{17,1},{2,18},{18,2},{3,19},{19,3},{4,20},{20... | collective-permute-start | bytes 24584 | tf_op jit(solution)/shard_map/ppermute | solution.py:62
  17.4 4.6 %collective-permute-start.8 = (bf16[32,1024]{1,0:T(8,128)(2,1)S(1)}, bf16[32,1024]{1,0:T(8,128)(2,1)S(1)}, u32[]{:S(2)}, u32[]{:S(2)}) collective-permute-start(bf16[32,1024]{1,0:T(8,128)(2,1)S(1)} %get-tuple-element.25), channel_id=1, source_target_pairs={{0,16},{16,0},{1,17},{17,1},{2,18},{18,2},{3,19},{19,3},{4,20},{20... | collective-permute-start | bytes 196616 | tf_op jit(solution)/shard_map/ppermute | solution.py:62
  17.7 4.3 %collective-permute-start.12 = (bf16[32,1024]{1,0:T(8,128)(2,1)S(1)}, bf16[32,1024]{1,0:T(8,128)(2,1)S(1)}, u32[]{:S(2)}, u32[]{:S(2)}) collective-permute-start(bf16[32,1024]{1,0:T(8,128)(2,1)S(1)} %get-tuple-element.29), channel_id=1, source_target_pairs={{0,2},{2,0},{1,3},{3,1},{4,6},{6,4},{5,7},{7,5},{8,10},{10,8},{9,1... | collective-permute-start | bytes 196616 | tf_op jit(solution)/shard_map/ppermute | solution.py:62
  20.3 8.3 %copy-start.3 = (bf16[512,1536]{1,0:T(8,128)(2,1)S(1)}, bf16[512,1536]{1,0:T(8,128)(2,1)}, u32[]{:S(2)}) copy-start(bf16[512,1536]{1,0:T(8,128)(2,1)} %constant_dynamic-update-slice_fusion.3) | copy-start | bytes 4718596
  22.1 11.5 %collective-permute-start.6 = (bf16[128,1536]{1,0:T(8,128)(2,1)S(1)}, bf16[128,1536]{1,0:T(8,128)(2,1)S(1)}, u32[]{:S(2)}, u32[]{:S(2)}) collective-permute-start(bf16[128,1536]{1,0:T(8,128)(2,1)S(1)} %pad_maximum_fusion.7), channel_id=1, source_target_pairs={{0,2},{2,0},{1,3},{3,1},{4,6},{6,4},{5,7},{7,5},{8,10},{10,8},{9,1... | collective-permute-start | bytes 1179656 | tf_op jit(solution)/shard_map/ppermute | solution.py:62
  23.9 8.9 %collective-permute-start.2 = (bf16[128,1536]{1,0:T(8,128)(2,1)S(1)}, bf16[128,1536]{1,0:T(8,128)(2,1)S(1)}, u32[]{:S(2)}, u32[]{:S(2)}) collective-permute-start(bf16[128,1536]{1,0:T(8,128)(2,1)S(1)} %pad_maximum_fusion.6), channel_id=1, source_target_pairs={{0,16},{16,0},{1,17},{17,1},{2,18},{18,2},{3,19},{19,3},{4,20},{20... | collective-permute-start | bytes 1179656 | tf_op jit(solution)/shard_map/ppermute | solution.py:62
  25.5 12.0 %collective-permute-start.13 = (bf16[64,1024]{1,0:T(8,128)(2,1)S(1)}, bf16[64,1024]{1,0:T(8,128)(2,1)S(1)}, u32[]{:S(2)}, u32[]{:S(2)}) collective-permute-start(bf16[64,1024]{1,0:T(8,128)(2,1)S(1)} %pad_maximum_fusion.13), channel_id=1, source_target_pairs={{0,8},{4,12},{8,0},{12,4},{1,9},{5,13},{9,1},{13,5},{2,10},{6,14},... | collective-permute-start | bytes 393224 | tf_op jit(solution)/shard_map/ppermute | solution.py:62
  28.5 11.1 %collective-permute-start.10 = (bf16[64,1152]{1,0:T(8,128)(2,1)S(1)}, bf16[64,1152]{1,0:T(8,128)(2,1)S(1)}, u32[]{:S(2)}, u32[]{:S(2)}) collective-permute-start(bf16[64,1152]{1,0:T(8,128)(2,1)S(1)} %pad_maximum_fusion.12), channel_id=1, source_target_pairs={{0,8},{4,12},{8,0},{12,4},{1,9},{5,13},{9,1},{13,5},{2,10},{6,14},... | collective-permute-start | bytes 442376 | tf_op jit(solution)/shard_map/ppermute | solution.py:62
  32.9 20.5 %collective-permute-start.3 = (bf16[256,1536]{1,0:T(8,128)(2,1)S(1)}, bf16[256,1536]{1,0:T(8,128)(2,1)S(1)}, u32[]{:S(2)}, u32[]{:S(2)}) collective-permute-start(bf16[256,1536]{1,0:T(8,128)(2,1)S(1)} %pad_maximum_fusion.2), channel_id=1, source_target_pairs={{0,2},{2,0},{1,3},{3,1},{4,6},{6,4},{5,7},{7,5},{8,10},{10,8},{9,1... | collective-permute-start | bytes 2359304 | tf_op jit(solution)/shard_map/ppermute | solution.py:62
  33.6 19.7 %collective-permute-start.7 = (bf16[256,1536]{1,0:T(8,128)(2,1)S(1)}, bf16[256,1536]{1,0:T(8,128)(2,1)S(1)}, u32[]{:S(2)}, u32[]{:S(2)}) collective-permute-start(bf16[256,1536]{1,0:T(8,128)(2,1)S(1)} %pad_maximum_fusion.3), channel_id=1, source_target_pairs={{0,16},{16,0},{1,17},{17,1},{2,18},{18,2},{3,19},{19,3},{4,20},{20... | collective-permute-start | bytes 2359304 | tf_op jit(solution)/shard_map/ppermute | solution.py:62
  39.6 9.3 %collective-permute-start.14 = (bf16[128,1024]{1,0:T(8,128)(2,1)S(1)}, bf16[128,1024]{1,0:T(8,128)(2,1)S(1)}, u32[]{:S(2)}, u32[]{:S(2)}) collective-permute-start(bf16[128,1024]{1,0:T(8,128)(2,1)S(1)} %pad_maximum_fusion.9), channel_id=1, source_target_pairs={{0,4},{4,0},{8,12},{12,8},{1,5},{5,1},{9,13},{13,9},{2,6},{6,2},{1... | collective-permute-start | bytes 786440 | tf_op jit(solution)/shard_map/ppermute | solution.py:62
  40.4 12.9 %collective-permute-start.11 = (bf16[128,1152]{1,0:T(8,128)(2,1)S(1)}, bf16[128,1152]{1,0:T(8,128)(2,1)S(1)}, u32[]{:S(2)}, u32[]{:S(2)}) collective-permute-start(bf16[128,1152]{1,0:T(8,128)(2,1)S(1)} %pad_maximum_fusion.8), channel_id=1, source_target_pairs={{0,4},{4,0},{8,12},{12,8},{1,5},{5,1},{9,13},{13,9},{2,6},{6,2},{1... | collective-permute-start | bytes 884744 | tf_op jit(solution)/shard_map/ppermute | solution.py:62
  41.8 13.9 %copy-start.4 = (bf16[1,768,5120]{2,1,0:T(8,128)(2,1)S(1)}, bf16[1,768,5120]{2,1,0:T(8,128)(2,1)}, u32[]{:S(2)}) copy-start(bf16[1,768,5120]{2,1,0:T(8,128)(2,1)} %param.10) | copy-start | bytes 23592964
  53.4 4.4 %slice-start = ((s8[7864320]{0:T(1024)(128)(4,1)}), s8[4194304]{0:T(1024)(128)(4,1)S(1)}, s32[]{:S(2)}) async-start(s8[7864320]{0:T(1024)(128)(4,1)} %bitcast.171), calls=%async_computation | async-start | bytes 8388608
  53.6 12.8 %collective-permute-start.16 = (bf16[256,1024]{1,0:T(8,128)(2,1)S(1)}, bf16[256,1024]{1,0:T(8,128)(2,1)S(1)}, u32[]{:S(2)}, u32[]{:S(2)}) collective-permute-start(bf16[256,1024]{1,0:T(8,128)(2,1)S(1)} %pad_maximum_fusion.5), channel_id=1, source_target_pairs={{0,16},{16,0},{1,17},{17,1},{2,18},{18,2},{3,19},{19,3},{4,20},{20... | collective-permute-start | bytes 1572872 | tf_op jit(solution)/shard_map/ppermute | solution.py:62
  54.2 13.2 %collective-permute-start.15 = (bf16[256,1152]{1,0:T(8,128)(2,1)S(1)}, bf16[256,1152]{1,0:T(8,128)(2,1)S(1)}, u32[]{:S(2)}, u32[]{:S(2)}) collective-permute-start(bf16[256,1152]{1,0:T(8,128)(2,1)S(1)} %pad_maximum_fusion.4), channel_id=1, source_target_pairs={{0,2},{2,0},{1,3},{3,1},{4,6},{6,4},{5,7},{7,5},{8,10},{10,8},{9,1... | collective-permute-start | bytes 1769480 | tf_op jit(solution)/shard_map/ppermute | solution.py:62
  55.7 6.3 %collective-permute-start.18 = (bf16[512,1536]{1,0:T(8,128)(2,1)S(1)}, bf16[512,1536]{1,0:T(8,128)(2,1)S(1)}, u32[]{:S(2)}, u32[]{:S(2)}) collective-permute-start(bf16[512,1536]{1,0:T(8,128)(2,1)S(1)} %bitcast.155), channel_id=1, source_target_pairs={{0,1},{1,0},{2,3},{3,2},{4,5},{5,4},{6,7},{7,6},{8,9},{9,8},{10,11... | collective-permute-start | bytes 4718600 | tf_op jit(solution)/shard_map/ppermute | solution.py:62
  57.2 6.3 %collective-permute-start.17 = (bf16[512,1536]{1,0:T(8,128)(2,1)S(1)}, bf16[512,1536]{1,0:T(8,128)(2,1)S(1)}, u32[]{:S(2)}, u32[]{:S(2)}) collective-permute-start(bf16[512,1536]{1,0:T(8,128)(2,1)S(1)} %constant_dynamic-update-slice_fusion), channel_id=1, source_target_pairs={{0,1},{1,0},{2,3},{3,2},{4,5},{5,4},{6,7},{7,6},{8,9},{9,8},{10,11... | collective-permute-start | bytes 4718600 | tf_op jit(solution)/shard_map/ppermute | solution.py:62
  67.5 5.5 %collective-permute-start.20 = (bf16[512,1024]{1,0:T(8,128)(2,1)S(1)}, bf16[512,1024]{1,0:T(8,128)(2,1)S(1)}, u32[]{:S(2)}, u32[]{:S(2)}) collective-permute-start(bf16[512,1024]{1,0:T(8,128)(2,1)S(1)} %bitcast.162), channel_id=1, source_target_pairs={{0,1},{1,0},{2,3},{3,2},{4,5},{5,4},{6,7},{7,6},{8,9},{9,8},{10,11... | collective-permute-start | bytes 3145736 | tf_op jit(solution)/shard_map/ppermute | solution.py:62
  68.9 5.3 %collective-permute-start.19 = (bf16[512,1152]{1,0:T(8,128)(2,1)S(1)}, bf16[512,1152]{1,0:T(8,128)(2,1)S(1)}, u32[]{:S(2)}, u32[]{:S(2)}) collective-permute-start(bf16[512,1152]{1,0:T(8,128)(2,1)S(1)} %bitcast.148), channel_id=1, source_target_pairs={{0,1},{1,0},{2,3},{3,2},{4,5},{5,4},{6,7},{7,6},{8,9},{9,8},{10,11... | collective-permute-start | bytes 3538952 | tf_op jit(solution)/shard_map/ppermute | solution.py:62
  75.1 2.8 %slice-start.2 = ((s8[7864320]{0:T(1024)(128)(4,1)}), s8[4194304]{0:T(1024)(128)(4,1)S(1)}, s32[]{:S(2)}) async-start(s8[7864320]{0:T(1024)(128)(4,1)} %bitcast.175), calls=%async_computation.2 | async-start | bytes 8388608
  81.1 8.4 %collective-permute-start.31 = (bf16[512,1152]{1,0:T(8,128)(2,1)S(1)}, bf16[512,1152]{1,0:T(8,128)(2,1)S(1)}, u32[]{:S(2)}, u32[]{:S(2)}) collective-permute-start(bf16[512,1152]{1,0:T(8,128)(2,1)S(1)} %convolution_convert_fusion.1), channel_id=1, source_target_pairs={{0,1},{1,0},{2,3},{3,2},{4,5},{5,4},{6,7},{7,6},{8,9},{9,8},{10,11... | collective-permute-start | bytes 3538952 | tf_op jit(solution)/shard_map/ppermute | solution.py:62
  81.2 5.4 %collective-permute-start.36 = (bf16[512,1152]{1,0:T(8,128)(2,1)S(1)}, bf16[512,1152]{1,0:T(8,128)(2,1)S(1)}, u32[]{:S(2)}, u32[]{:S(2)}) collective-permute-start(bf16[512,1152]{1,0:T(8,128)(2,1)S(1)} %convolution_convert_fusion), channel_id=1, source_target_pairs={{0,1},{1,0},{2,3},{3,2},{4,5},{5,4},{6,7},{7,6},{8,9},{9,8},{10,11... | collective-permute-start | bytes 3538952 | tf_op jit(solution)/shard_map/ppermute | solution.py:62
  83.2 9.4 %collective-permute-start.21 = (bf16[512,1408]{1,0:T(8,128)(2,1)S(1)}, bf16[512,1408]{1,0:T(8,128)(2,1)S(1)}, u32[]{:S(2)}, u32[]{:S(2)}) collective-permute-start(bf16[512,1408]{1,0:T(8,128)(2,1)S(1)} %convolution_convert_fusion.3), channel_id=1, source_target_pairs={{0,1},{1,0},{2,3},{3,2},{4,5},{5,4},{6,7},{7,6},{8,9},{9,8},{10,11... | collective-permute-start | bytes 4325384 | tf_op jit(solution)/shard_map/ppermute | solution.py:62
  84.7 9.9 %collective-permute-start.26 = (bf16[512,1408]{1,0:T(8,128)(2,1)S(1)}, bf16[512,1408]{1,0:T(8,128)(2,1)S(1)}, u32[]{:S(2)}, u32[]{:S(2)}) collective-permute-start(bf16[512,1408]{1,0:T(8,128)(2,1)S(1)} %convolution_convert_fusion.2), channel_id=1, source_target_pairs={{0,1},{1,0},{2,3},{3,2},{4,5},{5,4},{6,7},{7,6},{8,9},{9,8},{10,11... | collective-permute-start | bytes 4325384 | tf_op jit(solution)/shard_map/ppermute | solution.py:62
  87.9 16.3 %collective-permute-start.37 = (bf16[256,1152]{1,0:T(8,128)(2,1)S(1)}, bf16[256,1152]{1,0:T(8,128)(2,1)S(1)}, u32[]{:S(2)}, u32[]{:S(2)}) collective-permute-start(bf16[256,1152]{1,0:T(8,128)(2,1)S(1)} %split.75), channel_id=1, source_target_pairs={{0,16},{16,0},{1,17},{17,1},{2,18},{18,2},{3,19},{19,3},{4,20},{20... | collective-permute-start | bytes 1769480 | tf_op jit(solution)/shard_map/ppermute | solution.py:62
  91.0 16.3 %collective-permute-start.32 = (bf16[256,1152]{1,0:T(8,128)(2,1)S(1)}, bf16[256,1152]{1,0:T(8,128)(2,1)S(1)}, u32[]{:S(2)}, u32[]{:S(2)}) collective-permute-start(bf16[256,1152]{1,0:T(8,128)(2,1)S(1)} %split.69), channel_id=1, source_target_pairs={{0,2},{2,0},{1,3},{3,1},{4,6},{6,4},{5,7},{7,5},{8,10},{10,8},{9,1... | collective-permute-start | bytes 1769480 | tf_op jit(solution)/shard_map/ppermute | solution.py:62
  94.0 27.5 %collective-permute-start.22 = (bf16[256,1408]{1,0:T(8,128)(2,1)S(1)}, bf16[256,1408]{1,0:T(8,128)(2,1)S(1)}, u32[]{:S(2)}, u32[]{:S(2)}) collective-permute-start(bf16[256,1408]{1,0:T(8,128)(2,1)S(1)} %split.65), channel_id=1, source_target_pairs={{0,2},{2,0},{1,3},{3,1},{4,6},{6,4},{5,7},{7,5},{8,10},{10,8},{9,1... | collective-permute-start | bytes 2162696 | tf_op jit(solution)/shard_map/ppermute | solution.py:62
  96.1 26.3 %collective-permute-start.27 = (bf16[256,1408]{1,0:T(8,128)(2,1)S(1)}, bf16[256,1408]{1,0:T(8,128)(2,1)S(1)}, u32[]{:S(2)}, u32[]{:S(2)}) collective-permute-start(bf16[256,1408]{1,0:T(8,128)(2,1)S(1)} %split.67), channel_id=1, source_target_pairs={{0,16},{16,0},{1,17},{17,1},{2,18},{18,2},{3,19},{19,3},{4,20},{20... | collective-permute-start | bytes 2162696 | tf_op jit(solution)/shard_map/ppermute | solution.py:62
  104.3 12.0 %collective-permute-start.38 = (bf16[128,1152]{1,0:T(8,128)(2,1)S(1)}, bf16[128,1152]{1,0:T(8,128)(2,1)S(1)}, u32[]{:S(2)}, u32[]{:S(2)}) collective-permute-start(bf16[128,1152]{1,0:T(8,128)(2,1)S(1)} %split.77), channel_id=1, source_target_pairs={{0,4},{4,0},{8,12},{12,8},{1,5},{5,1},{9,13},{13,9},{2,6},{6,2},{1... | collective-permute-start | bytes 884744 | tf_op jit(solution)/shard_map/ppermute | solution.py:62
  107.4 15.1 %collective-permute-start.33 = (bf16[128,1152]{1,0:T(8,128)(2,1)S(1)}, bf16[128,1152]{1,0:T(8,128)(2,1)S(1)}, u32[]{:S(2)}, u32[]{:S(2)}) collective-permute-start(bf16[128,1152]{1,0:T(8,128)(2,1)S(1)} %split.71), channel_id=1, source_target_pairs={{0,4},{4,0},{8,12},{12,8},{1,5},{5,1},{9,13},{13,9},{2,6},{6,2},{1... | collective-permute-start | bytes 884744 | tf_op jit(solution)/shard_map/ppermute | solution.py:62
  116.5 12.3 %collective-permute-start.39 = (bf16[64,1152]{1,0:T(8,128)(2,1)S(1)}, bf16[64,1152]{1,0:T(8,128)(2,1)S(1)}, u32[]{:S(2)}, u32[]{:S(2)}) collective-permute-start(bf16[64,1152]{1,0:T(8,128)(2,1)S(1)} %split.79), channel_id=1, source_target_pairs={{0,8},{4,12},{8,0},{12,4},{1,9},{5,13},{9,1},{13,5},{2,10},{6,14},... | collective-permute-start | bytes 442376 | tf_op jit(solution)/shard_map/ppermute | solution.py:62
  121.7 9.3 %collective-permute-start.23 = (bf16[128,1408]{1,0:T(8,128)(2,1)S(1)}, bf16[128,1408]{1,0:T(8,128)(2,1)S(1)}, u32[]{:S(2)}, u32[]{:S(2)}) collective-permute-start(bf16[128,1408]{1,0:T(8,128)(2,1)S(1)} %slice.182), channel_id=1, source_target_pairs={{0,16},{16,0},{1,17},{17,1},{2,18},{18,2},{3,19},{19,3},{4,20},{20... | collective-permute-start | bytes 1081352 | tf_op jit(solution)/shard_map/ppermute | solution.py:62
  122.7 11.0 %collective-permute-start.34 = (bf16[64,1152]{1,0:T(8,128)(2,1)S(1)}, bf16[64,1152]{1,0:T(8,128)(2,1)S(1)}, u32[]{:S(2)}, u32[]{:S(2)}) collective-permute-start(bf16[64,1152]{1,0:T(8,128)(2,1)S(1)} %split.73), channel_id=1, source_target_pairs={{0,8},{4,12},{8,0},{12,4},{1,9},{5,13},{9,1},{13,5},{2,10},{6,14},... | collective-permute-start | bytes 442376 | tf_op jit(solution)/shard_map/ppermute | solution.py:62
  127.2 9.5 %collective-permute-start.28 = (bf16[128,1408]{1,0:T(8,128)(2,1)S(1)}, bf16[128,1408]{1,0:T(8,128)(2,1)S(1)}, u32[]{:S(2)}, u32[]{:S(2)}) collective-permute-start(bf16[128,1408]{1,0:T(8,128)(2,1)S(1)} %slice.189), channel_id=1, source_target_pairs={{0,2},{2,0},{1,3},{3,1},{4,6},{6,4},{5,7},{7,5},{8,10},{10,8},{9,1... | collective-permute-start | bytes 1081352 | tf_op jit(solution)/shard_map/ppermute | solution.py:62
  128.8 16.9 %collective-permute-start.40 = (bf16[32,1152]{1,0:T(8,128)(2,1)S(1)}, bf16[32,1152]{1,0:T(8,128)(2,1)S(1)}, u32[]{:S(2)}, u32[]{:S(2)}) collective-permute-start(bf16[32,1152]{1,0:T(8,128)(2,1)S(1)} %slice.199), channel_id=1, source_target_pairs={{0,2},{2,0},{1,3},{3,1},{4,6},{6,4},{5,7},{7,5},{8,10},{10,8},{9,1... | collective-permute-start | bytes 221192 | tf_op jit(solution)/shard_map/ppermute | solution.py:62
  131.2 7.2 %collective-permute-start.24 = (bf16[64,1408]{1,0:T(8,128)(2,1)S(1)}, bf16[64,1408]{1,0:T(8,128)(2,1)S(1)}, u32[]{:S(2)}, u32[]{:S(2)}) collective-permute-start(bf16[64,1408]{1,0:T(8,128)(2,1)S(1)} %slice.184), channel_id=1, source_target_pairs={{0,4},{4,0},{8,12},{12,8},{1,5},{5,1},{9,13},{13,9},{2,6},{6,2},{1... | collective-permute-start | bytes 540680 | tf_op jit(solution)/shard_map/ppermute | solution.py:62
  133.8 11.9 %copy-start.2 = (bf16[1,32,5120]{2,1,0:T(8,128)(2,1)S(1)}, bf16[1,32,5120]{2,1,0:T(8,128)(2,1)}, u32[]{:S(2)}) copy-start(bf16[1,32,5120]{2,1,0:T(8,128)(2,1)} %param.6) | copy-start | bytes 983044
  133.8 11.9 %collective-permute-start.35 = (bf16[32,1152]{1,0:T(8,128)(2,1)S(1)}, bf16[32,1152]{1,0:T(8,128)(2,1)S(1)}, u32[]{:S(2)}, u32[]{:S(2)}) collective-permute-start(bf16[32,1152]{1,0:T(8,128)(2,1)S(1)} %slice.196), channel_id=1, source_target_pairs={{0,16},{16,0},{1,17},{17,1},{2,18},{18,2},{3,19},{19,3},{4,20},{20... | collective-permute-start | bytes 221192 | tf_op jit(solution)/shard_map/ppermute | solution.py:62
  136.8 12.8 %copy-start.1 = (s32[1,64,6]{1,0,2:T(1,128)S(1)}, s32[1,64,6]{1,0,2:T(1,128)}, u32[]{:S(2)}) copy-start(s32[1,64,6]{1,0,2:T(1,128)} %param.7) | copy-start | bytes 4612
  136.8 6.4 %collective-permute-start.29 = (bf16[64,1408]{1,0:T(8,128)(2,1)S(1)}, bf16[64,1408]{1,0:T(8,128)(2,1)S(1)}, u32[]{:S(2)}, u32[]{:S(2)}) collective-permute-start(bf16[64,1408]{1,0:T(8,128)(2,1)S(1)} %slice.191), channel_id=1, source_target_pairs={{0,4},{4,0},{8,12},{12,8},{1,5},{5,1},{9,13},{13,9},{2,6},{6,2},{1... | collective-permute-start | bytes 540680 | tf_op jit(solution)/shard_map/ppermute | solution.py:62
  138.5 7.2 %collective-permute-start.25 = (bf16[32,1408]{1,0:T(8,128)(2,1)S(1)}, bf16[32,1408]{1,0:T(8,128)(2,1)S(1)}, u32[]{:S(2)}, u32[]{:S(2)}) collective-permute-start(bf16[32,1408]{1,0:T(8,128)(2,1)S(1)} %slice.186), channel_id=1, source_target_pairs={{0,8},{4,12},{8,0},{12,4},{1,9},{5,13},{9,1},{13,5},{2,10},{6,14},... | collective-permute-start | bytes 270344 | tf_op jit(solution)/shard_map/ppermute | solution.py:62
  143.2 5.5 %collective-permute-start.30 = (bf16[32,1408]{1,0:T(8,128)(2,1)S(1)}, bf16[32,1408]{1,0:T(8,128)(2,1)S(1)}, u32[]{:S(2)}, u32[]{:S(2)}) collective-permute-start(bf16[32,1408]{1,0:T(8,128)(2,1)S(1)} %slice.193), channel_id=1, source_target_pairs={{0,8},{4,12},{8,0},{12,4},{1,9},{5,13},{9,1},{13,5},{2,10},{6,14},... | collective-permute-start | bytes 270344 | tf_op jit(solution)/shard_map/ppermute | solution.py:62
  (2 other events, 4.4 us)
